TPU v7x, 256 devices: a whole 4x4x8 slice. The times are simulated.
256 devices in a mesh: img: 8 (over z_hi, core), sp: 32 (over x, z_lo, y).
Axes of the slice: x: 4, y: 4, z: 8 (z_hi: 4, z_lo: 2; z = z_hi * 2 + z_lo), core: 2. Of those that a mesh axis runs over, the one named last changes fastest.
Arguments:
- y_one: bfloat16 [32768, 1408], P(('img', 'sp')), parts along dimension 0, may hold values from -6 to 6
- second_stream_state: bfloat16 [32768, 1408], P(('img', 'sp')), parts along dimension 0, may hold values from -6 to 6
- cot: bfloat16 [1024, 128, 256], P(('img', 'sp')), parts along dimension 0, may hold values from -6 to 6
- layer_norm_gain: float32 [1408], replicated, may hold values from 0.1 to 1.9
- w_qkv: bfloat16 [1408, 2112], P('sp'), may hold values from -1 to 1
- w_out: bfloat16 [704, 1408], P('sp'), may hold values from -0.21875 to 0.21875
- w_deconv: bfloat16 [1408, 1536], P('sp'), may hold values from -0.15625 to 0.15625
- w_lateral: bfloat16 [384, 256], replicated, may hold values from -0.3125 to 0.3125
- lat_gain: float32 [256], replicated, may hold values from 0.1 to 1.9
- w_conv: bfloat16 [3, 3, 256, 256], replicated, may hold values from -0.125 to 0.125
- conv_gain: float32 [256], replicated, may hold values from 0.1 to 1.9
Outputs:
- x_one: bfloat16 [32768, 1408], P(('img', 'sp')), parts along dimension 0
- d_x1: bfloat16 [32768, 1408], P(('img', 'sp')), parts along dimension 0
- second_input_gradient: bfloat16 [32768, 1408], P(('img', 'sp')), parts along dimension 0
- g_out: float32 [5632, 1408], P(('img', 'sp')), parts along dimension 0
- g_deconv: float32 [11264, 1536], P(('img', 'sp')), parts along dimension 0
- g_lateral: float32 [3072, 256], P(('img', 'sp')), parts along dimension 0
- g_conv: float32 [24, 3, 256, 256], P('img', None, 'sp'), parts along dimension 0
There are 8 independent parts, one for each index of `img`. A program takes and returns all parts, laid end to end along the dimension named above; an argument that names none is the same for every part. Nothing has to cross between parts.
All inputs are finite; a program needn't handle non-finite values.
Results may differ from a plain program's by a relative error of at most 0.03.
Values may be sent and summed in bfloat16 or wider, within the bound.
A program may use at most 128 MiB of HBM per device.

v0:
```python
import jax
import jax.numpy as jnp
from jax import lax
from jax.sharding import PartitionSpec as P

HEADS = 8
HEAD = 88
DEC = 384
LAT = 256
GRID_W = 64


epsilon = 1e-06
grad_scale = 0.015625


def padded_2(block, sides, width):
    for axis, dim in sides:
        count = lax.axis_size(axis)
        forward = [(i, i + 1) for i in range(count - 1)]
        backward = [(target, source) for source, target in forward]
        low = lax.ppermute(
            lax.slice_in_dim(block, block.shape[dim] - width, None, axis=dim), axis, forward
        )
        high = lax.ppermute(lax.slice_in_dim(block, 0, width, axis=dim), axis, backward)
        block = jnp.concatenate([low, block, high], axis=dim)
    return block


def shifted_2(array, axis, by):
    count = lax.axis_size(axis)
    pairs = [(i, i + by) for i in range(count) if 0 <= i + by < count]
    return lax.ppermute(array, axis, pairs)


def apply_layer_norm(values):
    centered = values - jnp.mean(values, axis=-1, keepdims=True)
    inverse = lax.rsqrt(jnp.mean(centered * centered, axis=-1, keepdims=True) + epsilon)
    return (centered * inverse, inverse)


def layer_norm_reverse(upstream, normalized_rows, inverse):
    first = jnp.mean(upstream, axis=-1, keepdims=True)
    second = jnp.mean(upstream * normalized_rows, axis=-1, keepdims=True)
    return inverse * (upstream - first - normalized_rows * second)


def conv_valid(padded, kernel):
    result = lax.conv_general_dilated(
        padded[None],
        kernel,
        (1, 1),
        "VALID",
        dimension_numbers=("NHWC", "HWIO", "NHWC"),
        preferred_element_type=jnp.float32,
    )
    return result[0]


def rounded_part(left, right):
    product = lax.dot_general(
        left, right, (((0,), (0,)), ((), ())), preferred_element_type=jnp.float32
    )
    return (product * grad_scale).astype(jnp.bfloat16)


def to_heads(features, pieces):
    width = features.shape[0] // HEADS
    columns = features.shape[1] // pieces
    grouped = features.reshape(HEADS, width, pieces, columns).transpose(0, 2, 1, 3)
    return grouped.reshape(HEADS * pieces, width, columns)


def from_heads(received, pieces):
    width = received.shape[1]
    columns = received.shape[2]
    grouped = received.reshape(HEADS, pieces, width, columns).transpose(0, 2, 1, 3)
    return grouped.reshape(HEADS * width, pieces * columns)


def copies(features, pieces):
    width = features.shape[0] // HEADS
    columns = features.shape[1]
    spread = jnp.broadcast_to(
        features.reshape(HEADS, 1, width, columns), (HEADS, pieces, width, columns)
    )
    return spread.reshape(HEADS * pieces, width, columns)


def per_device(
    y_one,
    second_stream_state,
    cot,
    layer_norm_gain,
    w_qkv,
    w_out,
    w_deconv,
    w_lateral,
    lat_gain,
    w_conv,
    conv_gain,
):
    devices = lax.axis_size("sp")
    pieces = devices // HEADS
    tokens_here = y_one.shape[0]
    rows_here = tokens_here // GRID_W
    inner = HEADS * HEAD
    score_scale = HEAD ** (-0.5)
    standardized_input, inverse_deviation = apply_layer_norm(
        second_stream_state.astype(jnp.float32)
    )
    normalized_rows = (standardized_input * layer_norm_gain).astype(jnp.bfloat16)
    qkv_full = lax.all_gather(w_qkv, "sp", axis=0, tiled=True)
    projected = lax.dot_general(
        qkv_full, normalized_rows, (((0,), (1,)), ((), ())), preferred_element_type=jnp.float32
    )
    queries = (projected[:inner] * score_scale).astype(jnp.bfloat16)
    keys = projected[inner : 2 * inner].astype(jnp.bfloat16)
    values = projected[2 * inner :].astype(jnp.bfloat16)
    query_head = lax.all_to_all(
        to_heads(queries, pieces), "sp", split_axis=0, concat_axis=2, tiled=True
    )[0]
    key_routed, value_routed = (
        lax.all_to_all(copies(keys, pieces), "sp", split_axis=0, concat_axis=2, tiled=True),
        lax.all_to_all(copies(values, pieces), "sp", split_axis=0, concat_axis=2, tiled=True),
    )
    key_head = key_routed[0]
    value_head = value_routed[0]
    total_queries = query_head.shape[1]
    block = min(512, total_queries)
    count_blocks = total_queries // block
    query_blocks = query_head.reshape(HEAD, count_blocks, block).transpose(1, 0, 2)

    def attend(query_block):
        scores = lax.dot_general(
            query_block, key_head, (((0,), (0,)), ((), ())), preferred_element_type=jnp.float32
        )
        shifted = jnp.exp(scores - jnp.max(scores, axis=1, keepdims=True))
        weights = (shifted / jnp.sum(shifted, axis=1, keepdims=True)).astype(jnp.bfloat16)
        output = lax.dot_general(
            value_head, weights, (((1,), (1,)), ((), ())), preferred_element_type=jnp.float32
        ).astype(jnp.bfloat16)
        return (output, weights)

    attended, kept_weights = lax.map(attend, query_blocks)
    attended = attended.transpose(1, 0, 2).reshape(1, HEAD, total_queries)
    attn_band = from_heads(
        lax.all_to_all(attended, "sp", split_axis=2, concat_axis=0, tiled=True), pieces
    )
    out_full = lax.all_gather(w_out, "sp", axis=0, tiled=True)
    mixed = lax.dot_general(
        attn_band, out_full, (((0,), (0,)), ((), ())), preferred_element_type=jnp.float32
    )
    x_one = (y_one.astype(jnp.float32) - mixed).astype(jnp.bfloat16)
    feature = ((y_one.astype(jnp.float32) + second_stream_state.astype(jnp.float32)) * 0.5).astype(
        jnp.bfloat16
    )
    deconv_full = lax.all_gather(w_deconv, "sp", axis=0, tiled=True)
    upsampled = jnp.dot(feature, deconv_full, preferred_element_type=jnp.float32).astype(
        jnp.bfloat16
    )
    pixel_rows = 2 * rows_here
    pixel_cols = 2 * GRID_W
    pixels = (
        upsampled.reshape(rows_here, GRID_W, 2, 2, DEC)
        .transpose(0, 2, 1, 3, 4)
        .reshape(pixel_rows * pixel_cols, DEC)
    )
    lhat, linv = apply_layer_norm(jnp.dot(pixels, w_lateral, preferred_element_type=jnp.float32))
    activation = (lhat * lat_gain).astype(jnp.bfloat16).reshape(pixel_rows, pixel_cols, LAT)
    extended = padded_2(activation, (("sp", 0),), 1)
    padded = jnp.pad(extended, ((0, 0), (1, 1), (0, 0)))
    chat, cinv = apply_layer_norm(conv_valid(padded, w_conv))
    dconv = layer_norm_reverse(cot.astype(jnp.float32) * conv_gain, chat, cinv).astype(jnp.bfloat16)
    flipped = w_conv[::-1, ::-1].transpose(0, 1, 3, 2)
    spread_rows = conv_valid(jnp.pad(dconv, ((2, 2), (1, 1), (0, 0))), flipped)
    from_below = shifted_2(spread_rows[-1].astype(jnp.bfloat16), "sp", 1).astype(jnp.float32)
    from_above = shifted_2(spread_rows[0].astype(jnp.bfloat16), "sp", -1).astype(jnp.float32)
    dact = spread_rows[1:-1]
    dact = dact.at[0].add(from_below).at[-1].add(from_above)
    patches = jnp.stack(
        [
            padded[row_shift : row_shift + pixel_rows, col_shift : col_shift + pixel_cols].reshape(
                -1, LAT
            )
            for row_shift in range(3)
            for col_shift in range(3)
        ]
    )
    conv_product = jnp.einsum(
        "kpc,pd->ckd", patches, dconv.reshape(-1, LAT), preferred_element_type=jnp.float32
    )
    conv_part = (conv_product.reshape(LAT, 9 * LAT) * grad_scale).astype(jnp.bfloat16)
    dlat = layer_norm_reverse(dact.reshape(-1, LAT) * lat_gain, lhat, linv).astype(jnp.bfloat16)
    lat_part = rounded_part(pixels, dlat)
    dpixels = lax.dot_general(
        dlat, w_lateral, (((1,), (1,)), ((), ())), preferred_element_type=jnp.float32
    ).astype(jnp.bfloat16)
    dup = (
        dpixels.reshape(rows_here, 2, GRID_W, 2, DEC)
        .transpose(0, 2, 1, 3, 4)
        .reshape(tokens_here, 4 * DEC)
    )
    dec_part = rounded_part(feature, dup)
    g_deconv = lax.psum_scatter(dec_part, "sp", scatter_dimension=0, tiled=True).astype(jnp.float32)
    halfway_split = 0.5 * lax.dot_general(
        dup, deconv_full, (((1,), (1,)), ((), ())), preferred_element_type=jnp.float32
    )
    d_x1 = halfway_split.astype(jnp.bfloat16)
    dattn = lax.dot_general(
        out_full, d_x1, (((1,), (1,)), ((), ())), preferred_element_type=jnp.float32
    ).astype(jnp.bfloat16)
    out_product = lax.dot_general(
        attn_band, d_x1, (((1,), (0,)), ((), ())), preferred_element_type=jnp.float32
    )
    out_part = (out_product * grad_scale).astype(jnp.bfloat16)
    g_out = lax.psum_scatter(out_part, "sp", scatter_dimension=0, tiled=True).astype(jnp.float32)
    grad_head = lax.all_to_all(
        to_heads(dattn, pieces), "sp", split_axis=0, concat_axis=2, tiled=True
    )[0]
    grad_blocks = grad_head.reshape(HEAD, count_blocks, block).transpose(1, 0, 2)

    def backward_block(carry, operands):
        key_grad, value_grad = carry
        query_block, grad_block, weights = operands
        wide = weights.astype(jnp.float32)
        dprob = lax.dot_general(
            grad_block, value_head, (((0,), (0,)), ((), ())), preferred_element_type=jnp.float32
        )
        dscore = (wide * (dprob - jnp.sum(wide * dprob, axis=1, keepdims=True))).astype(
            jnp.bfloat16
        )
        query_grad = lax.dot_general(
            key_head, dscore, (((1,), (1,)), ((), ())), preferred_element_type=jnp.float32
        )
        query_grad = (query_grad * score_scale).astype(jnp.bfloat16)
        key_grad = key_grad + lax.dot_general(
            query_block, dscore, (((1,), (0,)), ((), ())), preferred_element_type=jnp.float32
        )
        value_grad = value_grad + lax.dot_general(
            grad_block, weights, (((1,), (0,)), ((), ())), preferred_element_type=jnp.float32
        )
        return ((key_grad, value_grad), query_grad)

    zero_grads = jnp.zeros(key_head.shape, jnp.float32)
    (key_grad, value_grad), query_grads = lax.scan(
        backward_block, (zero_grads, zero_grads), (query_blocks, grad_blocks, kept_weights)
    )
    query_grads = query_grads.transpose(1, 0, 2).reshape(1, HEAD, total_queries)
    dq_band = from_heads(
        lax.all_to_all(query_grads, "sp", split_axis=2, concat_axis=0, tiled=True), pieces
    )
    key_parts, value_parts = (
        lax.all_to_all(
            key_grad.astype(jnp.bfloat16), "sp", split_axis=1, concat_axis=0, tiled=True
        ).astype(key_grad.dtype),
        lax.all_to_all(
            value_grad.astype(jnp.bfloat16), "sp", split_axis=1, concat_axis=0, tiled=True
        ).astype(value_grad.dtype),
    )
    dk_band = (
        key_parts.reshape(HEADS, pieces, HEAD, tokens_here)
        .sum(axis=1)
        .reshape(inner, tokens_here)
        .astype(jnp.bfloat16)
    )
    dv_band = (
        value_parts.reshape(HEADS, pieces, HEAD, tokens_here)
        .sum(axis=1)
        .reshape(inner, tokens_here)
        .astype(jnp.bfloat16)
    )
    dqkv = jnp.concatenate([dq_band, dk_band, dv_band], axis=0)
    normalized_gradient = lax.dot_general(
        dqkv, qkv_full, (((0,), (1,)), ((), ())), preferred_element_type=jnp.float32
    )
    second_input_gradient = (
        halfway_split
        + layer_norm_reverse(
            normalized_gradient * layer_norm_gain, standardized_input, inverse_deviation
        )
    ).astype(jnp.bfloat16)
    g_lateral, conv_rows = (
        lax.psum_scatter(lat_part, "sp", scatter_dimension=0, tiled=True).astype(jnp.float32),
        lax.psum_scatter(conv_part, "sp", scatter_dimension=0, tiled=True).astype(jnp.float32),
    )
    g_conv = conv_rows.reshape(conv_rows.shape[0], 3, 3, LAT).transpose(1, 2, 0, 3)
    return (x_one, d_x1, second_input_gradient, g_out, g_deconv, g_lateral, g_conv)


def solution(mesh):
    return jax.shard_map(
        per_device,
        mesh=mesh,
        in_specs=(
            P(("img", "sp"), None),
            P(("img", "sp"), None),
            P(("img", "sp"), None, None),
            P(),
            P("sp", None),
            P("sp", None),
            P("sp", None),
            P(),
            P(),
            P(),
            P(),
        ),
        out_specs=(
            P(("img", "sp"), None),
            P(("img", "sp"), None),
            P(("img", "sp"), None),
            P(("img", "sp"), None),
            P(("img", "sp"), None),
            P(("img", "sp"), None),
            P("img", None, "sp", None),
        ),
        check_vma=False,
    )
```

profile of v0, /device:TPU:64, one launch (start us, length us, event | category | flops | bytes accessed | tf_op | source)
XLA Modules:
  0.0 913.9 jit_solution(12292637400893124045)
XLA Ops:
  11.8 161.1 %all-gather.11.cloned.1.call-done = bf16[32,44,1536]{2,1,0:T(8,128)(2,1)} async-done(((bf16[1,44,1536]{2,1,0:T(8,128)(2,1)}), bf16[32,44,1536]{2,1,0:T(8,128)(2,1)}) %all-gather.11.cloned.1.call-update) | async-done | bytes 4325392 | tf_op jit(solution)/shard_map/all_gather | solution.py:158
  172.9 7.0 reshape.331
  179.9 3.0 convolution_convert_fusion.1
  186.0 4.5 collective-permute-start
  191.1 138.8 %all-gather.9.cloned.1.call-done = bf16[32,22,1408]{2,1,0:T(8,128)(2,1)} async-done(((bf16[1,22,1408]{2,1,0:T(8,128)(2,1)}), bf16[32,22,1408]{2,1,0:T(8,128)(2,1)}) %all-gather.9.cloned.1.call-update) | async-done | bytes 1982480 | tf_op jit(solution)/shard_map/all_gather | solution.py:150
  329.9 3.8 reshape.329
  340.4 3.2 collective-permute-start.2
  356.2 4.9 fusion.94
  363.0 8.6 all-to-all-start.4
  371.7 126.9 %all-gather.7.cloned.1.call-done = bf16[32,44,2112]{2,1,0:T(8,128)(2,1)} async-done(((bf16[1,44,2112]{2,1,0:T(8,128)(2,1)}), bf16[32,44,2112]{2,1,0:T(8,128)(2,1)}) %all-gather.7.cloned.1.call-update) | async-done | bytes 5947408 | tf_op jit(solution)/shard_map/all_gather | solution.py:113
  498.5 8.8 reshape.327
  507.4 6.0 fusion.91
  514.7 8.3 all-to-all-start
  523.7 8.4 all-to-all-done
  533.1 3.9 all-to-all-start.2
  537.9 10.0 %all-to-all-done.2 = bf16[32,88,128]{2,1,0:T(8,128)(2,1)S(1)} async-done(((bf16[32,88,128]{2,1,0:T(8,128)(2,1)}), bf16[32,88,128]{2,1,0:T(8,128)(2,1)S(1)}, u32[]{:S(2)}, u32[]{:S(2)}) %all-to-all-start.2) | async-done | bytes 720928 | tf_op jit(solution)/shard_map/all_to_all | solution.py:125
  550.0 4.8 all-to-all-start.1
  559.8 5.9 all-to-all-done.1
  568.6 20.7 %while.29 = (s32[]{:T(128)}, bf16[2,88,512]{2,1,0:T(8,128)(2,1)S(1)}, bf16[2,512,4096]{2,1,0:T(8,128)(2,1)}, bf16[2,88,512]{2,1,0:T(8,128)(2,1)S(1)}, bf16[88,40...) while((s32[]{:T(128)}, bf16[2,88,512]{2,1,0:T(8,128)(2,1)S(1)}, ...), condition=%wide.region_5.6_spmd, body=%wide.region_2.5_spmd.sunk | while | flops 750824448 | bytes 106490008 | solution.py:145
  593.3 3.8 reduce.11
  599.2 4.8 all-to-all-start.3
  604.0 35.6 %while.30 = (s32[]{:T(128)}, f32[88,4096]{1,0:T(8,128)S(1)}, f32[88,4096]{1,0:T(8,128)}, bf16[2,88,512]{2,1,0:T(8,128)(2,1)S(1)}, bf16[2,88,512]{2,1,0:T(8,128)(...) while((s32[]{:T(128)}, f32[88,4096]{1,0:T(8,128)S(1)}, ...), condition=%wide.region_16.17_spmd.clone, body=%wide.region_14.16_spmd.clone.sunk | while | flops 1492606464 | bytes 77830880 | solution.py:246
  604.0 3.6 fusion.155
  607.6 6.0 fusion.156
  613.5 3.4 convolution_add_fusion.4
  616.9 3.4 convolution_add_fusion.5
  621.8 3.6 fusion.155
  625.4 6.0 fusion.156
  631.3 3.4 convolution_add_fusion.4
  634.7 3.4 convolution_add_fusion.5
  643.4 8.4 all-to-all-start.5
  653.5 7.2 all-to-all-done.5
  660.7 3.9 all-to-all-start.6
  671.0 3.4 fusion.27
  681.2 8.4 all-to-all-start.7
  689.6 107.1 %fusion.86 = (bf16[32,1408]{1,0:T(8,128)(2,1)S(1)}, bf16[48,1536]{1,0:T(8,128)(2,1)S(1)}, bf16[16,256]{1,0:T(8,128)(2,1)S(1)}) fusion(bf16[704,1408]{1,0:T(8,128)(2,1)} %multiply_convert_fusion, bf16[1408,1536]{1,0:T(8,128)(2,1)} %fusion.27, bf16[384,256]{1,0:T(8,128)(2,1)} %fusion.30), kind=kCustom, calls=%all-reduce-scatter.3 | all-reduce-scatter fusion | flops 3932163 | bytes 6751232
  803.3 5.4 collective-permute-start.20
  808.7 3.4 collective-permute-start.19
  812.1 5.1 collective-permute-start.18
  821.1 16.3 %reduce-scatter.8.cloned.1.call-done = bf16[8,2304]{1,0:T(8,128)(2,1)} async-done(((bf16[256,2304]{1,0:T(8,128)(2,1)}), bf16[8,2304]{1,0:T(8,128)(2,1)}) %reduce-scatter.8.cloned.1.call-update) | async-done | bytes 36880 | tf_op jit(solution)/shard_map/reduce_scatter | solution.py:285
  845.2 7.5 collective-permute-start.9
  863.8 3.7 collective-permute-start.6
  867.6 4.0 collective-permute-start.5
  871.6 2.9 collective-permute-start.4
  875.2 7.2 collective-permute-start.15
  884.9 5.2 collective-permute-start.16
  890.1 6.4 concatenate.22
  900.8 4.9 fusion.85
  (317 shorter events, 126.9 us)
Async XLA Ops:
  7.2 327.0 %copy-start = (bf16[3,3,256,256]{3,2,1,0:T(8,128)(2,1)S(1)}, bf16[3,3,256,256]{3,2,1,0:T(8,128)(2,1)}, u32[]{:S(2)}) copy-start(bf16[3,3,256,256]{3,2,1,0:T(8,128)(2,1)} %param.28) | copy-start | bytes 3538948
  7.2 165.7 %all-gather.11.cloned.1.call-start = ((), (), s32[]{:S(2)}) async-start(), calls=%async_computation.12 | async-start | bytes 4866048 | tf_op jit(solution)/shard_map/all_gather | solution.py:158
  7.9 322.0 %all-gather.9.cloned.1.call-start = ((), (), s32[]{:S(2)}) async-start(), calls=%async_computation.11 | async-start | bytes 2230272 | tf_op jit(solution)/shard_map/all_gather | solution.py:150
  8.7 489.9 %all-gather.7.cloned.1.call-start = ((), (), s32[]{:S(2)}) async-start(), calls=%async_computation.10 | async-start | bytes 6893568 | tf_op jit(solution)/shard_map/all_gather | solution.py:113
  10.5 496.9 %copy-start.44 = (f32[128]{0:T(128)}, f32[128]{0:T(128)S(1)}, u32[]{:S(2)}) copy-start(f32[128]{0:T(128)S(1)} %broadcast_multiply_fusion.8) | copy-start | bytes 1540
  11.8 168.1 %copy-start.8 = (bf16[128,1408]{1,0:T(8,128)(2,1)S(1)}, bf16[128,1408]{1,0:T(8,128)(2,1)}, u32[]{:S(2)}) copy-start(bf16[128,1408]{1,0:T(8,128)(2,1)} %param.20) | copy-start | bytes 1081348
  11.8 168.1 %copy-start.12 = (bf16[128,1408]{1,0:T(8,128)(2,1)S(1)}, bf16[128,1408]{1,0:T(8,128)(2,1)}, u32[]{:S(2)}) copy-start(bf16[128,1408]{1,0:T(8,128)(2,1)} %param.19) | copy-start | bytes 1081348
  183.9 149.8 %copy-start.25 = (bf16[512,384]{1,0:T(8,128)(2,1)}, bf16[512,384]{1,0:T(8,128)(2,1)S(1)}, u32[]{:S(2)}) copy-start(bf16[512,384]{1,0:T(8,128)(2,1)S(1)} %reshape.267) | copy-start | bytes 1179652
  184.7 149.0 %collective-permute-start.1 = (bf16[1,128,256]{2,1,0:T(8,128)(2,1)S(1)}, bf16[1,128,256]{2,1,0:T(8,128)(2,1)S(1)}, u32[]{:S(2)}, u32[]{:S(2)}) collective-permute-start(bf16[1,128,256]{2,1,0:T(8,128)(2,1)S(1)} %get-tuple-element.295), channel_id=1, source_target_pairs={{1,0},{2,1},{3,2},{4,3},{5,4},{6,5},{7,6},{8,7},{9,8},{10,9},{11,1... | collective-permute-start | bytes 196616 | tf_op jit(solution)/shard_map/ppermute | solution.py:25
  186.0 147.7 %collective-permute-start = (bf16[1,128,256]{2,1,0:T(8,128)(2,1)S(1)}, bf16[1,128,256]{2,1,0:T(8,128)(2,1)S(1)}, u32[]{:S(2)}, u32[]{:S(2)}) collective-permute-start(bf16[1,128,256]{2,1,0:T(8,128)(2,1)S(1)} %get-tuple-element.294), channel_id=1, source_target_pairs={{0,1},{1,2},{2,3},{3,4},{4,5},{5,6},{6,7},{7,8},{8,9},{9,10},{10,1... | collective-permute-start | bytes 196616 | tf_op jit(solution)/shard_map/ppermute | solution.py:22
  340.4 6.2 collective-permute-start.2
  344.8 6.5 collective-permute-start.3
  361.1 146.3 %copy-start.16 = (bf16[128,1408]{1,0:T(8,128)(2,1)}, bf16[128,1408]{1,0:T(8,128)(2,1)S(1)}, u32[]{:S(2)}) copy-start(bf16[128,1408]{1,0:T(8,128)(2,1)S(1)} %get-tuple-element.302) | copy-start | bytes 1081348
  363.0 151.7 %all-to-all-start.4 = ((bf16[32,88,32]{1,2,0:T(8,128)(2,1)}), bf16[32,88,32]{1,2,0:T(8,128)(2,1)S(1)}, u32[]{:S(2)}, u32[]{:S(2)}) async-start(bf16[32,88,32]{1,2,0:T(8,128)(2,1)} %bitcast.51), calls=%async_computation.4 | async-start | bytes 524288 | tf_op jit(solution)/shard_map/all_to_all | solution.py:218
  371.6 135.7 %copy-start.40 = (f32[1408]{0:T(1024)S(1)}, f32[1408]{0:T(1024)}, u32[]{:S(2)}) copy-start(f32[1408]{0:T(1024)} %param.22) | copy-start | bytes 16900
  371.7 135.7 %copy-start.48 = (f32[128]{0:T(128)S(1)}, f32[128]{0:T(128)}, u32[]{:S(2)}) copy-start(f32[128]{0:T(128)} %add_rsqrt_fusion.2) | copy-start | bytes 1540
  514.7 17.4 %all-to-all-start = ((bf16[32,88,32]{1,2,0:T(8,128)(2,1)}), bf16[32,88,32]{1,2,0:T(8,128)(2,1)S(1)}, u32[]{:S(2)}, u32[]{:S(2)}) async-start(bf16[32,88,32]{1,2,0:T(8,128)(2,1)} %bitcast.7), calls=%async_computation | async-start | bytes 524288 | tf_op jit(solution)/shard_map/all_to_all | solution.py:120
  533.1 14.8 %all-to-all-start.2 = ((bf16[32,88,128]{2,1,0:T(8,128)(2,1)}), bf16[32,88,128]{2,1,0:T(8,128)(2,1)S(1)}, u32[]{:S(2)}, u32[]{:S(2)}) async-start(bf16[32,88,128]{2,1,0:T(8,128)(2,1)} %bitcast.17), calls=%async_computation.2 | async-start | bytes 1441792 | tf_op jit(solution)/shard_map/all_to_all | solution.py:125
  550.0 15.7 %all-to-all-start.1 = ((bf16[32,88,128]{2,1,0:T(8,128)(2,1)}), bf16[32,88,128]{2,1,0:T(8,128)(2,1)}, u32[]{:S(2)}, u32[]{:S(2)}) async-start(bf16[32,88,128]{2,1,0:T(8,128)(2,1)} %bitcast.306), calls=%async_computation.1 | async-start | bytes 1441792 | tf_op jit(solution)/shard_map/all_to_all | solution.py:124
  599.2 44.2 %all-to-all-start.3 = ((bf16[32,2,1408]{2,1,0:T(2,128)(2,1)}), bf16[32,2,1408]{2,1,0:T(2,128)(2,1)}, u32[]{:S(2)}, u32[]{:S(2)}) async-start(bf16[32,2,1408]{2,1,0:T(2,128)(2,1)} %reshape.339), calls=%async_computation.3 | async-start | bytes 360448 | tf_op jit(solution)/shard_map/all_to_all | solution.py:148
  643.4 17.3 %all-to-all-start.5 = ((bf16[32,2,1408]{2,1,0:T(2,128)(2,1)}), bf16[32,2,1408]{2,1,0:T(2,128)(2,1)S(1)}, u32[]{:S(2)}, u32[]{:S(2)}) async-start(bf16[32,2,1408]{2,1,0:T(2,128)(2,1)} %reshape.341), calls=%async_computation.5 | async-start | bytes 360448 | tf_op jit(solution)/shard_map/all_to_all | solution.py:251
  660.7 19.6 %all-to-all-start.6 = ((bf16[88,32,128]{2,0,1:T(8,128)(2,1)}), bf16[88,32,128]{2,0,1:T(8,128)(2,1)S(1)}, u32[]{:S(2)}, u32[]{:S(2)}) async-start(bf16[88,32,128]{2,0,1:T(8,128)(2,1)} %copy_bitcast_fusion.3), calls=%async_computation.6 | async-start | bytes 1441792 | tf_op jit(solution)/shard_map/all_to_all | solution.py:254
  664.6 172.8 %reduce-scatter.8.cloned.1.call-start = ((), (), s32[]{:S(2)}) async-start(), calls=%async_computation.9 | async-start | bytes 1216512 | tf_op jit(solution)/shard_map/reduce_scatter | solution.py:285
  681.2 217.9 %all-to-all-start.7 = ((bf16[88,32,128]{2,0,1:T(8,128)(2,1)}), bf16[88,32,128]{2,0,1:T(8,128)(2,1)}, u32[]{:S(2)}, u32[]{:S(2)}) async-start(bf16[88,32,128]{2,0,1:T(8,128)(2,1)} %copy_bitcast_fusion.2), calls=%async_computation.7 | async-start | bytes 1441792 | tf_op jit(solution)/shard_map/all_to_all | solution.py:257
  689.6 129.5 %copy-start.51 = (u32[256]{0:T(256)S(1)}, u32[256]{0:T(256)}, u32[]{:S(2)}) copy-start(u32[256]{0:T(256)} %constant.147) | copy-start | bytes 3076
  689.6 165.0 %copy-start.11 = (bf16[704,1408]{1,0:T(8,128)(2,1)S(1)}, bf16[704,1408]{1,0:T(8,128)(2,1)}, u32[]{:S(2)}) copy-start(bf16[704,1408]{1,0:T(8,128)(2,1)} %reshape.329) | copy-start | bytes 5947396
  796.8 59.1 %copy-start.37 = (bf16[32,2,1408]{2,1,0:T(2,128)(2,1)S(1)}, bf16[32,2,1408]{2,1,0:T(2,128)(2,1)}, u32[]{:S(2)}) copy-start(bf16[32,2,1408]{2,1,0:T(2,128)(2,1)} %copy-done.36) | copy-start | bytes 540676
  796.8 15.3 %collective-permute-start.23 = (bf16[16,256]{1,0:T(8,128)(2,1)S(1)}, bf16[16,256]{1,0:T(8,128)(2,1)S(1)}, u32[]{:S(2)}, u32[]{:S(2)}) collective-permute-start(bf16[16,256]{1,0:T(8,128)(2,1)S(1)} %get-tuple-element.275), channel_id=1, source_target_pairs={{0,7},{1,8},{2,9},{3,10},{4,11},{5,12},{6,13},{7,14},{8,15},{9,16}... | collective-permute-start | bytes 24584
  798.2 19.1 %collective-permute-start.22 = (bf16[16,256]{1,0:T(8,128)(2,1)S(1)}, bf16[16,256]{1,0:T(8,128)(2,1)S(1)}, u32[]{:S(2)}, u32[]{:S(2)}) collective-permute-start(bf16[16,256]{1,0:T(8,128)(2,1)S(1)} %get-tuple-element.275), channel_id=1, source_target_pairs={{0,6},{1,7},{2,8},{3,9},{4,10},{5,11},{6,12},{7,13},{8,14},{9,15},... | collective-permute-start | bytes 24584
  799.5 9.2 %collective-permute-start.24 = (bf16[12,256]{1,0:T(8,128)(2,1)S(1)}, bf16[12,256]{1,0:T(8,128)(2,1)S(1)}, u32[]{:S(2)}, u32[]{:S(2)}) collective-permute-start(bf16[12,256]{1,0:T(8,128)(2,1)S(1)} %slice.171), channel_id=1, source_target_pairs={{0,8},{1,9},{2,10},{3,11},{4,12},{5,13},{6,14},{7,15},{8,16},{9,17... | collective-permute-start | bytes 18440
  800.8 38.7 %collective-permute-start.21 = (bf16[16,256]{1,0:T(8,128)(2,1)S(1)}, bf16[16,256]{1,0:T(8,128)(2,1)S(1)}, u32[]{:S(2)}, u32[]{:S(2)}) collective-permute-start(bf16[16,256]{1,0:T(8,128)(2,1)S(1)} %get-tuple-element.275), channel_id=1, source_target_pairs={{0,5},{1,6},{2,7},{3,8},{4,9},{5,10},{6,11},{7,12},{8,13},{9,14},{... | collective-permute-start | bytes 24584
  803.3 38.1 %collective-permute-start.20 = (bf16[16,256]{1,0:T(8,128)(2,1)S(1)}, bf16[16,256]{1,0:T(8,128)(2,1)S(1)}, u32[]{:S(2)}, u32[]{:S(2)}) collective-permute-start(bf16[16,256]{1,0:T(8,128)(2,1)S(1)} %get-tuple-element.275), channel_id=1, source_target_pairs={{0,4},{1,5},{2,6},{3,7},{4,8},{5,9},{6,10},{7,11},{8,12},{9,13},{1... | collective-permute-start | bytes 24584
  808.7 34.6 %collective-permute-start.19 = (bf16[16,256]{1,0:T(8,128)(2,1)S(1)}, bf16[16,256]{1,0:T(8,128)(2,1)S(1)}, u32[]{:S(2)}, u32[]{:S(2)}) collective-permute-start(bf16[16,256]{1,0:T(8,128)(2,1)S(1)} %get-tuple-element.275), channel_id=1, source_target_pairs={{0,3},{1,4},{2,5},{3,6},{4,7},{5,8},{6,9},{7,10},{8,11},{9,12},{10... | collective-permute-start | bytes 24584
  812.1 33.1 %collective-permute-start.18 = (bf16[16,256]{1,0:T(8,128)(2,1)S(1)}, bf16[16,256]{1,0:T(8,128)(2,1)S(1)}, u32[]{:S(2)}, u32[]{:S(2)}) collective-permute-start(bf16[16,256]{1,0:T(8,128)(2,1)S(1)} %get-tuple-element.275), channel_id=1, source_target_pairs={{0,2},{1,3},{2,4},{3,5},{4,6},{5,7},{6,8},{7,9},{8,10},{9,11},{10,... | collective-permute-start | bytes 24584
  817.3 35.5 %collective-permute-start.17 = (bf16[16,256]{1,0:T(8,128)(2,1)S(1)}, bf16[16,256]{1,0:T(8,128)(2,1)S(1)}, u32[]{:S(2)}, u32[]{:S(2)}) collective-permute-start(bf16[16,256]{1,0:T(8,128)(2,1)S(1)} %get-tuple-element.275), channel_id=1, source_target_pairs={{0,1},{1,2},{2,3},{3,4},{4,5},{5,6},{6,7},{7,8},{8,9},{9,10},{10,1... | collective-permute-start | bytes 24584
  839.5 22.6 %collective-permute-start.12 = (bf16[32,1408]{1,0:T(8,128)(2,1)S(1)}, bf16[32,1408]{1,0:T(8,128)(2,1)}, u32[]{:S(2)}, u32[]{:S(2)}) collective-permute-start(bf16[32,1408]{1,0:T(8,128)(2,1)S(1)} %get-tuple-element.273), channel_id=1, source_target_pairs={{0,9},{1,10},{2,11},{3,12},{4,13},{5,14},{6,15},{7,16},{8,17},{9,1... | collective-permute-start | bytes 270344
  841.4 22.4 %collective-permute-start.11 = (bf16[32,1408]{1,0:T(8,128)(2,1)S(1)}, bf16[32,1408]{1,0:T(8,128)(2,1)}, u32[]{:S(2)}, u32[]{:S(2)}) collective-permute-start(bf16[32,1408]{1,0:T(8,128)(2,1)S(1)} %get-tuple-element.273), channel_id=1, source_target_pairs={{0,8},{1,9},{2,10},{3,11},{4,12},{5,13},{6,14},{7,15},{8,16},{9,17... | collective-permute-start | bytes 270344
  843.3 24.3 %collective-permute-start.10 = (bf16[32,1408]{1,0:T(8,128)(2,1)S(1)}, bf16[32,1408]{1,0:T(8,128)(2,1)}, u32[]{:S(2)}, u32[]{:S(2)}) collective-permute-start(bf16[32,1408]{1,0:T(8,128)(2,1)S(1)} %get-tuple-element.273), channel_id=1, source_target_pairs={{0,7},{1,8},{2,9},{3,10},{4,11},{5,12},{6,13},{7,14},{8,15},{9,16}... | collective-permute-start | bytes 270344
  845.2 26.4 %collective-permute-start.9 = (bf16[32,1408]{1,0:T(8,128)(2,1)S(1)}, bf16[32,1408]{1,0:T(8,128)(2,1)}, u32[]{:S(2)}, u32[]{:S(2)}) collective-permute-start(bf16[32,1408]{1,0:T(8,128)(2,1)S(1)} %get-tuple-element.273), channel_id=1, source_target_pairs={{0,6},{1,7},{2,8},{3,9},{4,10},{5,11},{6,12},{7,13},{8,14},{9,15},... | collective-permute-start | bytes 270344
  852.7 7.0 collective-permute-start.13
  859.8 15.4 %collective-permute-start.8 = (bf16[32,1408]{1,0:T(8,128)(2,1)S(1)}, bf16[32,1408]{1,0:T(8,128)(2,1)S(1)}, u32[]{:S(2)}, u32[]{:S(2)}) collective-permute-start(bf16[32,1408]{1,0:T(8,128)(2,1)S(1)} %get-tuple-element.273), channel_id=1, source_target_pairs={{0,5},{1,6},{2,7},{3,8},{4,9},{5,10},{6,11},{7,12},{8,13},{9,14},{... | collective-permute-start | bytes 270344
  862.0 20.4 %collective-permute-start.7 = (bf16[32,1408]{1,0:T(8,128)(2,1)S(1)}, bf16[32,1408]{1,0:T(8,128)(2,1)S(1)}, u32[]{:S(2)}, u32[]{:S(2)}) collective-permute-start(bf16[32,1408]{1,0:T(8,128)(2,1)S(1)} %get-tuple-element.273), channel_id=1, source_target_pairs={{0,4},{1,5},{2,6},{3,7},{4,8},{5,9},{6,10},{7,11},{8,12},{9,13},{1... | collective-permute-start | bytes 270344
  863.8 21.1 %collective-permute-start.6 = (bf16[32,1408]{1,0:T(8,128)(2,1)S(1)}, bf16[32,1408]{1,0:T(8,128)(2,1)S(1)}, u32[]{:S(2)}, u32[]{:S(2)}) collective-permute-start(bf16[32,1408]{1,0:T(8,128)(2,1)S(1)} %get-tuple-element.273), channel_id=1, source_target_pairs={{0,3},{1,4},{2,5},{3,6},{4,7},{5,8},{6,9},{7,10},{8,11},{9,12},{10... | collective-permute-start | bytes 270344
  867.6 22.5 %collective-permute-start.5 = (bf16[32,1408]{1,0:T(8,128)(2,1)S(1)}, bf16[32,1408]{1,0:T(8,128)(2,1)S(1)}, u32[]{:S(2)}, u32[]{:S(2)}) collective-permute-start(bf16[32,1408]{1,0:T(8,128)(2,1)S(1)} %get-tuple-element.273), channel_id=1, source_target_pairs={{0,2},{1,3},{2,4},{3,5},{4,6},{5,7},{6,8},{7,9},{8,10},{9,11},{10,... | collective-permute-start | bytes 270344
  871.6 18.5 %collective-permute-start.4 = (bf16[32,1408]{1,0:T(8,128)(2,1)S(1)}, bf16[32,1408]{1,0:T(8,128)(2,1)S(1)}, u32[]{:S(2)}, u32[]{:S(2)}) collective-permute-start(bf16[32,1408]{1,0:T(8,128)(2,1)S(1)} %get-tuple-element.273), channel_id=1, source_target_pairs={{0,1},{1,2},{2,3},{3,4},{4,5},{5,6},{6,7},{7,8},{8,9},{9,10},{10,1... | collective-permute-start | bytes 270344
  875.2 22.1 %collective-permute-start.15 = (bf16[48,1536]{1,0:T(8,128)(2,1)S(1)}, bf16[48,1536]{1,0:T(8,128)(2,1)S(1)}, u32[]{:S(2)}, u32[]{:S(2)}) collective-permute-start(bf16[48,1536]{1,0:T(8,128)(2,1)S(1)} %get-tuple-element.274), channel_id=1, source_target_pairs={{0,2},{1,3},{2,4},{3,5},{4,6},{5,7},{6,8},{7,9},{8,10},{9,11},{10,... | collective-permute-start | bytes 442376
  882.4 14.8 %collective-permute-start.14 = (bf16[48,1536]{1,0:T(8,128)(2,1)S(1)}, bf16[48,1536]{1,0:T(8,128)(2,1)S(1)}, u32[]{:S(2)}, u32[]{:S(2)}) collective-permute-start(bf16[48,1536]{1,0:T(8,128)(2,1)S(1)} %get-tuple-element.274), channel_id=1, source_target_pairs={{0,1},{1,2},{2,3},{3,4},{4,5},{5,6},{6,7},{7,8},{8,9},{9,10},{10,1... | collective-permute-start | bytes 442376
  884.9 12.3 %collective-permute-start.16 = (bf16[28,1536]{1,0:T(8,128)(2,1)S(1)}, bf16[28,1536]{1,0:T(8,128)(2,1)S(1)}, u32[]{:S(2)}, u32[]{:S(2)}) collective-permute-start(bf16[28,1536]{1,0:T(8,128)(2,1)S(1)} %slice.170), channel_id=1, source_target_pairs={{0,3},{1,4},{2,5},{3,6},{4,7},{5,8},{6,9},{7,10},{8,11},{9,12},{10... | collective-permute-start | bytes 258056
  (48 other events, 266.1 us)
Sparse Core Ops, SparseCore 0:
  9.8 163.0 all-gather.10
  174.7 155.2 all-gather.8
  331.7 166.7 all-gather.6
  669.1 168.1 reduce-scatter.7
where the time goes:
time: 923 us; the launch traced here: 914 us
  waiting for transfers between devices  479 us (52%)
  starting transfers between devices  129 us (14%)
  blocking collectives  107 us (12%)
  local copies, waits for them, and re-layouts  79.7 us (9%)
  matrix products  62.3 us (7%)
  other arithmetic  38.5 us (4%)
  between operations  17.1 us (2%)
    all_gather x1, waiting for transfers between devices, per_device(): deconv_full = lax.all_gather(w_deconv, 'sp', axis=0, tiled=True)  161 us
    all_gather x1, waiting for transfers between devices, per_device(): out_full = lax.all_gather(w_out, 'sp', axis=0, tiled=True)  139 us
    all_gather x1, waiting for transfers between devices, per_device(): qkv_full = lax.all_gather(w_qkv, 'sp', axis=0, tiled=True)  127 us
    unnamed x1, blocking collectives  107 us
    unnamed x21, starting transfers between devices  67.1 us
    unnamed x124, local copies, waits for them, and re-layouts  43.2 us
  transfers between devices with their start and end apart: 37, of which 9 were waited for; matrix products, arithmetic and copies ran while one was open for 26% of the time, Pallas kernels for 0%

commit v1 on v0

--- a/solution.py
+++ b/solution.py
@@ -1,6 +1,10 @@
+import functools
+
 import jax
 import jax.numpy as jnp
 from jax import lax
+from jax.experimental import pallas as pl
+from jax.experimental.pallas import tpu as pltpu
 from jax.sharding import PartitionSpec as P
 
 HEADS = 8
@@ -85,6 +89,192 @@
         features.reshape(HEADS, 1, width, columns), (HEADS, pieces, width, columns)
     )
     return spread.reshape(HEADS * pieces, width, columns)
+
+
+MESH = pl.DeviceIdType.MESH
+ROWS_PAD = 48
+HEAD_PAD = 96
+OUT_ROWS_PAD = 32
+OUT_COLS_PAD = 1536
+
+
+def place():
+    s, i = lax.axis_index("sp"), lax.axis_index("img")
+    return s // 8, (s // 4) % 2, s % 4, i // 2, i % 2
+
+
+def at_sp(x, zl, y):
+    return {"sp": (x * 2 + zl) * 4 + y}
+
+
+def greet(targets):
+    barrier = pltpu.get_barrier_semaphore()
+    for target in targets:
+        pl.semaphore_signal(barrier, inc=1, device_id=target, device_id_type=MESH)
+    pl.semaphore_wait(barrier, len(targets))
+
+
+def gather_kernel(shapes, *refs):
+    count = len(shapes)
+    ins, outs, shards, packs = (refs[k * count : (k + 1) * count] for k in range(4))
+    send, recv, local = refs[4 * count :]
+    x, zl, y, zh, core = place()
+    xm, xp, xo = (x + 3) % 4, (x + 1) % 4, (x + 2) % 4
+    left, right = at_sp(xm, zl, y), at_sp(xp, zl, y)
+    across = (x * 2 + 1 - zl) * 4 + y
+    up = {"img": ((zh + zl) % 4) * 2 + core, "sp": across}
+    down = {"img": ((zh + zl + 3) % 4) * 2 + core, "sp": across}
+    twin = {"img": zh * 2 + 1 - core}
+    column = [at_sp(x, zl, (y + k) % 4) for k in (1, 2, 3)]
+    greet(column + [left, right, up, down, twin])
+    copies = {}
+
+    def push(a, slot, src, dst, target):
+        copy = pltpu.make_async_remote_copy(
+            src_ref=src,
+            dst_ref=dst,
+            send_sem=send.at[a, slot],
+            recv_sem=recv.at[a, slot],
+            device_id=target,
+            device_id_type=MESH,
+        )
+        copy.start()
+        copies[a, slot] = copy
+
+    def part(a):
+        half = shapes[a][3] // 2
+        return half, pl.multiple_of(core * half, 128)
+
+    def region(a, bx, bz, lo, size):
+        half, first = part(a)
+        return outs[a].at[bx * 2 + bz, pl.ds(lo, size), pl.ds(first, half)]
+
+    def forward(a, slot, bx, bz, lo, size, target):
+        piece = region(a, bx, bz, lo, size)
+        push(a, slot, piece, piece, target)
+
+    for a in range(count):
+        half, first = part(a)
+        mine = ins[a].at[:, pl.ds(first, half)]
+        for k in range(3):
+            push(a, k, mine, shards[a].at[y], column[k])
+        shards[a][y] = ins[a][:, pl.ds(first, half)]
+    keeps = []
+    for a in range(count):
+        rows, per, block, _ = shapes[a]
+        half, first = part(a)
+        low = (block // 32) * 16
+        high = block - low
+        for k in range(3):
+            copies[a, k].wait_recv()
+        r = lax.broadcasted_iota(jnp.int32, (block, 4 * rows), 0)
+        c = lax.broadcasted_iota(jnp.int32, (block, 4 * rows), 1)
+        skipped = jnp.zeros_like(r)
+        for k in (1, 2, 3):
+            skipped += jnp.where(r >= k * per, rows - per, 0)
+        pick = jnp.where(c == r + skipped, 1.0, 0.0).astype(jnp.bfloat16)
+        packs[a][...] = jnp.dot(
+            pick, shards[a][...].reshape(4 * rows, half), preferred_element_type=jnp.float32
+        ).astype(jnp.bfloat16)
+        own, whole = packs[a], region(a, x, zl, 0, block)
+        keep = pltpu.make_async_copy(own, whole, local.at[a])
+        keep.start()
+        keeps.append(keep)
+        push(a, 3, own, whole, right)
+        push(a, 4, own, whole, left)
+        push(a, 7, own.at[pl.ds(0, low)], region(a, x, zl, 0, low), up)
+        push(a, 8, own.at[pl.ds(low, high)], region(a, x, zl, low, high), down)
+        push(a, 15, own, whole, twin)
+
+    def near(a):
+        block = shapes[a][2]
+        low = (block // 32) * 16
+        high = block - low
+        copies[a, 3].wait_recv()
+        forward(a, 5, xm, zl, 0, low, right)
+        forward(a, 9, xm, zl, 0, low, up)
+        forward(a, 10, xm, zl, low, high, down)
+        forward(a, 16, xm, zl, 0, block, twin)
+        copies[a, 4].wait_recv()
+        forward(a, 6, xp, zl, low, high, left)
+        forward(a, 11, xp, zl, 0, low, up)
+        forward(a, 12, xp, zl, low, high, down)
+        forward(a, 17, xp, zl, 0, block, twin)
+
+    def far(a):
+        block = shapes[a][2]
+        low = (block // 32) * 16
+        high = block - low
+        copies[a, 5].wait_recv()
+        forward(a, 13, xo, zl, 0, low, up)
+        forward(a, 18, xo, zl, 0, low, twin)
+        copies[a, 6].wait_recv()
+        forward(a, 14, xo, zl, low, high, down)
+        forward(a, 19, xo, zl, low, high, twin)
+
+    def deep(a):
+        block = shapes[a][2]
+        low = (block // 32) * 16
+        high = block - low
+        for n, bx in enumerate((x, xm, xp, xo)):
+            copies[a, 7 + 2 * n].wait_recv()
+            forward(a, 20 + 2 * n, bx, 1 - zl, 0, low, twin)
+            copies[a, 8 + 2 * n].wait_recv()
+            forward(a, 21 + 2 * n, bx, 1 - zl, low, high, twin)
+
+    for step in range(count + 2):
+        if step < count:
+            near(step)
+        if 0 <= step - 1 < count:
+            far(step - 1)
+        if 0 <= step - 2 < count:
+            deep(step - 2)
+    for a in range(count):
+        for slot in range(15, 28):
+            copies[a, slot].wait_recv()
+    for keep in keeps:
+        keep.wait()
+    for copy in copies.values():
+        copy.wait_send()
+
+
+def gather_weights(shards, pers):
+    count = len(shards)
+    shapes = []
+    for shard, per in zip(shards, pers):
+        block = -(-4 * per // 16) * 16
+        shapes.append((shard.shape[0], per, block, shard.shape[1]))
+    halves = [(rows, block, width // 2) for rows, _, block, width in shapes]
+    return pl.pallas_call(
+        functools.partial(gather_kernel, shapes),
+        out_shape=[
+            jax.ShapeDtypeStruct((8, block, width), jnp.bfloat16) for _, _, block, width in shapes
+        ],
+        in_specs=[pl.BlockSpec(memory_space=pltpu.VMEM)] * count,
+        out_specs=[pl.BlockSpec(memory_space=pl.ANY)] * count,
+        scratch_shapes=[pltpu.VMEM((4, rows, half), jnp.bfloat16) for rows, _, half in halves]
+        + [pltpu.VMEM((block, half), jnp.bfloat16) for _, block, half in halves]
+        + [
+            pltpu.SemaphoreType.DMA((count, 28)),
+            pltpu.SemaphoreType.DMA((count, 28)),
+            pltpu.SemaphoreType.DMA((count,)),
+        ],
+        compiler_params=pltpu.CompilerParams(
+            collective_id=0, has_side_effects=True, vmem_limit_bytes=32 * 2**20
+        ),
+    )(*shards)
+
+
+def pad_heads(features):
+    groups = features.reshape(-1, HEAD, features.shape[-1])
+    return jnp.pad(groups, ((0, 0), (0, HEAD_PAD - HEAD), (0, 0))).reshape(
+        -1, features.shape[-1]
+    )
+
+
+def trim_heads(features):
+    groups = features.reshape(-1, HEAD_PAD, features.shape[-1])
+    return groups[:, :HEAD].reshape(-1, features.shape[-1])
 
 
 def per_device(
@@ -110,9 +300,25 @@
         second_stream_state.astype(jnp.float32)
     )
     normalized_rows = (standardized_input * layer_norm_gain).astype(jnp.bfloat16)
-    qkv_full = lax.all_gather(w_qkv, "sp", axis=0, tiled=True)
-    projected = lax.dot_general(
-        qkv_full, normalized_rows, (((0,), (1,)), ((), ())), preferred_element_type=jnp.float32
+    depth, out_depth = w_qkv.shape[0], w_out.shape[0]
+    qkv_shard = jnp.pad(
+        w_qkv.reshape(depth, 3 * HEADS, HEAD),
+        ((0, ROWS_PAD - depth), (0, 0), (0, HEAD_PAD - HEAD)),
+    ).reshape(ROWS_PAD, 3 * HEADS * HEAD_PAD)
+    out_shard = jnp.pad(
+        w_out, ((0, OUT_ROWS_PAD - out_depth), (0, OUT_COLS_PAD - w_out.shape[1]))
+    )
+    deconv_shard = jnp.pad(w_deconv, ((0, ROWS_PAD - depth), (0, 0)))
+    deconv_full, qkv_full, out_full = gather_weights(
+        [deconv_shard, qkv_shard, out_shard], [depth, depth, out_depth]
+    )
+    deconv_full = deconv_full.reshape(devices * depth, -1)
+    qkv_full = qkv_full.reshape(devices * depth, -1)
+    out_full = out_full[:, :HEAD, : w_out.shape[1]].reshape(inner, -1)
+    projected = trim_heads(
+        lax.dot_general(
+            qkv_full, normalized_rows, (((0,), (1,)), ((), ())), preferred_element_type=jnp.float32
+        )
     )
     queries = (projected[:inner] * score_scale).astype(jnp.bfloat16)
     keys = projected[inner : 2 * inner].astype(jnp.bfloat16)
@@ -147,7 +353,6 @@
     attn_band = from_heads(
         lax.all_to_all(attended, "sp", split_axis=2, concat_axis=0, tiled=True), pieces
     )
-    out_full = lax.all_gather(w_out, "sp", axis=0, tiled=True)
     mixed = lax.dot_general(
         attn_band, out_full, (((0,), (0,)), ((), ())), preferred_element_type=jnp.float32
     )
@@ -155,7 +360,6 @@
     feature = ((y_one.astype(jnp.float32) + second_stream_state.astype(jnp.float32)) * 0.5).astype(
         jnp.bfloat16
     )
-    deconv_full = lax.all_gather(w_deconv, "sp", axis=0, tiled=True)
     upsampled = jnp.dot(feature, deconv_full, preferred_element_type=jnp.float32).astype(
         jnp.bfloat16
     )
@@ -272,7 +476,7 @@
     )
     dqkv = jnp.concatenate([dq_band, dk_band, dv_band], axis=0)
     normalized_gradient = lax.dot_general(
-        dqkv, qkv_full, (((0,), (1,)), ((), ())), preferred_element_type=jnp.float32
+        pad_heads(dqkv), qkv_full, (((0,), (1,)), ((), ())), preferred_element_type=jnp.float32
     )
     second_input_gradient = (
         halfway_split

time: 923 us -> 547 us (0.59)
  waiting for transfers between devices: 479 us -> 32.3 us
  Pallas kernels: 0 us -> 54.2 us
  local copies, waits for them, and re-layouts: 79.7 us -> 89 us
    all_gather x3 -> x0, waiting for transfers between devices: 427 us -> none  [the longest x1 161 us: per_device(): deconv_full = lax.all_gather(w_deconv, 'sp', axis=0, tiled=True)]
    pallas_call x0 -> x1, Pallas kernels: none -> 54.2 us  [gather_weights(): pl.pallas_call(functools.partial(gather_kernel, shapes), out_shape=[jax.S...]
    reduce_scatter x1, waiting for transfers between devices: 16.3 us -> 0.01 us  [per_device(): lax.psum_scatter(conv_part, 'sp', scatter_dimension=0, tiled=True)]
    unnamed x124 -> x119, local copies, waits for them, and re-layouts: 43.2 us -> 28.7 us
    dot_general x0 -> x1, local copies, waits for them, and re-layouts: none -> 9.58 us  [per_device(): lax.dot_general(qkv_full, normalized_rows, (((0,), (1,)), ((), ())), pref...]
  transfers between devices with their start and end apart: 37 -> 34, of which waited for: 9 -> 5; matrix products, arithmetic and copies ran while one was open for 26% -> 43% of each run, Pallas kernels for 0% -> 0%
where the time goes in v1:
time: 547 us; the launch traced here: 537 us
  starting transfers between devices  129 us (24%)
  blocking collectives  109 us (20%)
  local copies, waits for them, and re-layouts  89 us (16%)
  matrix products  65.2 us (12%)
  Pallas kernels  54.2 us (10%)
  other arithmetic  41.7 us (8%)
  waiting for transfers between devices  32.3 us (6%)
  between operations  17.1 us (3%)
    unnamed x1, blocking collectives  109 us
    unnamed x21, starting transfers between devices  63.4 us
    pallas_call x1, Pallas kernels, gather_weights(): pl.pallas_call(functools.partial(gather_kernel, shapes), out_shape=[jax.S...  54.2 us
    unnamed x119, local copies, waits for them, and re-layouts  28.7 us
    convert_element_type x2, other arithmetic, backward_block(): (wide * (dprob - jnp.sum(wide * dprob, axis=1, keepdims=True))).astype(jn...  11.9 us
  transfers between devices with their start and end apart: 34, of which 5 were waited for; matrix products, arithmetic and copies ran while one was open for 43% of the time, Pallas kernels for 0%

profile of v1, /device:TPU:64, one launch (start us, length us, event | category | flops | bytes accessed | tf_op | source)
XLA Modules:
  0.0 537.2 jit_solution(17604431810992278392)
XLA Ops:
  12.3 54.2 %shard_map.162 = (bf16[8,176,1536]{2,1,0:T(8,128)(2,1)S(1)}, bf16[8,176,2304]{2,1,0:T(8,128)(2,1)S(1)}, bf16[8,96,1536]{2,1,0:T(8,128)(2,1)S(1)}) custom-call(bf16[48,1536]{1,0:T(8,128)(2,1)S(1)} %pad.28.refs_0_, bf16[48,2304]{1,0:T(8,128)(2,1)S(1)} %copy-done.4, bf16[32,1536]{1,0:T(8,128)(2,1)S(1)} %pad.30.refs_2_), custom_call_target="tpu_custom_call" | custom-call | tf_op jit(solution)/shard_map/pallas_call | solution.py:248
  66.5 2.7 copy-done.2
  71.2 2.6 convolution_convert_fusion.1
  82.3 3.1 collective-permute-start
  87.7 9.6 %copy.231 = bf16[2304,1408]{1,0:T(8,128)(2,1)} copy(bf16[2304,1408]{0,1:T(8,128)(2,1)} %bitcast.299) | data formatting | bytes 12976128 | tf_op jit(solution)/shard_map/dot_general | solution.py:319
  97.3 5.8 %fusion.93 = (bf16[24,96,128]{2,1,0:T(8,128)(2,1)}, f32[24,96,128]{2,1,0:T(8,128)S(1)}) fusion(bf16[24,96,1408]{2,1,0:T(8,128)(2,1)} %bitcast.303, bf16[128,1408]{1,0:T(8,128)(2,1)} %param.20, f32[1408]{0:T(1024)S(1)} %copy-done.38, f32[128]{0:T(128)} %add_rsqrt_fusion.2, f32[128]{0:T(128)} %copy-done.45), kind=kOutput, calls=%fused_computation.173 | convolution fusion | flops 831668224 | bytes 8624640 | tf_op jit(solution)/shard_map/dot_general | solution.py:319
  106.4 10.2 %all-to-all-start = ((bf16[32,88,32]{1,2,0:T(8,128)(2,1)}), bf16[32,88,32]{1,2,0:T(8,128)(2,1)}, u32[]{:S(2)}, u32[]{:S(2)}) async-start(bf16[32,88,32]{1,2,0:T(8,128)(2,1)} %copy.233), calls=%async_computation | async-start | bytes 524288 | tf_op jit(solution)/shard_map/all_to_all | solution.py:326
  125.1 3.8 collective-permute-start.2
  132.8 2.9 collective-permute-done.3
  140.7 4.8 fusion.96
  147.4 10.4 %all-to-all-start.4 = ((bf16[32,88,32]{1,2,0:T(8,128)(2,1)}), bf16[32,88,32]{1,2,0:T(8,128)(2,1)S(1)}, u32[]{:S(2)}, u32[]{:S(2)}) async-start(bf16[32,88,32]{1,2,0:T(8,128)(2,1)} %bitcast.49), calls=%async_computation.4 | async-start | bytes 524288 | tf_op jit(solution)/shard_map/all_to_all | solution.py:422
  157.9 9.1 %all-to-all-done.4 = bf16[32,88,32]{1,2,0:T(8,128)(2,1)S(1)} async-done(((bf16[32,88,32]{1,2,0:T(8,128)(2,1)}), bf16[32,88,32]{1,2,0:T(8,128)(2,1)S(1)}, u32[]{:S(2)}, u32[]{:S(2)}) %all-to-all-start.4) | async-done | bytes 180256 | tf_op jit(solution)/shard_map/all_to_all | solution.py:422
  167.9 4.6 all-to-all-start.1
  174.3 9.1 %all-to-all-done.1 = bf16[32,88,128]{2,1,0:T(8,128)(2,1)} async-done(((bf16[32,88,128]{2,1,0:T(8,128)(2,1)}), bf16[32,88,128]{2,1,0:T(8,128)(2,1)}, u32[]{:S(2)}, u32[]{:S(2)}) %all-to-all-start.1) | async-done | bytes 720928 | tf_op jit(solution)/shard_map/all_to_all | solution.py:330
  184.4 4.8 all-to-all-start.2
  196.3 3.9 all-to-all-done.2
  203.1 23.5 %while.29 = (s32[]{:T(128)}, bf16[2,88,512]{2,1,0:T(8,128)(2,1)S(1)}, bf16[2,512,4096]{2,1,0:T(8,128)(2,1)}, bf16[2,88,512]{2,1,0:T(8,128)(2,1)S(1)}, bf16[88,40...) while((s32[]{:T(128)}, bf16[2,88,512]{2,1,0:T(8,128)(2,1)S(1)}, ...), condition=%wide.region_5.6_spmd, body=%wide.region_2.5_spmd.sunk | while | flops 750824448 | bytes 106489992 | solution.py:351
  210.2 3.3 copy-done.7
  221.9 3.3 copy-done.7
  230.6 3.8 reduce.11
  236.5 5.0 all-to-all-start.3
  241.5 37.6 %while.30 = (s32[]{:T(128)}, f32[88,4096]{1,0:T(8,128)S(1)}, f32[88,4096]{1,0:T(8,128)}, bf16[2,88,512]{2,1,0:T(8,128)(2,1)S(1)}, bf16[2,88,512]{2,1,0:T(8,128)(...) while((s32[]{:T(128)}, f32[88,4096]{1,0:T(8,128)S(1)}, ...), condition=%wide.region_16.17_spmd.clone, body=%wide.region_14.16_spmd.clone.sunk | while | flops 1492606464 | bytes 66295964 | solution.py:450
  241.5 3.6 fusion.157
  245.1 5.9 %fusion.158 = bf16[512,4096]{1,0:T(8,128)(2,1)} fusion(f32[512,4096]{1,0:T(8,128)S(1)} %get-tuple-element.465, f32[512]{0:T(512)S(1)} %get-tuple-element.466, bf16[2,512,4096]{2,1,0:T(8,128)(2,1)} %get-tuple-element.515, s32[]{:T(128)} %get-tuple-element.499), kind=kLoop, calls=%fused_computation.14.clone.1 | loop fusion | flops 8388608 | bytes 16779268 | tf_op jit(solution)/shard_map/while/body/eval_jaxpr/convert_element_type | solution.py:434
  251.0 3.4 convolution_add_fusion.4
  255.9 4.2 convolution_add_fusion.5
  260.1 3.6 fusion.157
  263.6 5.9 %fusion.158 = bf16[512,4096]{1,0:T(8,128)(2,1)} fusion(f32[512,4096]{1,0:T(8,128)S(1)} %get-tuple-element.465, f32[512]{0:T(512)S(1)} %get-tuple-element.466, bf16[2,512,4096]{2,1,0:T(8,128)(2,1)} %get-tuple-element.515, s32[]{:T(128)} %get-tuple-element.499), kind=kLoop, calls=%fused_computation.14.clone.1 | loop fusion | flops 8388608 | bytes 16779268 | tf_op jit(solution)/shard_map/while/body/eval_jaxpr/convert_element_type | solution.py:434
  269.6 3.4 convolution_add_fusion.4
  274.5 4.6 convolution_add_fusion.5
  282.9 8.4 %all-to-all-start.5 = ((bf16[32,2,1408]{2,1,0:T(2,128)(2,1)}), bf16[32,2,1408]{2,1,0:T(2,128)(2,1)S(1)}, u32[]{:S(2)}, u32[]{:S(2)}) async-start(bf16[32,2,1408]{2,1,0:T(2,128)(2,1)} %reshape.375), calls=%async_computation.5 | async-start | bytes 360448 | tf_op jit(solution)/shard_map/all_to_all | solution.py:455
  293.0 7.1 %all-to-all-done.5 = bf16[32,2,1408]{2,1,0:T(2,128)(2,1)S(1)} async-done(((bf16[32,2,1408]{2,1,0:T(2,128)(2,1)}), bf16[32,2,1408]{2,1,0:T(2,128)(2,1)S(1)}, u32[]{:S(2)}, u32[]{:S(2)}) %all-to-all-start.5) | async-done | bytes 180256 | tf_op jit(solution)/shard_map/all_to_all | solution.py:455
  300.1 3.9 all-to-all-start.6
  310.4 3.4 fusion.27
  322.0 8.4 %all-to-all-start.7 = ((bf16[88,32,128]{2,0,1:T(8,128)(2,1)}), bf16[88,32,128]{2,0,1:T(8,128)(2,1)}, u32[]{:S(2)}, u32[]{:S(2)}) async-start(bf16[88,32,128]{2,0,1:T(8,128)(2,1)} %copy_bitcast_fusion.2), calls=%async_computation.7 | async-start | bytes 1441792 | tf_op jit(solution)/shard_map/all_to_all | solution.py:461
  330.4 108.8 %fusion.87 = (bf16[32,1408]{1,0:T(8,128)(2,1)S(1)}, bf16[48,1536]{1,0:T(8,128)(2,1)S(1)}, bf16[16,256]{1,0:T(8,128)(2,1)S(1)}) fusion(bf16[704,1408]{1,0:T(8,128)(2,1)} %multiply_convert_fusion, bf16[1408,1536]{1,0:T(8,128)(2,1)} %fusion.27, bf16[384,256]{1,0:T(8,128)(2,1)} %fusion.30), kind=kCustom, calls=%all-reduce-scatter.3 | all-reduce-scatter fusion | flops 3932163 | bytes 6751232
  443.6 4.0 collective-permute-start.19
  447.6 5.0 collective-permute-start.20
  454.8 6.4 %collective-permute-start.22 = (bf16[16,256]{1,0:T(8,128)(2,1)S(1)}, bf16[16,256]{1,0:T(8,128)(2,1)S(1)}, u32[]{:S(2)}, u32[]{:S(2)}) collective-permute-start(bf16[16,256]{1,0:T(8,128)(2,1)S(1)} %get-tuple-element.325), channel_id=1, source_target_pairs={{0,6},{1,7},{2,8},{3,9},{4,10},{5,11},{6,12},{7,13},{8,14},{9,15},... | collective-permute-start | bytes 24584
  461.3 3.4 collective-permute-start.23
  483.2 3.5 collective-permute-start.5
  486.7 3.2 collective-permute-start.6
  491.9 3.4 collective-permute-start.8
  495.2 5.4 %collective-permute-start.9 = (bf16[32,1408]{1,0:T(8,128)(2,1)S(1)}, bf16[32,1408]{1,0:T(8,128)(2,1)S(1)}, u32[]{:S(2)}, u32[]{:S(2)}) collective-permute-start(bf16[32,1408]{1,0:T(8,128)(2,1)S(1)} %get-tuple-element.323), channel_id=1, source_target_pairs={{0,6},{1,7},{2,8},{3,9},{4,10},{5,11},{6,12},{7,13},{8,14},{9,15},... | collective-permute-start | bytes 270344
  501.3 3.1 collective-permute-start.14
  506.8 4.4 collective-permute-start.16
  511.2 6.4 %concatenate.26 = bf16[342,1408]{1,0:T(8,128)(2,1)S(1)} concatenate(bf16[22,1408]{1,0:T(8,128)(2,1)} %collective-permute-done.13, bf16[32,1408]{1,0:T(8,128)(2,1)} %collective-permute-done.12, bf16[32,1408]{1,0:T(8,128)(2,1)} %collective-permute-done.11, bf16[32,1408]{1,0:T(8,128)(2,1)} %collective-permute-done.10, bf16[32,1408]{1,0:T(8,128)(2,1)S(1)} %collective-permute-done.9, ...), dimensions={0} | concatenate | bytes 1926144
  523.7 5.3 fusion.86
  (305 shorter events, 134.7 us)
Async XLA Ops:
  7.2 112.2 %copy-start = (bf16[3,3,256,256]{3,2,1,0:T(8,128)(2,1)S(1)}, bf16[3,3,256,256]{3,2,1,0:T(8,128)(2,1)}, u32[]{:S(2)}) copy-start(bf16[3,3,256,256]{3,2,1,0:T(8,128)(2,1)} %param.28) | copy-start | bytes 3538948
  82.3 35.8 %collective-permute-start = (bf16[1,128,256]{2,1,0:T(8,128)(2,1)}, bf16[1,128,256]{2,1,0:T(8,128)(2,1)}, u32[]{:S(2)}, u32[]{:S(2)}) collective-permute-start(bf16[1,128,256]{2,1,0:T(8,128)(2,1)} %get-tuple-element.344), channel_id=1, source_target_pairs={{0,1},{1,2},{2,3},{3,4},{4,5},{5,6},{6,7},{7,8},{8,9},{9,10},{10,1... | collective-permute-start | bytes 196616 | tf_op jit(solution)/shard_map/ppermute | solution.py:26
  85.4 32.6 %collective-permute-start.1 = (bf16[1,128,256]{2,1,0:T(8,128)(2,1)}, bf16[1,128,256]{2,1,0:T(8,128)(2,1)}, u32[]{:S(2)}, u32[]{:S(2)}) collective-permute-start(bf16[1,128,256]{2,1,0:T(8,128)(2,1)} %get-tuple-element.345), channel_id=1, source_target_pairs={{1,0},{2,1},{3,2},{4,3},{5,4},{6,5},{7,6},{8,7},{9,8},{10,9},{11,1... | collective-permute-start | bytes 196616 | tf_op jit(solution)/shard_map/ppermute | solution.py:29
  87.7 9.6 %copy-start.38 = (f32[1408]{0:T(1024)S(1)}, f32[1408]{0:T(1024)}, u32[]{:S(2)}) copy-start(f32[1408]{0:T(1024)} %param.22) | copy-start | bytes 16900
  106.4 41.0 %all-to-all-start = ((bf16[32,88,32]{1,2,0:T(8,128)(2,1)}), bf16[32,88,32]{1,2,0:T(8,128)(2,1)}, u32[]{:S(2)}, u32[]{:S(2)}) async-start(bf16[32,88,32]{1,2,0:T(8,128)(2,1)} %copy.233), calls=%async_computation | async-start | bytes 524288 | tf_op jit(solution)/shard_map/all_to_all | solution.py:326
  125.1 5.7 %collective-permute-start.2 = (bf16[128,256]{1,0:T(8,128)(2,1)S(1)}, bf16[128,256]{1,0:T(8,128)(2,1)S(1)}, u32[]{:S(2)}, u32[]{:S(2)}) collective-permute-start(bf16[128,256]{1,0:T(8,128)(2,1)S(1)} %slice_bitcast_fusion.2), channel_id=1, source_target_pairs={{0,1},{1,2},{2,3},{3,4},{4,5},{5,6},{6,7},{7,8},{8,9},{9,10},{10,1... | collective-permute-start | bytes 196616 | tf_op jit(solution)/shard_map/ppermute | solution.py:37
  129.2 8.7 %copy-start.42 = (f32[256]{0:T(256)S(1)}, f32[256]{0:T(256)}, u32[]{:S(2)}) copy-start(f32[256]{0:T(256)} %param.27) | copy-start | bytes 3076
  129.3 8.9 %copy-start.11 = (f32[512,256]{1,0:T(8,128)S(1)}, f32[512,256]{1,0:T(8,128)}, u32[]{:S(2)}) copy-start(f32[512,256]{1,0:T(8,128)} %copy-done.10) | copy-start | bytes 1572868
  129.6 6.2 %collective-permute-start.3 = (bf16[128,256]{1,0:T(8,128)(2,1)S(1)}, bf16[128,256]{1,0:T(8,128)(2,1)S(1)}, u32[]{:S(2)}, u32[]{:S(2)}) collective-permute-start(bf16[128,256]{1,0:T(8,128)(2,1)S(1)} %slice_bitcast_fusion.1), channel_id=1, source_target_pairs={{1,0},{2,1},{3,2},{4,3},{5,4},{6,5},{7,6},{8,7},{9,8},{10,9},{11,1... | collective-permute-start | bytes 196616 | tf_op jit(solution)/shard_map/ppermute | solution.py:37
  145.5 12.3 %copy-start.28 = (bf16[24,96,128]{2,1,0:T(8,128)(2,1)S(1)}, bf16[24,96,128]{2,1,0:T(8,128)(2,1)}, u32[]{:S(2)}) copy-start(bf16[24,96,128]{2,1,0:T(8,128)(2,1)} %get-tuple-element.350) | copy-start | bytes 1769476
  146.4 26.2 %copy-start.26 = (bf16[4,128,256]{2,0,1:T(4,128)(2,1)S(1)}, bf16[4,128,256]{2,0,1:T(4,128)(2,1)}, u32[]{:S(2)}) copy-start(bf16[4,128,256]{2,0,1:T(4,128)(2,1)} %copy-done.25) | copy-start | bytes 786436
  146.7 26.7 %copy-start.16 = (bf16[512,256]{1,0:T(8,128)(2,1)S(1)}, bf16[512,256]{1,0:T(8,128)(2,1)}, u32[]{:S(2)}) copy-start(bf16[512,256]{1,0:T(8,128)(2,1)} %copy-done.14) | copy-start | bytes 786436
  147.4 19.5 %all-to-all-start.4 = ((bf16[32,88,32]{1,2,0:T(8,128)(2,1)}), bf16[32,88,32]{1,2,0:T(8,128)(2,1)S(1)}, u32[]{:S(2)}, u32[]{:S(2)}) async-start(bf16[32,88,32]{1,2,0:T(8,128)(2,1)} %bitcast.49), calls=%async_computation.4 | async-start | bytes 524288 | tf_op jit(solution)/shard_map/all_to_all | solution.py:422
  167.0 17.5 %copy-start.30 = (bf16[32,88,32]{1,2,0:T(8,128)(2,1)}, bf16[32,88,32]{1,2,0:T(8,128)(2,1)S(1)}, u32[]{:S(2)}) copy-start(bf16[32,88,32]{1,2,0:T(8,128)(2,1)S(1)} %all-to-all-done.4) | copy-start | bytes 540676
  167.9 15.5 %all-to-all-start.1 = ((bf16[32,88,128]{2,1,0:T(8,128)(2,1)}), bf16[32,88,128]{2,1,0:T(8,128)(2,1)}, u32[]{:S(2)}, u32[]{:S(2)}) async-start(bf16[32,88,128]{2,1,0:T(8,128)(2,1)} %bitcast.13), calls=%async_computation.1 | async-start | bytes 1441792 | tf_op jit(solution)/shard_map/all_to_all | solution.py:330
  184.4 15.7 %all-to-all-start.2 = ((bf16[32,88,128]{2,1,0:T(8,128)(2,1)}), bf16[32,88,128]{2,1,0:T(8,128)(2,1)}, u32[]{:S(2)}, u32[]{:S(2)}) async-start(bf16[32,88,128]{2,1,0:T(8,128)(2,1)} %bitcast.313), calls=%async_computation.2 | async-start | bytes 1441792 | tf_op jit(solution)/shard_map/all_to_all | solution.py:331
  236.5 46.4 %all-to-all-start.3 = ((bf16[32,2,1408]{2,1,0:T(2,128)(2,1)}), bf16[32,2,1408]{2,1,0:T(2,128)(2,1)}, u32[]{:S(2)}, u32[]{:S(2)}) async-start(bf16[32,2,1408]{2,1,0:T(2,128)(2,1)} %reshape.373), calls=%async_computation.3 | async-start | bytes 360448 | tf_op jit(solution)/shard_map/all_to_all | solution.py:354
  279.1 12.2 %copy-start.29 = (bf16[4,128,256]{2,1,0:T(8,128)(2,1)S(1)}, bf16[4,128,256]{2,1,0:T(8,128)(2,1)}, u32[]{:S(2)}) copy-start(bf16[4,128,256]{2,1,0:T(8,128)(2,1)} %get-tuple-element.334) | copy-start | bytes 786436
  281.7 22.6 %copy-start.37 = (bf16[4,128,256]{2,1,0:T(8,128)(2,1)S(1)}, bf16[4,128,256]{2,1,0:T(8,128)(2,1)}, u32[]{:S(2)}) copy-start(bf16[4,128,256]{2,1,0:T(8,128)(2,1)} %copy.271) | copy-start | bytes 786436
  282.9 17.3 %all-to-all-start.5 = ((bf16[32,2,1408]{2,1,0:T(2,128)(2,1)}), bf16[32,2,1408]{2,1,0:T(2,128)(2,1)S(1)}, u32[]{:S(2)}, u32[]{:S(2)}) async-start(bf16[32,2,1408]{2,1,0:T(2,128)(2,1)} %reshape.375), calls=%async_computation.5 | async-start | bytes 360448 | tf_op jit(solution)/shard_map/all_to_all | solution.py:455
  300.1 20.9 %all-to-all-start.6 = ((bf16[88,32,128]{2,0,1:T(8,128)(2,1)}), bf16[88,32,128]{2,0,1:T(8,128)(2,1)S(1)}, u32[]{:S(2)}, u32[]{:S(2)}) async-start(bf16[88,32,128]{2,0,1:T(8,128)(2,1)} %copy_bitcast_fusion.3), calls=%async_computation.6 | async-start | bytes 1441792 | tf_op jit(solution)/shard_map/all_to_all | solution.py:458
  304.1 215.8 %reduce-scatter.8.cloned.1.call-start = ((), (), s32[]{:S(2)}) async-start(), calls=%async_computation.9 | async-start | bytes 1216512 | tf_op jit(solution)/shard_map/reduce_scatter | solution.py:489
  322.0 199.6 %all-to-all-start.7 = ((bf16[88,32,128]{2,0,1:T(8,128)(2,1)}), bf16[88,32,128]{2,0,1:T(8,128)(2,1)}, u32[]{:S(2)}, u32[]{:S(2)}) async-start(bf16[88,32,128]{2,0,1:T(8,128)(2,1)} %copy_bitcast_fusion.2), calls=%async_computation.7 | async-start | bytes 1441792 | tf_op jit(solution)/shard_map/all_to_all | solution.py:461
  330.4 134.4 %copy-start.49 = (u32[256]{0:T(256)S(1)}, u32[256]{0:T(256)}, u32[]{:S(2)}) copy-start(u32[256]{0:T(256)} %constant.155) | copy-start | bytes 3076
  330.4 147.7 %copy-start.13 = (bf16[8,88,1408]{2,1,0:T(8,128)(2,1)S(1)}, bf16[8,88,1408]{2,1,0:T(8,128)(2,1)}, u32[]{:S(2)}) copy-start(bf16[8,88,1408]{2,1,0:T(8,128)(2,1)} %slice.143) | copy-start | bytes 5947396
  439.2 40.1 %copy-start.36 = (bf16[32,2,1408]{2,1,0:T(2,128)(2,1)S(1)}, bf16[32,2,1408]{2,1,0:T(2,128)(2,1)}, u32[]{:S(2)}) copy-start(bf16[32,2,1408]{2,1,0:T(2,128)(2,1)} %copy-done.35) | copy-start | bytes 540676
  439.2 15.6 %collective-permute-start.17 = (bf16[16,256]{1,0:T(8,128)(2,1)S(1)}, bf16[16,256]{1,0:T(8,128)(2,1)S(1)}, u32[]{:S(2)}, u32[]{:S(2)}) collective-permute-start(bf16[16,256]{1,0:T(8,128)(2,1)S(1)} %get-tuple-element.325), channel_id=1, source_target_pairs={{0,1},{1,2},{2,3},{3,4},{4,5},{5,6},{6,7},{7,8},{8,9},{9,10},{10,1... | collective-permute-start | bytes 24584
  440.6 20.7 %collective-permute-start.18 = (bf16[16,256]{1,0:T(8,128)(2,1)S(1)}, bf16[16,256]{1,0:T(8,128)(2,1)S(1)}, u32[]{:S(2)}, u32[]{:S(2)}) collective-permute-start(bf16[16,256]{1,0:T(8,128)(2,1)S(1)} %get-tuple-element.325), channel_id=1, source_target_pairs={{0,2},{1,3},{2,4},{3,5},{4,6},{5,7},{6,8},{7,9},{8,10},{9,11},{10,... | collective-permute-start | bytes 24584
  442.0 10.6 %collective-permute-start.24 = (bf16[12,256]{1,0:T(8,128)(2,1)S(1)}, bf16[12,256]{1,0:T(8,128)(2,1)S(1)}, u32[]{:S(2)}, u32[]{:S(2)}) collective-permute-start(bf16[12,256]{1,0:T(8,128)(2,1)S(1)} %slice.202), channel_id=1, source_target_pairs={{0,8},{1,9},{2,10},{3,11},{4,12},{5,13},{6,14},{7,15},{8,16},{9,17... | collective-permute-start | bytes 18440
  443.6 23.7 %collective-permute-start.19 = (bf16[16,256]{1,0:T(8,128)(2,1)S(1)}, bf16[16,256]{1,0:T(8,128)(2,1)S(1)}, u32[]{:S(2)}, u32[]{:S(2)}) collective-permute-start(bf16[16,256]{1,0:T(8,128)(2,1)S(1)} %get-tuple-element.325), channel_id=1, source_target_pairs={{0,3},{1,4},{2,5},{3,6},{4,7},{5,8},{6,9},{7,10},{8,11},{9,12},{10... | collective-permute-start | bytes 24584
  447.6 22.3 %collective-permute-start.20 = (bf16[16,256]{1,0:T(8,128)(2,1)S(1)}, bf16[16,256]{1,0:T(8,128)(2,1)S(1)}, u32[]{:S(2)}, u32[]{:S(2)}) collective-permute-start(bf16[16,256]{1,0:T(8,128)(2,1)S(1)} %get-tuple-element.325), channel_id=1, source_target_pairs={{0,4},{1,5},{2,6},{3,7},{4,8},{5,9},{6,10},{7,11},{8,12},{9,13},{1... | collective-permute-start | bytes 24584
  452.6 19.1 %collective-permute-start.21 = (bf16[16,256]{1,0:T(8,128)(2,1)S(1)}, bf16[16,256]{1,0:T(8,128)(2,1)S(1)}, u32[]{:S(2)}, u32[]{:S(2)}) collective-permute-start(bf16[16,256]{1,0:T(8,128)(2,1)S(1)} %get-tuple-element.325), channel_id=1, source_target_pairs={{0,5},{1,6},{2,7},{3,8},{4,9},{5,10},{6,11},{7,12},{8,13},{9,14},{... | collective-permute-start | bytes 24584
  454.8 18.8 %collective-permute-start.22 = (bf16[16,256]{1,0:T(8,128)(2,1)S(1)}, bf16[16,256]{1,0:T(8,128)(2,1)S(1)}, u32[]{:S(2)}, u32[]{:S(2)}) collective-permute-start(bf16[16,256]{1,0:T(8,128)(2,1)S(1)} %get-tuple-element.325), channel_id=1, source_target_pairs={{0,6},{1,7},{2,8},{3,9},{4,10},{5,11},{6,12},{7,13},{8,14},{9,15},... | collective-permute-start | bytes 24584
  461.3 14.9 %collective-permute-start.23 = (bf16[16,256]{1,0:T(8,128)(2,1)S(1)}, bf16[16,256]{1,0:T(8,128)(2,1)S(1)}, u32[]{:S(2)}, u32[]{:S(2)}) collective-permute-start(bf16[16,256]{1,0:T(8,128)(2,1)S(1)} %get-tuple-element.325), channel_id=1, source_target_pairs={{0,7},{1,8},{2,9},{3,10},{4,11},{5,12},{6,13},{7,14},{8,15},{9,16}... | collective-permute-start | bytes 24584
  467.3 19.4 %collective-permute-start.10 = (bf16[32,1408]{1,0:T(8,128)(2,1)S(1)}, bf16[32,1408]{1,0:T(8,128)(2,1)}, u32[]{:S(2)}, u32[]{:S(2)}) collective-permute-start(bf16[32,1408]{1,0:T(8,128)(2,1)S(1)} %get-tuple-element.323), channel_id=1, source_target_pairs={{0,7},{1,8},{2,9},{3,10},{4,11},{5,12},{6,13},{7,14},{8,15},{9,16}... | collective-permute-start | bytes 270344
  469.8 20.0 %collective-permute-start.11 = (bf16[32,1408]{1,0:T(8,128)(2,1)S(1)}, bf16[32,1408]{1,0:T(8,128)(2,1)}, u32[]{:S(2)}, u32[]{:S(2)}) collective-permute-start(bf16[32,1408]{1,0:T(8,128)(2,1)S(1)} %get-tuple-element.323), channel_id=1, source_target_pairs={{0,8},{1,9},{2,10},{3,11},{4,12},{5,13},{6,14},{7,15},{8,16},{9,17... | collective-permute-start | bytes 270344
  471.8 20.1 %collective-permute-start.12 = (bf16[32,1408]{1,0:T(8,128)(2,1)S(1)}, bf16[32,1408]{1,0:T(8,128)(2,1)}, u32[]{:S(2)}, u32[]{:S(2)}) collective-permute-start(bf16[32,1408]{1,0:T(8,128)(2,1)S(1)} %get-tuple-element.323), channel_id=1, source_target_pairs={{0,9},{1,10},{2,11},{3,12},{4,13},{5,14},{6,15},{7,16},{8,17},{9,1... | collective-permute-start | bytes 270344
  473.7 21.6 %collective-permute-start.4 = (bf16[32,1408]{1,0:T(8,128)(2,1)S(1)}, bf16[32,1408]{1,0:T(8,128)(2,1)}, u32[]{:S(2)}, u32[]{:S(2)}) collective-permute-start(bf16[32,1408]{1,0:T(8,128)(2,1)S(1)} %get-tuple-element.323), channel_id=1, source_target_pairs={{0,1},{1,2},{2,3},{3,4},{4,5},{5,6},{6,7},{7,8},{8,9},{9,10},{10,1... | collective-permute-start | bytes 270344
  476.2 7.0 %collective-permute-start.13 = (bf16[22,1408]{1,0:T(8,128)(2,1)}, bf16[22,1408]{1,0:T(8,128)(2,1)}, u32[]{:S(2)}, u32[]{:S(2)}) collective-permute-start(bf16[22,1408]{1,0:T(8,128)(2,1)} %slice.200), channel_id=1, source_target_pairs={{0,10},{1,11},{2,12},{3,13},{4,14},{5,15},{6,16},{7,17},{8,18},{9,... | collective-permute-start | bytes 185864
  480.6 40.7 %copy-start.24 = (bf16[88,32,128]{2,0,1:T(8,128)(2,1)S(1)}, bf16[88,32,128]{2,0,1:T(8,128)(2,1)}, u32[]{:S(2)}) copy-start(bf16[88,32,128]{2,0,1:T(8,128)(2,1)} %copy-done.23) | copy-start | bytes 2162692
  483.2 18.1 %collective-permute-start.5 = (bf16[32,1408]{1,0:T(8,128)(2,1)S(1)}, bf16[32,1408]{1,0:T(8,128)(2,1)S(1)}, u32[]{:S(2)}, u32[]{:S(2)}) collective-permute-start(bf16[32,1408]{1,0:T(8,128)(2,1)S(1)} %get-tuple-element.323), channel_id=1, source_target_pairs={{0,2},{1,3},{2,4},{3,5},{4,6},{5,7},{6,8},{7,9},{8,10},{9,11},{10,... | collective-permute-start | bytes 270344
  486.7 17.6 %collective-permute-start.6 = (bf16[32,1408]{1,0:T(8,128)(2,1)S(1)}, bf16[32,1408]{1,0:T(8,128)(2,1)S(1)}, u32[]{:S(2)}, u32[]{:S(2)}) collective-permute-start(bf16[32,1408]{1,0:T(8,128)(2,1)S(1)} %get-tuple-element.323), channel_id=1, source_target_pairs={{0,3},{1,4},{2,5},{3,6},{4,7},{5,8},{6,9},{7,10},{8,11},{9,12},{10... | collective-permute-start | bytes 270344
  489.9 16.9 %collective-permute-start.7 = (bf16[32,1408]{1,0:T(8,128)(2,1)S(1)}, bf16[32,1408]{1,0:T(8,128)(2,1)S(1)}, u32[]{:S(2)}, u32[]{:S(2)}) collective-permute-start(bf16[32,1408]{1,0:T(8,128)(2,1)S(1)} %get-tuple-element.323), channel_id=1, source_target_pairs={{0,4},{1,5},{2,6},{3,7},{4,8},{5,9},{6,10},{7,11},{8,12},{9,13},{1... | collective-permute-start | bytes 270344
  491.9 19.3 %collective-permute-start.8 = (bf16[32,1408]{1,0:T(8,128)(2,1)S(1)}, bf16[32,1408]{1,0:T(8,128)(2,1)S(1)}, u32[]{:S(2)}, u32[]{:S(2)}) collective-permute-start(bf16[32,1408]{1,0:T(8,128)(2,1)S(1)} %get-tuple-element.323), channel_id=1, source_target_pairs={{0,5},{1,6},{2,7},{3,8},{4,9},{5,10},{6,11},{7,12},{8,13},{9,14},{... | collective-permute-start | bytes 270344
  495.2 16.0 %collective-permute-start.9 = (bf16[32,1408]{1,0:T(8,128)(2,1)S(1)}, bf16[32,1408]{1,0:T(8,128)(2,1)S(1)}, u32[]{:S(2)}, u32[]{:S(2)}) collective-permute-start(bf16[32,1408]{1,0:T(8,128)(2,1)S(1)} %get-tuple-element.323), channel_id=1, source_target_pairs={{0,6},{1,7},{2,8},{3,9},{4,10},{5,11},{6,12},{7,13},{8,14},{9,15},... | collective-permute-start | bytes 270344
  501.3 17.1 %collective-permute-start.14 = (bf16[48,1536]{1,0:T(8,128)(2,1)S(1)}, bf16[48,1536]{1,0:T(8,128)(2,1)S(1)}, u32[]{:S(2)}, u32[]{:S(2)}) collective-permute-start(bf16[48,1536]{1,0:T(8,128)(2,1)S(1)} %get-tuple-element.324), channel_id=1, source_target_pairs={{0,1},{1,2},{2,3},{3,4},{4,5},{5,6},{6,7},{7,8},{8,9},{9,10},{10,1... | collective-permute-start | bytes 442376
  504.4 14.0 %collective-permute-start.15 = (bf16[48,1536]{1,0:T(8,128)(2,1)S(1)}, bf16[48,1536]{1,0:T(8,128)(2,1)S(1)}, u32[]{:S(2)}, u32[]{:S(2)}) collective-permute-start(bf16[48,1536]{1,0:T(8,128)(2,1)S(1)} %get-tuple-element.324), channel_id=1, source_target_pairs={{0,2},{1,3},{2,4},{3,5},{4,6},{5,7},{6,8},{7,9},{8,10},{9,11},{10,... | collective-permute-start | bytes 442376
  506.8 11.5 %collective-permute-start.16 = (bf16[28,1536]{1,0:T(8,128)(2,1)S(1)}, bf16[28,1536]{1,0:T(8,128)(2,1)S(1)}, u32[]{:S(2)}, u32[]{:S(2)}) collective-permute-start(bf16[28,1536]{1,0:T(8,128)(2,1)S(1)} %slice.201), channel_id=1, source_target_pairs={{0,3},{1,4},{2,5},{3,6},{4,7},{5,8},{6,9},{7,10},{8,11},{9,12},{10... | collective-permute-start | bytes 258056
  (40 other events, 130.2 us)
Sparse Core Ops, SparseCore 0:
  308.5 167.9 reduce-scatter.7

commit v2 on v1

--- a/solution.py
+++ b/solution.py
@@ -277,6 +277,116 @@
     return groups[:, :HEAD].reshape(-1, features.shape[-1])
 
 
+def scatter_kernel(plan, *refs):
+    count = len(plan)
+    arrays = 1 + max(source for source, _, _, _ in plan)
+    ins, outs = refs[:arrays], refs[arrays : arrays + count]
+    rest = refs[arrays + count :]
+    land1, sum1, land2, sum2, land3 = (rest[k * count : (k + 1) * count] for k in range(5))
+    send, recv = rest[5 * count :]
+    x, zl, y, zh, core = place()
+    across = at_sp(x, 1 - zl, y)
+    row = [(x + k) % 4 for k in (1, 2, 3)]
+    column = [(y + k) % 4 for k in (1, 2, 3)]
+    greet([at_sp(k, zl, y) for k in row] + [at_sp(x, zl, k) for k in column] + [across])
+    copies = {}
+
+    def push(n, slot, src, dst, target):
+        copy = pltpu.make_async_remote_copy(
+            src_ref=src,
+            dst_ref=dst,
+            send_sem=send.at[n, slot],
+            recv_sem=recv.at[n, slot],
+            device_id=target,
+            device_id_type=MESH,
+        )
+        copy.start()
+        copies[n, slot] = copy
+
+    def to_row(k):
+        return at_sp(row[k], zl, y)
+
+    def to_column(k):
+        return at_sp(x, zl, column[k])
+
+    for n, (source, first, width, x_first) in enumerate(plan):
+        view = ins[source].at[:, :, :, :, pl.ds(first, width)]
+        for k in range(3):
+            if x_first:
+                push(n, k, view.at[row[k]], land1[n].at[k], to_row(k))
+            else:
+                push(n, k, view.at[:, :, column[k]], land1[n].at[k], to_column(k))
+    for n, (source, first, width, x_first) in enumerate(plan):
+        for k in range(3):
+            copies[n, k].wait_recv()
+        outer, inner = sum1[n].shape[0], sum1[n].shape[1]
+
+        def add(t, carry):
+            p, q = t // inner, t % inner
+            if x_first:
+                own = ins[source][x, p, q, :, pl.ds(first, width)]
+            else:
+                own = ins[source][p, q, y, :, pl.ds(first, width)]
+            total = own.astype(jnp.float32)
+            for k in range(3):
+                total += land1[n][k, p, q].astype(jnp.float32)
+            sum1[n][p, q] = total.astype(jnp.bfloat16)
+            return carry
+
+        lax.fori_loop(0, outer * inner, add, 0)
+        for k in range(3):
+            if x_first:
+                push(n, 3 + k, sum1[n].at[:, column[k]], land2[n].at[k], to_column(k))
+            else:
+                push(n, 3 + k, sum1[n].at[row[k]], land2[n].at[k], to_row(k))
+    for n, (source, first, width, x_first) in enumerate(plan):
+        for k in range(3):
+            copies[n, 3 + k].wait_recv()
+        for p in range(2):
+            own = sum1[n][p, y] if x_first else sum1[n][x, p]
+            total = own.astype(jnp.float32)
+            for k in range(3):
+                total += land2[n][k, p].astype(jnp.float32)
+            sum2[n][p] = total.astype(jnp.bfloat16)
+        push(n, 6, sum2[n].at[1 - zl], land3[n], across)
+    for n in range(count):
+        copies[n, 6].wait_recv()
+        outs[n][...] = sum2[n][zl].astype(jnp.float32) + land3[n][...].astype(jnp.float32)
+    for copy in copies.values():
+        copy.wait_send()
+
+
+def scatter_sums(parts, plan):
+    count = len(plan)
+    rows = [parts[source].shape[3] for source, _, _, _ in plan]
+    widths = [width for _, _, width, _ in plan]
+
+    def buffers(*lead):
+        return [pltpu.VMEM((*lead, r, w), jnp.bfloat16) for r, w in zip(rows, widths)]
+
+    def by_order(first, second, lead=()):
+        return [
+            pltpu.VMEM((*lead, *(first if order else second), r, w), jnp.bfloat16)
+            for r, w, (_, _, _, order) in zip(rows, widths, plan)
+        ]
+
+    return pl.pallas_call(
+        functools.partial(scatter_kernel, plan),
+        out_shape=[jax.ShapeDtypeStruct((r, w), jnp.float32) for r, w in zip(rows, widths)],
+        in_specs=[pl.BlockSpec(memory_space=pltpu.VMEM)] * len(parts),
+        out_specs=[pl.BlockSpec(memory_space=pltpu.VMEM)] * count,
+        scratch_shapes=by_order((2, 4), (4, 2), (3,))
+        + by_order((2, 4), (4, 2))
+        + buffers(3, 2)
+        + buffers(2)
+        + buffers()
+        + [pltpu.SemaphoreType.DMA((count, 7)), pltpu.SemaphoreType.DMA((count, 7))],
+        compiler_params=pltpu.CompilerParams(
+            collective_id=1, has_side_effects=True, vmem_limit_bytes=48 * 2**20
+        ),
+    )(*parts)
+
+
 def per_device(
     y_one,
     second_stream_state,
@@ -394,9 +504,13 @@
     conv_product = jnp.einsum(
         "kpc,pd->ckd", patches, dconv.reshape(-1, LAT), preferred_element_type=jnp.float32
     )
-    conv_part = (conv_product.reshape(LAT, 9 * LAT) * grad_scale).astype(jnp.bfloat16)
+    conv_part = (conv_product.reshape(4, 2, 4, LAT // devices, 9 * LAT) * grad_scale).astype(
+        jnp.bfloat16
+    )
     dlat = layer_norm_reverse(dact.reshape(-1, LAT) * lat_gain, lhat, linv).astype(jnp.bfloat16)
-    lat_part = rounded_part(pixels, dlat)
+    lat_rows = DEC // devices
+    lat_part = rounded_part(pixels, dlat).reshape(devices, lat_rows, LAT)
+    lat_part = jnp.pad(lat_part, ((0, 0), (0, 16 - lat_rows), (0, 0))).reshape(4, 2, 4, 16, LAT)
     dpixels = lax.dot_general(
         dlat, w_lateral, (((1,), (1,)), ((), ())), preferred_element_type=jnp.float32
     ).astype(jnp.bfloat16)
@@ -405,8 +519,10 @@
         .transpose(0, 2, 1, 3, 4)
         .reshape(tokens_here, 4 * DEC)
     )
-    dec_part = rounded_part(feature, dup)
-    g_deconv = lax.psum_scatter(dec_part, "sp", scatter_dimension=0, tiled=True).astype(jnp.float32)
+    spread_feature = jnp.pad(
+        feature.reshape(tokens_here, devices, depth), ((0, 0), (0, 0), (0, ROWS_PAD - depth))
+    ).reshape(tokens_here, devices * ROWS_PAD)
+    dec_part = rounded_part(spread_feature, dup).reshape(4, 2, 4, ROWS_PAD, 4 * DEC)
     halfway_split = 0.5 * lax.dot_general(
         dup, deconv_full, (((1,), (1,)), ((), ())), preferred_element_type=jnp.float32
     )
@@ -414,11 +530,13 @@
     dattn = lax.dot_general(
         out_full, d_x1, (((1,), (1,)), ((), ())), preferred_element_type=jnp.float32
     ).astype(jnp.bfloat16)
+    spread_attn = jnp.pad(
+        attn_band.reshape(devices, out_depth, tokens_here), ((0, 0), (0, 24 - out_depth), (0, 0))
+    ).reshape(devices * 24, tokens_here)
     out_product = lax.dot_general(
-        attn_band, d_x1, (((1,), (0,)), ((), ())), preferred_element_type=jnp.float32
-    )
-    out_part = (out_product * grad_scale).astype(jnp.bfloat16)
-    g_out = lax.psum_scatter(out_part, "sp", scatter_dimension=0, tiled=True).astype(jnp.float32)
+        spread_attn, d_x1, (((1,), (0,)), ((), ())), preferred_element_type=jnp.float32
+    )
+    out_part = (out_product * grad_scale).astype(jnp.bfloat16).reshape(4, 2, 4, 24, -1)
     grad_head = lax.all_to_all(
         to_heads(dattn, pieces), "sp", split_axis=0, concat_axis=2, tiled=True
     )[0]
@@ -484,10 +602,20 @@
             normalized_gradient * layer_norm_gain, standardized_input, inverse_deviation
         )
     ).astype(jnp.bfloat16)
-    g_lateral, conv_rows = (
-        lax.psum_scatter(lat_part, "sp", scatter_dimension=0, tiled=True).astype(jnp.float32),
-        lax.psum_scatter(conv_part, "sp", scatter_dimension=0, tiled=True).astype(jnp.float32),
-    )
+    half = 2 * DEC
+    dec_low, out_rows, dec_high, conv_rows, lat_sums = scatter_sums(
+        [dec_part, out_part, conv_part, lat_part],
+        [
+            (0, 0, half, True),
+            (1, 0, out_part.shape[4], False),
+            (0, half, half, True),
+            (2, 0, 9 * LAT, False),
+            (3, 0, LAT, False),
+        ],
+    )
+    g_deconv = jnp.concatenate([dec_low[:depth], dec_high[:depth]], axis=1)
+    g_out = out_rows[:out_depth]
+    g_lateral = lat_sums[:lat_rows]
     g_conv = conv_rows.reshape(conv_rows.shape[0], 3, 3, LAT).transpose(1, 2, 0, 3)
     return (x_one, d_x1, second_input_gradient, g_out, g_deconv, g_lateral, g_conv)
 

time: 547 us -> 428 us (0.78)
  blocking collectives: 109 us -> 14.6 us
  Pallas kernels: 54.2 us -> 123 us
  starting transfers between devices: 129 us -> 64.9 us
  between operations: 17.1 us -> 1.98 us
  local copies, waits for them, and re-layouts: 89 us -> 78.9 us
  waiting for transfers between devices: 32.3 us -> 22.7 us
  matrix products: 65.2 us -> 71.8 us
    unnamed x1 -> x0, blocking collectives: 109 us -> none
    pallas_call x0 -> x1, Pallas kernels: none -> 68.8 us  [scatter_sums(): pl.pallas_call(functools.partial(scatter_kernel, plan), out_shape=[jax.Sh...]
    unnamed x21 -> x0, starting transfers between devices: 63.4 us -> none
    all_to_all x0 -> x1, blocking collectives: none -> 14.6 us  [per_device(): lax.all_to_all(copies(keys, pieces), 'sp', split_axis=0, concat_axis=2, t...]
    all_to_all x1 -> x0, waiting for transfers between devices: 9.15 us -> none  [per_device(): lax.all_to_all(copies(keys, pieces), 'sp', split_axis=0, concat_axis=2, t...]
    conv_general_dilated x2, matrix products: 2 us -> 10.9 us  [conv_valid(): lax.conv_general_dilated(padded[None], kernel, (1, 1), 'VALID', dimension...]
    unnamed x119 -> x121, local copies, waits for them, and re-layouts: 28.7 us -> 25.4 us
  transfers between devices with their start and end apart: 34 -> 11, of which waited for: 5 -> 4; matrix products, arithmetic and copies ran while one was open for 43% -> 26% of each run, Pallas kernels for 0% -> 16%
where the time goes in v2:
time: 428 us; the launch traced here: 422 us
  Pallas kernels  123 us (29%)
  local copies, waits for them, and re-layouts  78.9 us (18%)
  matrix products  71.8 us (17%)
  starting transfers between devices  64.9 us (15%)
  other arithmetic  43.6 us (10%)
  waiting for transfers between devices  22.7 us (5%)
  blocking collectives  14.6 us (3%)
    pallas_call x1, Pallas kernels, scatter_sums(): pl.pallas_call(functools.partial(scatter_kernel, plan), out_shape=[jax.Sh...  68.8 us
    pallas_call x1, Pallas kernels, gather_weights(): pl.pallas_call(functools.partial(gather_kernel, shapes), out_shape=[jax.S...  54.2 us
    unnamed x121, local copies, waits for them, and re-layouts  25.4 us
    all_to_all x1, blocking collectives, per_device(): lax.all_to_all(copies(keys, pieces), 'sp', split_axis=0, concat_axis=2, t...  14.6 us
    convert_element_type x2, other arithmetic, backward_block(): (wide * (dprob - jnp.sum(wide * dprob, axis=1, keepdims=True))).astype(jn...  12 us
    conv_general_dilated x2, matrix products, conv_valid(): lax.conv_general_dilated(padded[None], kernel, (1, 1), 'VALID', dimension...  10.9 us
    all_to_all x1, starting transfers between devices, per_device(): lax.all_to_all(to_heads(dattn, pieces), 'sp', split_axis=0, concat_axis=2...  10.9 us
    while x12, local copies, waits for them, and re-layouts  10.7 us
  transfers between devices with their start and end apart: 11, of which 4 were waited for; matrix products, arithmetic and copies ran while one was open for 26% of the time, Pallas kernels for 16%

profile of v2, /device:TPU:64, one launch (start us, length us, event | category | flops | bytes accessed | tf_op | source)
XLA Modules:
  0.0 421.5 jit_solution(9961823717701826645)
XLA Ops:
  6.6 54.2 %shard_map.162 = (bf16[8,176,1536]{2,1,0:T(8,128)(2,1)S(1)}, bf16[8,176,2304]{2,1,0:T(8,128)(2,1)S(1)}, bf16[8,96,1536]{2,1,0:T(8,128)(2,1)S(1)}) custom-call(bf16[48,1536]{1,0:T(8,128)(2,1)S(1)} %pad.40.refs_0_, bf16[48,2304]{1,0:T(8,128)(2,1)S(1)} %copy-done.4, bf16[32,1536]{1,0:T(8,128)(2,1)S(1)} %pad.42.refs_2_), custom_call_target="tpu_custom_call" | custom-call | tf_op jit(solution)/shard_map/pallas_call | solution.py:248
  60.8 2.7 copy-done.2
  76.7 3.1 collective-permute-start
  81.7 9.7 %copy.182 = bf16[2304,1408]{1,0:T(8,128)(2,1)} copy(bf16[2304,1408]{0,1:T(8,128)(2,1)} %bitcast.294) | data formatting | bytes 12976128 | tf_op jit(solution)/shard_map/dot_general | solution.py:429
  91.4 5.9 %fusion.69 = (bf16[24,96,128]{2,1,0:T(8,128)(2,1)}, f32[24,96,128]{2,1,0:T(8,128)S(1)}) fusion(bf16[24,96,1408]{2,1,0:T(8,128)(2,1)} %bitcast.306, bf16[128,1408]{1,0:T(8,128)(2,1)} %param.20, f32[1408]{0:T(1024)S(1)} %copy-done.45, f32[128]{0:T(128)} %add_rsqrt_fusion.2, f32[128]{0:T(128)} %copy-done.49), kind=kOutput, calls=%fused_computation.149 | convolution fusion | flops 831668224 | bytes 8624640 | tf_op jit(solution)/shard_map/dot_general | solution.py:429
  98.6 4.5 %fusion.71 = (f32[4,128]{1,0:T(4,128)S(1)}, f32[1,4,128,256]{3,0,2,1:T(1,128)S(1)}) fusion(bf16[3,3,256,256]{3,2,1,0:T(8,128)(2,1)S(1)} %copy-done, bf16[1,6,130,256]{3,2,1,0:T(8,128)(2,1)S(1)} %fusion.106), kind=kOutput, calls=%fused_computation.151 | convolution fusion | flops 604110336 | bytes 2105344 | tf_op jit(solution)/shard_map/conv_general_dilated | solution.py:53
  104.9 6.4 %fusion.72 = (bf16[1,6,128,256]{3,0,2,1:T(2,128)(2,1)S(1)}, f32[1,6,128,256]{3,0,2,1:T(1,128)}) fusion(bf16[3,3,256,256]{3,2,1,0:T(8,128)(2,1)S(1)} %copy-done, bf16[1,8,130,256]{3,2,1,0:T(8,128)(2,1)S(1)} %pad_bitcast_fusion), kind=kOutput, calls=%fused_computation.152 | convolution fusion | flops 906166272 | bytes 2891776 | tf_op jit(solution)/shard_map/conv_general_dilated | solution.py:53
  112.9 5.2 %collective-permute-start.2 = (bf16[128,256]{1,0:T(8,128)(2,1)}, bf16[128,256]{1,0:T(8,128)(2,1)}, u32[]{:S(2)}, u32[]{:S(2)}) collective-permute-start(bf16[128,256]{1,0:T(8,128)(2,1)} %bitcast.247), channel_id=1, source_target_pairs={{0,1},{1,2},{2,3},{3,4},{4,5},{5,6},{6,7},{7,8},{8,9},{9,10},{10,1... | collective-permute-start | bytes 196616 | tf_op jit(solution)/shard_map/ppermute | solution.py:37
  119.1 10.2 %all-to-all-start = ((bf16[32,88,32]{1,2,0:T(8,128)(2,1)}), bf16[32,88,32]{1,2,0:T(8,128)(2,1)}, u32[]{:S(2)}, u32[]{:S(2)}) async-start(bf16[32,88,32]{1,2,0:T(8,128)(2,1)} %copy.184), calls=%async_computation | async-start | bytes 524288 | tf_op jit(solution)/shard_map/all_to_all | solution.py:436
  133.5 4.1 collective-permute-done.3
  140.2 4.8 %fusion.73 = (bf16[128,1408]{1,0:T(8,128)(2,1)S(1)}, f32[128,1408]{1,0:T(8,128)}) fusion(bf16[128,1536]{1,0:T(8,128)(2,1)S(1)} %reshape.330, bf16[1408,1536]{1,0:T(8,128)(2,1)} %bitcast.297), kind=kOutput, calls=%fused_computation.153 | convolution fusion | flops 554008576 | bytes 5799936 | tf_op jit(solution)/shard_map/dot_general | solution.py:526
  146.9 10.9 %all-to-all-start.4 = ((bf16[32,88,32]{1,2,0:T(8,128)(2,1)}), bf16[32,88,32]{1,2,0:T(8,128)(2,1)S(1)}, u32[]{:S(2)}, u32[]{:S(2)}) async-start(bf16[32,88,32]{1,2,0:T(8,128)(2,1)} %bitcast.40), calls=%async_computation.4 | async-start | bytes 524288 | tf_op jit(solution)/shard_map/all_to_all | solution.py:540
  157.8 9.1 %all-to-all-done.4 = bf16[32,88,32]{1,2,0:T(8,128)(2,1)S(1)} async-done(((bf16[32,88,32]{1,2,0:T(8,128)(2,1)}), bf16[32,88,32]{1,2,0:T(8,128)(2,1)S(1)}, u32[]{:S(2)}, u32[]{:S(2)}) %all-to-all-start.4) | async-done | bytes 180256 | tf_op jit(solution)/shard_map/all_to_all | solution.py:540
  167.7 14.6 %all_to_all.116 = bf16[32,88,128]{2,1,0:T(8,128)(2,1)} all-to-all(bf16[32,88,128]{2,1,0:T(8,128)(2,1)S(1)} %bitcast.317), channel_id=1, replica_groups=mesh['img'=8,'sp'=32] {'sp'}, dimensions={0} | all-to-all | bytes 1441792 | tf_op jit(solution)/shard_map/all_to_all | solution.py:440
  183.3 5.0 %all-to-all-start.2 = ((bf16[32,88,128]{2,1,0:T(8,128)(2,1)}), bf16[32,88,128]{2,1,0:T(8,128)(2,1)}, u32[]{:S(2)}, u32[]{:S(2)}) async-start(bf16[32,88,128]{2,1,0:T(8,128)(2,1)} %bitcast.16), calls=%async_computation.2 | async-start | bytes 1441792 | tf_op jit(solution)/shard_map/all_to_all | solution.py:441
  196.8 2.4 all-to-all-done.2
  202.2 23.3 %while.29 = (s32[]{:T(128)}, bf16[2,88,512]{2,1,0:T(8,128)(2,1)S(1)}, bf16[2,512,4096]{2,1,0:T(8,128)(2,1)}, bf16[2,88,512]{2,1,0:T(8,128)(2,1)S(1)}, bf16[88,40...) while((s32[]{:T(128)}, bf16[2,88,512]{2,1,0:T(8,128)(2,1)S(1)}, ...), condition=%wide.region_5.6_spmd, body=%wide.region_2.5_spmd.sunk | while | flops 750824448 | bytes 106489992 | solution.py:461
  204.8 2.1 copy-done.6
  206.9 2.2 bitcast_dynamic-update-slice_fusion.11
  209.2 3.2 copy-done.7
  216.5 2.1 copy-done.6
  218.6 2.2 bitcast_dynamic-update-slice_fusion.11
  220.8 3.2 copy-done.7
  226.3 2.6 reshape.350
  229.4 3.8 reduce.10
  235.3 6.3 %all-to-all-start.3 = ((bf16[32,2,1408]{2,1,0:T(2,128)(2,1)}), bf16[32,2,1408]{2,1,0:T(2,128)(2,1)}, u32[]{:S(2)}, u32[]{:S(2)}) async-start(bf16[32,2,1408]{2,1,0:T(2,128)(2,1)} %reshape.353), calls=%async_computation.3 | async-start | bytes 360448 | tf_op jit(solution)/shard_map/all_to_all | solution.py:464
  241.7 37.7 %while.30 = (s32[]{:T(128)}, f32[88,4096]{1,0:T(8,128)S(1)}, f32[88,4096]{1,0:T(8,128)}, bf16[2,88,512]{2,1,0:T(8,128)(2,1)S(1)}, bf16[2,88,512]{2,1,0:T(8,128)(...) while((s32[]{:T(128)}, f32[88,4096]{1,0:T(8,128)S(1)}, ...), condition=%wide.region_16.17_spmd.clone, body=%wide.region_14.16_spmd.clone.sunk | while | flops 1492606464 | bytes 66295964 | solution.py:568
  241.7 3.6 fusion.136
  245.3 6.0 %fusion.137 = bf16[512,4096]{1,0:T(8,128)(2,1)} fusion(f32[512,4096]{1,0:T(8,128)S(1)} %get-tuple-element.431, f32[512]{0:T(512)S(1)} %get-tuple-element.432, bf16[2,512,4096]{2,1,0:T(8,128)(2,1)} %get-tuple-element.481, s32[]{:T(128)} %get-tuple-element.465), kind=kLoop, calls=%fused_computation.14.clone.1 | loop fusion | flops 8388608 | bytes 16779268 | tf_op jit(solution)/shard_map/while/body/eval_jaxpr/convert_element_type | solution.py:552
  251.3 3.4 convolution_add_fusion.4
  256.1 4.2 convolution_add_fusion.5
  260.3 3.6 fusion.136
  263.9 6.0 %fusion.137 = bf16[512,4096]{1,0:T(8,128)(2,1)} fusion(f32[512,4096]{1,0:T(8,128)S(1)} %get-tuple-element.431, f32[512]{0:T(512)S(1)} %get-tuple-element.432, bf16[2,512,4096]{2,1,0:T(8,128)(2,1)} %get-tuple-element.481, s32[]{:T(128)} %get-tuple-element.465), kind=kLoop, calls=%fused_computation.14.clone.1 | loop fusion | flops 8388608 | bytes 16779268 | tf_op jit(solution)/shard_map/while/body/eval_jaxpr/convert_element_type | solution.py:552
  269.9 3.4 convolution_add_fusion.4
  274.7 4.6 %convolution_add_fusion.5 = f32[88,4096]{1,0:T(8,128)} fusion(bf16[2,512,4096]{2,1,0:T(8,128)(2,1)} %get-tuple-element.481, s32[]{:T(128)} %get-tuple-element.465, f32[88,4096]{1,0:T(8,128)} %get-tuple-element.467, pred[]{:T(512)S(6)} %compare.67, bf16[2,88,512]{2,1,0:T(8,128)(2,1)S(1)} %get-tuple-element.482), kind=kOutput, calls=%fused_computation.15.clone.1 | convolution fusion | flops 369819648 | bytes 7169025 | tf_op jit(solution)/shard_map/while/body/eval_jaxpr/dot_general | solution.py:562
  279.7 2.3 reduce.11
  283.1 8.4 %all-to-all-start.5 = ((bf16[32,2,1408]{2,1,0:T(2,128)(2,1)}), bf16[32,2,1408]{2,1,0:T(2,128)(2,1)S(1)}, u32[]{:S(2)}, u32[]{:S(2)}) async-start(bf16[32,2,1408]{2,1,0:T(2,128)(2,1)} %reshape.355), calls=%async_computation.5 | async-start | bytes 360448 | tf_op jit(solution)/shard_map/all_to_all | solution.py:573
  293.3 7.1 %all-to-all-done.5 = bf16[32,2,1408]{2,1,0:T(2,128)(2,1)S(1)} async-done(((bf16[32,2,1408]{2,1,0:T(2,128)(2,1)}), bf16[32,2,1408]{2,1,0:T(2,128)(2,1)S(1)}, u32[]{:S(2)}, u32[]{:S(2)}) %all-to-all-start.5) | async-done | bytes 180256 | tf_op jit(solution)/shard_map/all_to_all | solution.py:573
  300.4 4.6 %all-to-all-start.6 = ((bf16[88,32,128]{2,0,1:T(8,128)(2,1)}), bf16[88,32,128]{2,0,1:T(8,128)(2,1)}, u32[]{:S(2)}, u32[]{:S(2)}) async-start(bf16[88,32,128]{2,0,1:T(8,128)(2,1)} %copy_bitcast_fusion.3), calls=%async_computation.6 | async-start | bytes 1441792 | tf_op jit(solution)/shard_map/all_to_all | solution.py:576
  310.5 2.5 fusion.26
  313.0 2.2 copy.214
  315.9 2.4 copy_bitcast_fusion.2
  318.3 8.6 %all-to-all-start.7 = ((bf16[88,32,128]{2,0,1:T(8,128)(2,1)}), bf16[88,32,128]{2,0,1:T(8,128)(2,1)}, u32[]{:S(2)}, u32[]{:S(2)}) async-start(bf16[88,32,128]{2,0,1:T(8,128)(2,1)} %copy_bitcast_fusion.2), calls=%async_computation.7 | async-start | bytes 1441792 | tf_op jit(solution)/shard_map/all_to_all | solution.py:579
  327.3 3.5 fusion.24
  330.9 2.5 reshape.354
  335.6 68.8 %shard_map.163 = (f32[48,768]{1,0:T(8,128)S(1)}, f32[24,1408]{1,0:T(8,128)S(1)}, f32[48,768]{1,0:T(8,128)S(1)}, f32[8,2304]{1,0:T(8,128)S(1)}, f32[16,256]{1,0:T(8,128)S(1)}) custom-call(bf16[4,2,4,48,1536]{4,3,2,1,0:T(8,128)(2,1)} %bitcast.305, bf16[4,2,4,24,1408]{4,3,2,1,0:T(8,128)(2,1)S(1)} %bitcast.298, ...), custom_call_target="tpu_custom_call" | custom-call | tf_op jit(solution)/shard_map/pallas_call | solution.py:373
  406.6 2.8 fusion.25
  413.0 5.3 %fusion.63 = (f32[128]{0:T(128)S(1)}, f32[128]{0:T(128)S(1)}, f32[128,1408]{1,0:T(8,128)S(1)}) fusion(f32[128]{0:T(128)S(1)} %copy-done.51, f32[128]{0:T(128)S(1)} %copy-done.50, bf16[128,1408]{1,0:T(8,128)(2,1)S(1)} %copy-done.12, f32[1408]{0:T(1024)S(1)} %copy-done.46, bf16[2304,128]{1,0:T(8,128)(2,1)S(1)} %bitcast.321, bf16[1408,2304]{1,0:T(8,128)(2,1)} %bitcast.295), kind=kOutput, calls=%fused_computation.143 | convolution fusion | flops 831733504 | bytes 8166912 | tf_op jit(solution)/shard_map/dot_general | solution.py:596
  (240 shorter events, 83.3 us)
Async XLA Ops:
  0.6 97.9 %copy-start = (bf16[3,3,256,256]{3,2,1,0:T(8,128)(2,1)S(1)}, bf16[3,3,256,256]{3,2,1,0:T(8,128)(2,1)}, u32[]{:S(2)}) copy-start(bf16[3,3,256,256]{3,2,1,0:T(8,128)(2,1)} %param.28) | copy-start | bytes 3538948
  0.6 4.9 %copy-start.43 = (bf16[44,1536]{1,0:T(8,128)(2,1)S(1)}, bf16[44,1536]{1,0:T(8,128)(2,1)}, u32[]{:S(2)}) copy-start(bf16[44,1536]{1,0:T(8,128)(2,1)} %param.25) | copy-start | bytes 405508
  0.7 4.9 %copy-start.44 = (bf16[22,1408]{1,0:T(8,128)(2,1)S(1)}, bf16[22,1408]{1,0:T(8,128)(2,1)}, u32[]{:S(2)}) copy-start(bf16[22,1408]{1,0:T(8,128)(2,1)} %param.24) | copy-start | bytes 185860
  1.9 3.7 copy-start.49
  5.6 58.0 %copy-start.20 = (bf16[128,1408]{1,0:T(8,128)(2,1)}, bf16[128,1408]{1,0:T(8,128)(2,1)S(1)}, u32[]{:S(2)}) copy-start(bf16[128,1408]{1,0:T(8,128)(2,1)S(1)} %get-tuple-element.304) | copy-start | bytes 1081348
  67.1 8.0 %copy-start.47 = (f32[256]{0:T(256)S(1)}, f32[256]{0:T(256)}, u32[]{:S(2)}) copy-start(f32[256]{0:T(256)} %param.27) | copy-start | bytes 3076
  76.7 20.8 %collective-permute-start = (bf16[1,128,256]{2,1,0:T(8,128)(2,1)}, bf16[1,128,256]{2,1,0:T(8,128)(2,1)}, u32[]{:S(2)}, u32[]{:S(2)}) collective-permute-start(bf16[1,128,256]{2,1,0:T(8,128)(2,1)} %get-tuple-element.308), channel_id=1, source_target_pairs={{0,1},{1,2},{2,3},{3,4},{4,5},{5,6},{6,7},{7,8},{8,9},{9,10},{10,1... | collective-permute-start | bytes 196616 | tf_op jit(solution)/shard_map/ppermute | solution.py:26
  79.8 17.7 %collective-permute-start.1 = (bf16[1,128,256]{2,1,0:T(8,128)(2,1)}, bf16[1,128,256]{2,1,0:T(8,128)(2,1)}, u32[]{:S(2)}, u32[]{:S(2)}) collective-permute-start(bf16[1,128,256]{2,1,0:T(8,128)(2,1)} %get-tuple-element.309), channel_id=1, source_target_pairs={{1,0},{2,1},{3,2},{4,3},{5,4},{6,5},{7,6},{8,7},{9,8},{10,9},{11,1... | collective-permute-start | bytes 196616 | tf_op jit(solution)/shard_map/ppermute | solution.py:29
  81.7 9.7 %copy-start.45 = (f32[1408]{0:T(1024)S(1)}, f32[1408]{0:T(1024)}, u32[]{:S(2)}) copy-start(f32[1408]{0:T(1024)} %param.22) | copy-start | bytes 16900
  91.4 6.2 %copy-start.14 = (bf16[512,256]{1,0:T(8,128)(2,1)S(1)}, bf16[512,256]{1,0:T(8,128)(2,1)}, u32[]{:S(2)}) copy-start(bf16[512,256]{1,0:T(8,128)(2,1)} %copy-done.13) | copy-start | bytes 786436
  98.6 4.8 %copy-start.30 = (bf16[4,128,256]{2,1,0:T(8,128)(2,1)S(1)}, bf16[4,128,256]{2,1,0:T(8,128)(2,1)}, u32[]{:S(2)}) copy-start(bf16[4,128,256]{2,1,0:T(8,128)(2,1)} %param.21) | copy-start | bytes 786436
  98.6 4.8 %copy-start.52 = (f32[256]{0:T(256)S(1)}, f32[256]{0:T(256)}, u32[]{:S(2)}) copy-start(f32[256]{0:T(256)} %param.29) | copy-start | bytes 3076
  112.9 19.8 %collective-permute-start.2 = (bf16[128,256]{1,0:T(8,128)(2,1)}, bf16[128,256]{1,0:T(8,128)(2,1)}, u32[]{:S(2)}, u32[]{:S(2)}) collective-permute-start(bf16[128,256]{1,0:T(8,128)(2,1)} %bitcast.247), channel_id=1, source_target_pairs={{0,1},{1,2},{2,3},{3,4},{4,5},{5,6},{6,7},{7,8},{8,9},{9,10},{10,1... | collective-permute-start | bytes 196616 | tf_op jit(solution)/shard_map/ppermute | solution.py:37
  119.1 27.7 %all-to-all-start = ((bf16[32,88,32]{1,2,0:T(8,128)(2,1)}), bf16[32,88,32]{1,2,0:T(8,128)(2,1)}, u32[]{:S(2)}, u32[]{:S(2)}) async-start(bf16[32,88,32]{1,2,0:T(8,128)(2,1)} %copy.184), calls=%async_computation | async-start | bytes 524288 | tf_op jit(solution)/shard_map/all_to_all | solution.py:436
  130.9 6.8 %copy-start.9 = (f32[512,256]{1,0:T(8,128)S(1)}, f32[512,256]{1,0:T(8,128)}, u32[]{:S(2)}) copy-start(f32[512,256]{1,0:T(8,128)} %copy-done.8) | copy-start | bytes 1572868
  130.9 6.8 %copy-start.48 = (f32[256]{0:T(256)S(1)}, f32[256]{0:T(256)}, u32[]{:S(2)}) copy-start(f32[256]{0:T(256)} %param.27) | copy-start | bytes 3076
  131.3 7.9 %copy-start.40 = (bf16[384,256]{1,0:T(8,128)(2,1)S(1)}, bf16[384,256]{1,0:T(8,128)(2,1)}, u32[]{:S(2)}) copy-start(bf16[384,256]{1,0:T(8,128)(2,1)} %param.26) | copy-start | bytes 589828
  131.4 6.2 %collective-permute-start.3 = (bf16[128,256]{1,0:T(8,128)(2,1)S(1)}, bf16[128,256]{1,0:T(8,128)(2,1)S(1)}, u32[]{:S(2)}, u32[]{:S(2)}) collective-permute-start(bf16[128,256]{1,0:T(8,128)(2,1)S(1)} %bitcast.348), channel_id=1, source_target_pairs={{1,0},{2,1},{3,2},{4,3},{5,4},{6,5},{7,6},{8,7},{9,8},{10,9},{11,1... | collective-permute-start | bytes 196616 | tf_op jit(solution)/shard_map/ppermute | solution.py:37
  140.2 4.8 %copy-start.16 = (bf16[128,1536]{1,0:T(8,128)(2,1)}, bf16[128,1536]{1,0:T(8,128)(2,1)S(1)}, u32[]{:S(2)}) copy-start(bf16[128,1536]{1,0:T(8,128)(2,1)S(1)} %reshape.330) | copy-start | bytes 1179652
  140.2 4.8 %copy-start.11 = (bf16[8,88,1408]{2,1,0:T(8,128)(2,1)S(1)}, bf16[8,88,1408]{2,1,0:T(8,128)(2,1)}, u32[]{:S(2)}) copy-start(bf16[8,88,1408]{2,1,0:T(8,128)(2,1)} %slice.155) | copy-start | bytes 5947396
  145.0 12.8 %copy-start.18 = (bf16[128,1408]{1,0:T(8,128)(2,1)}, bf16[128,1408]{1,0:T(8,128)(2,1)S(1)}, u32[]{:S(2)}) copy-start(bf16[128,1408]{1,0:T(8,128)(2,1)S(1)} %get-tuple-element.495) | copy-start | bytes 1081348
  145.0 12.8 %copy-start.26 = (bf16[24,96,128]{2,1,0:T(8,128)(2,1)S(1)}, bf16[24,96,128]{2,1,0:T(8,128)(2,1)}, u32[]{:S(2)}) copy-start(bf16[24,96,128]{2,1,0:T(8,128)(2,1)} %get-tuple-element.314) | copy-start | bytes 1769476
  146.9 20.0 %all-to-all-start.4 = ((bf16[32,88,32]{1,2,0:T(8,128)(2,1)}), bf16[32,88,32]{1,2,0:T(8,128)(2,1)S(1)}, u32[]{:S(2)}, u32[]{:S(2)}) async-start(bf16[32,88,32]{1,2,0:T(8,128)(2,1)} %bitcast.40), calls=%async_computation.4 | async-start | bytes 524288 | tf_op jit(solution)/shard_map/all_to_all | solution.py:540
  157.8 30.5 %copy-start.21 = (bf16[128,1408]{1,0:T(8,128)(2,1)S(1)}, bf16[128,1408]{1,0:T(8,128)(2,1)}, u32[]{:S(2)}) copy-start(bf16[128,1408]{1,0:T(8,128)(2,1)} %copy-done.20) | copy-start | bytes 1081348
  182.3 7.1 %copy-start.15 = (bf16[512,256]{1,0:T(8,128)(2,1)S(1)}, bf16[512,256]{1,0:T(8,128)(2,1)}, u32[]{:S(2)}) copy-start(bf16[512,256]{1,0:T(8,128)(2,1)} %copy-done.13) | copy-start | bytes 786436
  183.3 15.9 %all-to-all-start.2 = ((bf16[32,88,128]{2,1,0:T(8,128)(2,1)}), bf16[32,88,128]{2,1,0:T(8,128)(2,1)}, u32[]{:S(2)}, u32[]{:S(2)}) async-start(bf16[32,88,128]{2,1,0:T(8,128)(2,1)} %bitcast.16), calls=%async_computation.2 | async-start | bytes 1441792 | tf_op jit(solution)/shard_map/all_to_all | solution.py:441
  190.4 5.2 %copy-start.37 = (bf16[32,88,32]{1,2,0:T(8,128)(2,1)S(1)}, bf16[32,88,32]{1,2,0:T(8,128)(2,1)}, u32[]{:S(2)}) copy-start(bf16[32,88,32]{1,2,0:T(8,128)(2,1)} %copy-done.36) | copy-start | bytes 540676
  191.5 4.3 %copy-start.23 = (bf16[32,88,128]{2,1,0:T(8,128)(2,1)S(1)}, bf16[32,88,128]{2,1,0:T(8,128)(2,1)}, u32[]{:S(2)}) copy-start(bf16[32,88,128]{2,1,0:T(8,128)(2,1)} %all_to_all.116) | copy-start | bytes 2162692
  235.3 47.8 %all-to-all-start.3 = ((bf16[32,2,1408]{2,1,0:T(2,128)(2,1)}), bf16[32,2,1408]{2,1,0:T(2,128)(2,1)}, u32[]{:S(2)}, u32[]{:S(2)}) async-start(bf16[32,2,1408]{2,1,0:T(2,128)(2,1)} %reshape.353), calls=%async_computation.3 | async-start | bytes 360448 | tf_op jit(solution)/shard_map/all_to_all | solution.py:464
  251.3 3.4 copy-start.5
  269.9 3.4 copy-start.5
  279.4 12.2 %copy-start.35 = (bf16[4,128,256]{2,1,0:T(8,128)(2,1)S(1)}, bf16[4,128,256]{2,1,0:T(8,128)(2,1)}, u32[]{:S(2)}) copy-start(bf16[4,128,256]{2,1,0:T(8,128)(2,1)} %get-tuple-element.302) | copy-start | bytes 786436
  283.1 17.3 %all-to-all-start.5 = ((bf16[32,2,1408]{2,1,0:T(2,128)(2,1)}), bf16[32,2,1408]{2,1,0:T(2,128)(2,1)S(1)}, u32[]{:S(2)}, u32[]{:S(2)}) async-start(bf16[32,2,1408]{2,1,0:T(2,128)(2,1)} %reshape.355), calls=%async_computation.5 | async-start | bytes 360448 | tf_op jit(solution)/shard_map/all_to_all | solution.py:573
  291.5 15.2 %copy-start.10 = (f32[512,256]{1,0:T(8,128)S(1)}, f32[512,256]{1,0:T(8,128)}, u32[]{:S(2)}) copy-start(f32[512,256]{1,0:T(8,128)} %copy-done.8) | copy-start | bytes 1572868
  292.3 15.3 %copy-start.33 = (bf16[4,128,256]{2,1,0:T(8,128)(2,1)S(1)}, bf16[4,128,256]{2,1,0:T(8,128)(2,1)}, u32[]{:S(2)}) copy-start(bf16[4,128,256]{2,1,0:T(8,128)(2,1)} %get-tuple-element.300) | copy-start | bytes 786436
  292.3 16.0 %copy-start.32 = (bf16[4,128,256]{2,1,0:T(8,128)(2,1)S(1)}, bf16[4,128,256]{2,1,0:T(8,128)(2,1)}, u32[]{:S(2)}) copy-start(bf16[4,128,256]{2,1,0:T(8,128)(2,1)} %get-tuple-element.299) | copy-start | bytes 786436
  293.3 15.8 %copy-start.34 = (bf16[4,128,256]{2,1,0:T(8,128)(2,1)S(1)}, bf16[4,128,256]{2,1,0:T(8,128)(2,1)}, u32[]{:S(2)}) copy-start(bf16[4,128,256]{2,1,0:T(8,128)(2,1)} %get-tuple-element.306) | copy-start | bytes 786436
  293.3 16.5 %copy-start.31 = (bf16[4,128,256]{2,1,0:T(8,128)(2,1)S(1)}, bf16[4,128,256]{2,1,0:T(8,128)(2,1)}, u32[]{:S(2)}) copy-start(bf16[4,128,256]{2,1,0:T(8,128)(2,1)} %get-tuple-element.298) | copy-start | bytes 786436
  293.3 17.2 %copy-start.29 = (bf16[4,128,256]{2,1,0:T(8,128)(2,1)S(1)}, bf16[4,128,256]{2,1,0:T(8,128)(2,1)}, u32[]{:S(2)}) copy-start(bf16[4,128,256]{2,1,0:T(8,128)(2,1)} %copy-done.28) | copy-start | bytes 786436
  300.4 17.9 %all-to-all-start.6 = ((bf16[88,32,128]{2,0,1:T(8,128)(2,1)}), bf16[88,32,128]{2,0,1:T(8,128)(2,1)}, u32[]{:S(2)}, u32[]{:S(2)}) async-start(bf16[88,32,128]{2,0,1:T(8,128)(2,1)} %copy_bitcast_fusion.3), calls=%async_computation.6 | async-start | bytes 1441792 | tf_op jit(solution)/shard_map/all_to_all | solution.py:576
  315.9 11.0 %copy-start.25 = (bf16[512,384]{1,0:T(8,128)(2,1)S(1)}, bf16[512,384]{1,0:T(8,128)(2,1)}, u32[]{:S(2)}) copy-start(bf16[512,384]{1,0:T(8,128)(2,1)} %reshape.324) | copy-start | bytes 1179652
  315.9 11.0 %copy-start.39 = (bf16[512,256]{1,0:T(8,128)(2,1)S(1)}, bf16[512,256]{1,0:T(8,128)(2,1)}, u32[]{:S(2)}) copy-start(bf16[512,256]{1,0:T(8,128)(2,1)} %copy-done.38) | copy-start | bytes 786436
  315.9 11.4 %copy-start.17 = (bf16[128,1536]{1,0:T(8,128)(2,1)S(1)}, bf16[128,1536]{1,0:T(8,128)(2,1)}, u32[]{:S(2)}) copy-start(bf16[128,1536]{1,0:T(8,128)(2,1)} %copy-done.16) | copy-start | bytes 1179652
  315.9 11.4 %copy-start.24 = (bf16[128,32,48]{0,2,1:T(8,128)(2,1)S(1)}, bf16[128,32,48]{0,2,1:T(8,128)(2,1)}, u32[]{:S(2)}) copy-start(bf16[128,32,48]{0,2,1:T(8,128)(2,1)} %pad.46) | copy-start | bytes 1179652
  318.3 92.4 %all-to-all-start.7 = ((bf16[88,32,128]{2,0,1:T(8,128)(2,1)}), bf16[88,32,128]{2,0,1:T(8,128)(2,1)}, u32[]{:S(2)}, u32[]{:S(2)}) async-start(bf16[88,32,128]{2,0,1:T(8,128)(2,1)} %copy_bitcast_fusion.2), calls=%async_computation.7 | async-start | bytes 1441792 | tf_op jit(solution)/shard_map/all_to_all | solution.py:579
  330.9 4.0 copy-start.19
  412.9 5.4 %copy-start.22 = (f32[128,1408]{1,0:T(8,128)S(1)}, f32[128,1408]{1,0:T(8,128)}, u32[]{:S(2)}) copy-start(f32[128,1408]{1,0:T(8,128)} %get-tuple-element.323) | copy-start | bytes 2162692
  412.9 8.4 %copy-start.1 = (bf16[3,3,256,256]{3,2,1,0:T(8,128)(2,1)S(1)}, bf16[3,3,256,256]{3,2,1,0:T(8,128)(2,1)}, u32[]{:S(2)}) copy-start(bf16[3,3,256,256]{3,2,1,0:T(8,128)(2,1)} %param.28) | copy-start | bytes 3538948
  (19 other events, 37.0 us)

commit v3 on v2

--- a/solution.py
+++ b/solution.py
@@ -66,29 +66,6 @@
         left, right, (((0,), (0,)), ((), ())), preferred_element_type=jnp.float32
     )
     return (product * grad_scale).astype(jnp.bfloat16)
-
-
-def to_heads(features, pieces):
-    width = features.shape[0] // HEADS
-    columns = features.shape[1] // pieces
-    grouped = features.reshape(HEADS, width, pieces, columns).transpose(0, 2, 1, 3)
-    return grouped.reshape(HEADS * pieces, width, columns)
-
-
-def from_heads(received, pieces):
-    width = received.shape[1]
-    columns = received.shape[2]
-    grouped = received.reshape(HEADS, pieces, width, columns).transpose(0, 2, 1, 3)
-    return grouped.reshape(HEADS * width, pieces * columns)
-
-
-def copies(features, pieces):
-    width = features.shape[0] // HEADS
-    columns = features.shape[1]
-    spread = jnp.broadcast_to(
-        features.reshape(HEADS, 1, width, columns), (HEADS, pieces, width, columns)
-    )
-    return spread.reshape(HEADS * pieces, width, columns)
 
 
 MESH = pl.DeviceIdType.MESH
@@ -265,18 +242,6 @@
     )(*shards)
 
 
-def pad_heads(features):
-    groups = features.reshape(-1, HEAD, features.shape[-1])
-    return jnp.pad(groups, ((0, 0), (0, HEAD_PAD - HEAD), (0, 0))).reshape(
-        -1, features.shape[-1]
-    )
-
-
-def trim_heads(features):
-    groups = features.reshape(-1, HEAD_PAD, features.shape[-1])
-    return groups[:, :HEAD].reshape(-1, features.shape[-1])
-
-
 def scatter_kernel(plan, *refs):
     count = len(plan)
     arrays = 1 + max(source for source, _, _, _ in plan)
@@ -387,6 +352,283 @@
     )(*parts)
 
 
+TILE = 128
+QUERY_BLOCK = 512
+KEY_BLOCK = 1024
+
+
+def turned(block):
+    wide = block.astype(jnp.float32)
+    zeros = jnp.zeros((TILE - HEAD_PAD, TILE), jnp.float32)
+    return jnp.concatenate([wide, zeros], axis=0).T
+
+
+def head_rows(block):
+    return block.T[:HEAD_PAD].astype(jnp.bfloat16)
+
+
+def attention_kernel(
+    proj,
+    grad,
+    attn_out,
+    dqkv_out,
+    q_in,
+    g_in,
+    kv_in,
+    key_t,
+    value_t,
+    key,
+    value,
+    query,
+    cot,
+    query_t,
+    cot_t,
+    score,
+    weight,
+    inverse,
+    offset,
+    attended,
+    o_send,
+    dq_send,
+    d_send,
+    d_land,
+    d_sum,
+    o_land,
+    d_res,
+    send,
+    recv,
+):
+    x, zl, y, zh, core = place()
+    m = x * 2 + zl
+    plane = [(m + k) % 8 for k in range(8)]
+    source = [(m + 8 - k) % 8 for k in range(8)]
+    column = [(y + k) % 4 for k in range(4)]
+
+    def at_plane(k):
+        return {"sp": plane[k] * 4 + y}
+
+    def at_column(k):
+        return {"sp": m * 4 + column[k]}
+
+    greet([at_plane(k) for k in range(1, 8)] + [at_column(k) for k in range(1, 4)])
+    copies = {}
+
+    def push(slot, src, dst, target):
+        copy = pltpu.make_async_remote_copy(
+            src_ref=src,
+            dst_ref=dst,
+            send_sem=send.at[slot],
+            recv_sem=recv.at[slot],
+            device_id=target,
+            device_id_type=MESH,
+        )
+        copy.start()
+        copies[slot] = copy
+
+    kv_at, q_at, g_at, ring_at, o_at, dq_at, back_at, home_at = 0, 8, 16, 24, 48, 56, 64, 72
+    for k in range(1, 8):
+        push(kv_at + k, proj.at[pl.ds(1, 2), plane[k]], kv_in.at[y, m], at_plane(k))
+    kv_in[y, m, 0] = proj[1, m]
+    kv_in[y, m, 1] = proj[2, m]
+    q_in[m] = proj[0, m]
+    g_in[m] = grad[m]
+
+    def pass_on(k):
+        piece = kv_in.at[y, source[k]]
+        for j in range(1, 4):
+            push(ring_at + 3 * k + j - 1, piece, piece, at_column(j))
+
+    pass_on(0)
+    for k in range(1, 8):
+        push(q_at + k, proj.at[0, plane[k]], q_in.at[m], at_plane(k))
+    for k in range(1, 8):
+        copies[kv_at + k].wait_recv()
+        pass_on(k)
+    for k in range(1, 8):
+        push(g_at + k, grad.at[plane[k]], g_in.at[m], at_plane(k))
+    zero_rows = jnp.zeros((TILE - HEAD_PAD, key_t.shape[1]), jnp.bfloat16)
+    key_t[HEAD_PAD:] = zero_rows
+    value_t[HEAD_PAD:] = zero_rows
+
+    def prepare(t, carry):
+        at = pl.ds(pl.multiple_of(t * TILE, TILE), TILE)
+        block = kv_in[t // 8, t % 8, 0]
+        key_t[:HEAD_PAD, at] = block
+        key[at, :] = turned(block).astype(jnp.bfloat16)
+        block = kv_in[t // 8, t % 8, 1]
+        value_t[:HEAD_PAD, at] = block
+        value[at, :] = turned(block).astype(jnp.bfloat16)
+        return carry
+
+    def prepare_queries(t, carry):
+        query[pl.ds(pl.multiple_of(t * TILE, TILE), TILE), :] = turned(q_in[t]).astype(jnp.bfloat16)
+        return carry
+
+    def prepare_cots(t, carry):
+        cot[pl.ds(pl.multiple_of(t * TILE, TILE), TILE), :] = turned(g_in[t]).astype(jnp.bfloat16)
+        return carry
+
+    lax.fori_loop(y * 8, y * 8 + 8, prepare, 0)
+    for k in range(1, 8):
+        copies[q_at + k].wait_recv()
+    lax.fori_loop(0, 8, prepare_queries, 0)
+    for j in range(1, 4):
+        for k in range(8):
+            copies[ring_at + 3 * k + j - 1].wait_recv()
+        first = ((y + 4 - j) % 4) * 8
+        lax.fori_loop(first, first + 8, prepare, 0)
+    for k in range(1, 8):
+        copies[g_at + k].wait_recv()
+    lax.fori_loop(0, 8, prepare_cots, 0)
+
+    tokens = key.shape[0]
+    queries = query.shape[0]
+    blocks = [pl.ds(c * KEY_BLOCK, KEY_BLOCK) for c in range(tokens // KEY_BLOCK)]
+
+    def forward(i, carry):
+        at = pl.ds(pl.multiple_of(i * QUERY_BLOCK, QUERY_BLOCK), QUERY_BLOCK)
+        top = jnp.full((QUERY_BLOCK, 1), -jnp.inf, jnp.float32)
+        for block in blocks:
+            part = jnp.dot(query[at, :], key_t[:, block], preferred_element_type=jnp.float32)
+            score[:, block] = part
+            top = jnp.maximum(top, jnp.max(part, axis=1, keepdims=True))
+        total = jnp.zeros((QUERY_BLOCK, 1), jnp.float32)
+        mixed = jnp.zeros((QUERY_BLOCK, TILE), jnp.float32)
+        for block in blocks:
+            part = jnp.exp(score[:, block] - top)
+            total += jnp.sum(part, axis=1, keepdims=True)
+            rounded = part.astype(jnp.bfloat16)
+            weight[at, block] = rounded
+            mixed += jnp.dot(rounded, value[block, :], preferred_element_type=jnp.float32)
+        inv = 1.0 / total
+        mixed = mixed * inv
+        attended[at, :] = mixed
+        inverse[at, :] = inv
+        offset[at, :] = jnp.sum(mixed * cot[at, :].astype(jnp.float32), axis=1, keepdims=True)
+        return carry
+
+    lax.fori_loop(0, queries // QUERY_BLOCK, forward, 0)
+    for t in range(8):
+        at = pl.ds(t * TILE, TILE)
+        o_send[t] = head_rows(attended[at, :])
+    for k in range(1, 8):
+        push(o_at + k, o_send.at[plane[k]], o_land.at[m], at_plane(k))
+    o_land[m] = o_send[m]
+    for t in range(8):
+        at = pl.ds(t * TILE, TILE)
+        inv = inverse[at, :]
+        query_t[:, at] = (query[at, :].astype(jnp.float32) * inv).T.astype(jnp.bfloat16)
+        cot_t[:, at] = (cot[at, :].astype(jnp.float32) * inv).T.astype(jnp.bfloat16)
+
+    def key_side(left, kind):
+        for j in (1, 2, 3, 0):
+            yy = column[j]
+            at = pl.ds(pl.multiple_of(yy * 8 * TILE, 8 * TILE), 8 * TILE)
+            result = jnp.dot(left[...], weight[:, at], preferred_element_type=jnp.float32)
+            for t in range(8):
+                d_send[kind, j, t] = result[:HEAD_PAD, t * TILE : (t + 1) * TILE].astype(
+                    jnp.bfloat16
+                )
+            if j:
+                push(back_at + 4 * kind + j, d_send.at[kind, j], d_land.at[kind, j - 1], at_column(j))
+
+    def key_home(kind):
+        for j in range(1, 4):
+            copies[back_at + 4 * kind + j].wait_recv()
+        for t in range(8):
+            total = d_send[kind, 0, t].astype(jnp.float32)
+            for j in range(3):
+                total += d_land[kind, j, t].astype(jnp.float32)
+            d_sum[kind, t] = total.astype(jnp.bfloat16)
+        for k in range(1, 8):
+            push(
+                home_at + 8 * kind + k,
+                d_sum.at[kind, plane[k]],
+                d_res.at[kind + 1, m],
+                at_plane(k),
+            )
+        d_res[kind + 1, m] = d_sum[kind, m]
+
+    key_side(cot_t, 1)
+
+    def backward(i, carry):
+        at = pl.ds(pl.multiple_of(i * QUERY_BLOCK, QUERY_BLOCK), QUERY_BLOCK)
+        query_grad = jnp.zeros((QUERY_BLOCK, TILE), jnp.float32)
+        shift = offset[at, :]
+        for block in blocks:
+            dprob = jnp.dot(cot[at, :], value_t[:, block], preferred_element_type=jnp.float32)
+            dscore = (weight[at, block].astype(jnp.float32) * (dprob - shift)).astype(jnp.bfloat16)
+            weight[at, block] = dscore
+            query_grad += jnp.dot(dscore, key[block, :], preferred_element_type=jnp.float32)
+        attended[at, :] = query_grad * (inverse[at, :] * HEAD ** (-0.5))
+        return carry
+
+    lax.fori_loop(0, queries // QUERY_BLOCK, backward, 0)
+    key_side(query_t, 0)
+    for t in range(8):
+        dq_send[t] = head_rows(attended[pl.ds(t * TILE, TILE), :])
+    for k in range(1, 8):
+        push(dq_at + k, dq_send.at[plane[k]], d_res.at[0, m], at_plane(k))
+    d_res[0, m] = dq_send[m]
+    key_home(1)
+    key_home(0)
+    for k in range(1, 8):
+        copies[o_at + k].wait_recv()
+    attn_out[...] = o_land[...]
+    for first in (dq_at, home_at, home_at + 8):
+        for k in range(1, 8):
+            copies[first + k].wait_recv()
+    dqkv_out[...] = d_res[...]
+    for copy in copies.values():
+        copy.wait_send()
+
+
+def attend_both_ways(proj, grad):
+    heads = grad.shape[0]
+    tokens, queries = 32 * TILE, 8 * TILE
+    bf16, f32 = jnp.bfloat16, jnp.float32
+    block = (HEAD_PAD, TILE)
+    shapes = [
+        ((8, *block), bf16),
+        ((8, *block), bf16),
+        ((4, 8, 2, *block), bf16),
+        ((TILE, tokens), bf16),
+        ((TILE, tokens), bf16),
+        ((tokens, TILE), bf16),
+        ((tokens, TILE), bf16),
+        ((queries, TILE), bf16),
+        ((queries, TILE), bf16),
+        ((TILE, queries), bf16),
+        ((TILE, queries), bf16),
+        ((QUERY_BLOCK, tokens), f32),
+        ((queries, tokens), bf16),
+        ((queries, 1), f32),
+        ((queries, 1), f32),
+        ((queries, TILE), f32),
+        ((8, *block), bf16),
+        ((8, *block), bf16),
+        ((2, 4, 8, *block), bf16),
+        ((2, 3, 8, *block), bf16),
+        ((2, 8, *block), bf16),
+        ((8, *block), bf16),
+        ((3, 8, *block), bf16),
+    ]
+    return pl.pallas_call(
+        attention_kernel,
+        out_shape=[
+            jax.ShapeDtypeStruct((heads, *block), bf16),
+            jax.ShapeDtypeStruct((3, heads, *block), bf16),
+        ],
+        in_specs=[pl.BlockSpec(memory_space=pltpu.VMEM)] * 2,
+        out_specs=[pl.BlockSpec(memory_space=pltpu.VMEM)] * 2,
+        scratch_shapes=[pltpu.VMEM(shape, kind) for shape, kind in shapes]
+        + [pltpu.SemaphoreType.DMA((88,)), pltpu.SemaphoreType.DMA((88,))],
+        compiler_params=pltpu.CompilerParams(
+            collective_id=2, has_side_effects=True, vmem_limit_bytes=56 * 2**20
+        ),
+    )(proj, grad)
+
+
 def per_device(
     y_one,
     second_stream_state,
@@ -401,10 +643,8 @@
     conv_gain,
 ):
     devices = lax.axis_size("sp")
-    pieces = devices // HEADS
     tokens_here = y_one.shape[0]
     rows_here = tokens_here // GRID_W
-    inner = HEADS * HEAD
     score_scale = HEAD ** (-0.5)
     standardized_input, inverse_deviation = apply_layer_norm(
         second_stream_state.astype(jnp.float32)
@@ -424,49 +664,7 @@
     )
     deconv_full = deconv_full.reshape(devices * depth, -1)
     qkv_full = qkv_full.reshape(devices * depth, -1)
-    out_full = out_full[:, :HEAD, : w_out.shape[1]].reshape(inner, -1)
-    projected = trim_heads(
-        lax.dot_general(
-            qkv_full, normalized_rows, (((0,), (1,)), ((), ())), preferred_element_type=jnp.float32
-        )
-    )
-    queries = (projected[:inner] * score_scale).astype(jnp.bfloat16)
-    keys = projected[inner : 2 * inner].astype(jnp.bfloat16)
-    values = projected[2 * inner :].astype(jnp.bfloat16)
-    query_head = lax.all_to_all(
-        to_heads(queries, pieces), "sp", split_axis=0, concat_axis=2, tiled=True
-    )[0]
-    key_routed, value_routed = (
-        lax.all_to_all(copies(keys, pieces), "sp", split_axis=0, concat_axis=2, tiled=True),
-        lax.all_to_all(copies(values, pieces), "sp", split_axis=0, concat_axis=2, tiled=True),
-    )
-    key_head = key_routed[0]
-    value_head = value_routed[0]
-    total_queries = query_head.shape[1]
-    block = min(512, total_queries)
-    count_blocks = total_queries // block
-    query_blocks = query_head.reshape(HEAD, count_blocks, block).transpose(1, 0, 2)
-
-    def attend(query_block):
-        scores = lax.dot_general(
-            query_block, key_head, (((0,), (0,)), ((), ())), preferred_element_type=jnp.float32
-        )
-        shifted = jnp.exp(scores - jnp.max(scores, axis=1, keepdims=True))
-        weights = (shifted / jnp.sum(shifted, axis=1, keepdims=True)).astype(jnp.bfloat16)
-        output = lax.dot_general(
-            value_head, weights, (((1,), (1,)), ((), ())), preferred_element_type=jnp.float32
-        ).astype(jnp.bfloat16)
-        return (output, weights)
-
-    attended, kept_weights = lax.map(attend, query_blocks)
-    attended = attended.transpose(1, 0, 2).reshape(1, HEAD, total_queries)
-    attn_band = from_heads(
-        lax.all_to_all(attended, "sp", split_axis=2, concat_axis=0, tiled=True), pieces
-    )
-    mixed = lax.dot_general(
-        attn_band, out_full, (((0,), (0,)), ((), ())), preferred_element_type=jnp.float32
-    )
-    x_one = (y_one.astype(jnp.float32) - mixed).astype(jnp.bfloat16)
+    out_full = out_full.reshape(HEADS * HEAD_PAD, -1)[:, : w_out.shape[1]]
     feature = ((y_one.astype(jnp.float32) + second_stream_state.astype(jnp.float32)) * 0.5).astype(
         jnp.bfloat16
     )
@@ -530,6 +728,22 @@
     dattn = lax.dot_general(
         out_full, d_x1, (((1,), (1,)), ((), ())), preferred_element_type=jnp.float32
     ).astype(jnp.bfloat16)
+    projected = lax.dot_general(
+        qkv_full, normalized_rows, (((0,), (1,)), ((), ())), preferred_element_type=jnp.float32
+    ).reshape(3, HEADS, HEAD_PAD, tokens_here)
+    scales = jnp.array([score_scale, 1.0, 1.0], jnp.float32).reshape(3, 1, 1, 1)
+    projected = (projected * scales).astype(jnp.bfloat16)
+    attn_heads, dqkv = attend_both_ways(
+        projected, dattn.reshape(HEADS, HEAD_PAD, tokens_here)
+    )
+    mixed = lax.dot_general(
+        attn_heads.reshape(HEADS * HEAD_PAD, tokens_here),
+        out_full,
+        (((0,), (0,)), ((), ())),
+        preferred_element_type=jnp.float32,
+    )
+    x_one = (y_one.astype(jnp.float32) - mixed).astype(jnp.bfloat16)
+    attn_band = attn_heads[:, :HEAD]
     spread_attn = jnp.pad(
         attn_band.reshape(devices, out_depth, tokens_here), ((0, 0), (0, 24 - out_depth), (0, 0))
     ).reshape(devices * 24, tokens_here)
@@ -537,64 +751,9 @@
         spread_attn, d_x1, (((1,), (0,)), ((), ())), preferred_element_type=jnp.float32
     )
     out_part = (out_product * grad_scale).astype(jnp.bfloat16).reshape(4, 2, 4, 24, -1)
-    grad_head = lax.all_to_all(
-        to_heads(dattn, pieces), "sp", split_axis=0, concat_axis=2, tiled=True
-    )[0]
-    grad_blocks = grad_head.reshape(HEAD, count_blocks, block).transpose(1, 0, 2)
-
-    def backward_block(carry, operands):
-        key_grad, value_grad = carry
-        query_block, grad_block, weights = operands
-        wide = weights.astype(jnp.float32)
-        dprob = lax.dot_general(
-            grad_block, value_head, (((0,), (0,)), ((), ())), preferred_element_type=jnp.float32
-        )
-        dscore = (wide * (dprob - jnp.sum(wide * dprob, axis=1, keepdims=True))).astype(
-            jnp.bfloat16
-        )
-        query_grad = lax.dot_general(
-            key_head, dscore, (((1,), (1,)), ((), ())), preferred_element_type=jnp.float32
-        )
-        query_grad = (query_grad * score_scale).astype(jnp.bfloat16)
-        key_grad = key_grad + lax.dot_general(
-            query_block, dscore, (((1,), (0,)), ((), ())), preferred_element_type=jnp.float32
-        )
-        value_grad = value_grad + lax.dot_general(
-            grad_block, weights, (((1,), (0,)), ((), ())), preferred_element_type=jnp.float32
-        )
-        return ((key_grad, value_grad), query_grad)
-
-    zero_grads = jnp.zeros(key_head.shape, jnp.float32)
-    (key_grad, value_grad), query_grads = lax.scan(
-        backward_block, (zero_grads, zero_grads), (query_blocks, grad_blocks, kept_weights)
-    )
-    query_grads = query_grads.transpose(1, 0, 2).reshape(1, HEAD, total_queries)
-    dq_band = from_heads(
-        lax.all_to_all(query_grads, "sp", split_axis=2, concat_axis=0, tiled=True), pieces
-    )
-    key_parts, value_parts = (
-        lax.all_to_all(
-            key_grad.astype(jnp.bfloat16), "sp", split_axis=1, concat_axis=0, tiled=True
-        ).astype(key_grad.dtype),
-        lax.all_to_all(
-            value_grad.astype(jnp.bfloat16), "sp", split_axis=1, concat_axis=0, tiled=True
-        ).astype(value_grad.dtype),
-    )
-    dk_band = (
-        key_parts.reshape(HEADS, pieces, HEAD, tokens_here)
-        .sum(axis=1)
-        .reshape(inner, tokens_here)
-        .astype(jnp.bfloat16)
-    )
-    dv_band = (
-        value_parts.reshape(HEADS, pieces, HEAD, tokens_here)
-        .sum(axis=1)
-        .reshape(inner, tokens_here)
-        .astype(jnp.bfloat16)
-    )
-    dqkv = jnp.concatenate([dq_band, dk_band, dv_band], axis=0)
     normalized_gradient = lax.dot_general(
-        pad_heads(dqkv), qkv_full, (((0,), (1,)), ((), ())), preferred_element_type=jnp.float32
+        dqkv.reshape(3 * HEADS * HEAD_PAD, tokens_here),
+        qkv_full, (((0,), (1,)), ((), ())), preferred_element_type=jnp.float32
     )
     second_input_gradient = (
         halfway_split

time: 428 us -> 301 us (0.70)
  Pallas kernels: 123 us -> 198 us
  starting transfers between devices: 64.9 us -> 9.63 us
  local copies, waits for them, and re-layouts: 78.9 us -> 41.2 us
  other arithmetic: 43.6 us -> 6.84 us
  matrix products: 71.8 us -> 39.6 us
  waiting for transfers between devices: 22.7 us -> 0.01 us
  blocking collectives: 14.6 us -> 0 us
    pallas_call x0 -> x1, Pallas kernels: none -> 70.6 us  [attend_both_ways(): pl.pallas_call(attention_kernel, out_shape=[jax.ShapeDtypeStruct((heads,...]
    all_to_all x7 -> x0, starting transfers between devices: 54 us -> none  [the longest x1 10.9 us: per_device(): lax.all_to_all(to_heads(dattn, pieces), 'sp', split_axis=0, concat_axis=2...]
    dot_general x14 -> x2, matrix products: 39.3 us -> 6.08 us  [the longest x1 3.15 us: per_device(): lax.dot_general(dqkv.reshape(3 * HEADS * HEAD_PAD, tokens_here), qkv_full...]
    all_to_all x7 -> x0, waiting for transfers between devices: 18.6 us -> none  [the longest x1 9.07 us: per_device(): lax.all_to_all(to_heads(dattn, pieces), 'sp', split_axis=0, concat_axis=2...]
    all_to_all x1 -> x0, blocking collectives: 14.6 us -> none  [per_device(): lax.all_to_all(copies(keys, pieces), 'sp', split_axis=0, concat_axis=2, t...]
    unnamed x121 -> x71, local copies, waits for them, and re-layouts: 25.4 us -> 12.6 us
    convert_element_type x3 -> x0, other arithmetic: 12 us -> none  [the longest x2 12 us: backward_block(): (wide * (dprob - jnp.sum(wide * dprob, axis=1, keepdims=True))).astype(jn...]
    while x13 -> x0, local copies, waits for them, and re-layouts: 11.8 us -> none
  transfers between devices with their start and end apart: 11 -> 4, of which waited for: 4 -> 0; matrix products, arithmetic and copies ran while one was open for 26% -> 9% of each run, Pallas kernels for 16% -> 0%
where the time goes in v3:
time: 301 us; the launch traced here: 296 us
  Pallas kernels  198 us (66%)
  local copies, waits for them, and re-layouts  41.2 us (14%)
  matrix products  39.6 us (13%)
  starting transfers between devices  9.63 us (3%)
  other arithmetic  6.84 us (2%)
    pallas_call x1, Pallas kernels, scatter_sums(): pl.pallas_call(functools.partial(scatter_kernel, plan), out_shape=[jax.Sh...  72.6 us
    pallas_call x1, Pallas kernels, attend_both_ways(): pl.pallas_call(attention_kernel, out_shape=[jax.ShapeDtypeStruct((heads,...  70.6 us
    pallas_call x1, Pallas kernels, gather_weights(): pl.pallas_call(functools.partial(gather_kernel, shapes), out_shape=[jax.S...  54.4 us
    unnamed x71, local copies, waits for them, and re-layouts  12.6 us
    conv_general_dilated x2, matrix products, conv_valid(): lax.conv_general_dilated(padded[None], kernel, (1, 1), 'VALID', dimension...  10.4 us
    dot_general x1, local copies, waits for them, and re-layouts, per_device(): lax.dot_general(qkv_full, normalized_rows, (((0,), (1,)), ((), ())), pref...  9.72 us
    convert_element_type x2, local copies, waits for them, and re-layouts, per_device(): (conv_product.reshape(4, 2, 4, LAT // devices, 9 * LAT) * grad_scale).ast...  8.16 us
  transfers between devices with their start and end apart: 4, of which 0 were waited for; matrix products, arithmetic and copies ran while one was open for 9% of the time, Pallas kernels for 0%

profile of v3, /device:TPU:64, one launch (start us, length us, event | category | flops | bytes accessed | tf_op | source)
XLA Modules:
  0.0 296.5 jit_solution(17802220738412574142)
XLA Ops:
  0.7 1.4 reshape.243
  2.1 0.9 pad.36.refs_0_
  3.3 0.9 pad.38.refs_2_
  4.2 1.1 convert_reduce_fusion
  5.6 54.4 %shard_map.171 = (bf16[8,176,1536]{2,1,0:T(8,128)(2,1)S(1)}, bf16[8,176,2304]{2,1,0:T(8,128)(2,1)S(1)}, bf16[8,96,1536]{2,1,0:T(8,128)(2,1)S(1)}) custom-call(bf16[48,1536]{1,0:T(8,128)(2,1)S(1)} %pad.36.refs_0_, bf16[48,2304]{1,0:T(8,128)(2,1)S(1)} %reshape.244.refs_1_, bf16[32,1536]{1,0:T(8,128)(2,1)S(1)} %pad.38.refs_2_), custom_call_target="tpu_custom_call" | custom-call | tf_op jit(solution)/shard_map/pallas_call | solution.py:225
  60.0 2.7 copy-done.1
  62.7 1.4 copy-done.4
  64.2 2.0 copy-done.2
  66.1 0.8 convolution_convert_fusion
  67.5 0.4 copy-done.17
  68.7 0.6 slice_bitcast_fusion.1
  69.3 1.3 collective-permute-start.1
  70.6 4.5 %collective-permute-start = (bf16[1,128,256]{2,1,0:T(8,128)(2,1)S(1)}, bf16[1,128,256]{2,1,0:T(8,128)(2,1)S(1)}, u32[]{:S(2)}, u32[]{:S(2)}) collective-permute-start(bf16[1,128,256]{2,1,0:T(8,128)(2,1)S(1)} %get-tuple-element.67), channel_id=1, source_target_pairs={{0,1},{1,2},{2,3},{3,4},{4,5},{5,6},{6,7},{7,8},{8,9},{9,10},{10,1... | collective-permute-start | bytes 196616 | tf_op jit(solution)/shard_map/ppermute | solution.py:26
  75.2 9.7 %copy.35 = bf16[2304,1408]{1,0:T(8,128)(2,1)} copy(bf16[2304,1408]{0,1:T(8,128)(2,1)} %bitcast.135) | data formatting | bytes 12976128 | tf_op jit(solution)/shard_map/dot_general | solution.py:731
  85.0 5.6 %fusion.6.proj = bf16[3,8,96,128]{3,2,1,0:T(8,128)(2,1)} fusion(bf16[3,8,96,1408]{3,2,1,0:T(8,128)(2,1)} %bitcast.152, f32[3]{0:T(128)S(1)} %copy-done.26, bf16[128,1408]{1,0:T(8,128)(2,1)S(1)} %copy-done.5, f32[1408]{0:T(1024)S(1)} %copy-done.24, f32[128]{0:T(128)S(1)} %add_rsqrt_fusion.2, f32[128]{0:T(128)S(1)} %broadcast_multiply_fusion.7), kind=kOutput, calls=%fused_computation.14 | convolution fusion | flops 831963136 | bytes 7445004 | tf_op jit(solution)/shard_map/dot_general | solution.py:731
  90.9 0.8 pad.41
  91.7 0.6 copy-done.18
  92.5 4.5 %fusion.48 = (f32[4,128]{1,0:T(4,128)S(1)}, f32[1,4,128,256]{3,0,2,1:T(1,128)S(1)}) fusion(bf16[3,3,256,256]{3,2,1,0:T(8,128)(2,1)S(1)} %copy-done, bf16[1,6,130,256]{3,2,1,0:T(8,128)(2,1)S(1)} %fusion.74), kind=kOutput, calls=%fused_computation.106 | convolution fusion | flops 604110336 | bytes 2105344 | tf_op jit(solution)/shard_map/conv_general_dilated | solution.py:53
  97.3 0.4 fusion.30
  98.1 5.8 %fusion.49 = (bf16[1,6,128,256]{3,0,2,1:T(2,128)(2,1)S(1)}, f32[1,6,128,256]{3,0,2,1:T(1,128)S(1)}) fusion(bf16[3,3,256,256]{3,2,1,0:T(8,128)(2,1)S(1)} %copy-done, bf16[1,8,130,256]{3,2,1,0:T(8,128)(2,1)S(1)} %pad_bitcast_fusion), kind=kOutput, calls=%fused_computation.107 | convolution fusion | flops 906166272 | bytes 2891776 | tf_op jit(solution)/shard_map/conv_general_dilated | solution.py:53
  104.3 0.7 slice.149
  105.3 0.6 copy.76
  105.9 2.5 collective-permute-start.2
  108.5 0.6 copy.75
  109.1 1.3 collective-permute-start.3
  111.2 1.9 fusion.5
  113.1 4.4 %copy.42 = bf16[256,9,256]{2,1,0:T(8,128)(2,1)} copy(bf16[256,9,256]{0,2,1:T(8,128)(2,1)} %fusion.5) | data formatting | bytes 2359296 | tf_op jit(solution)/shard_map/convert_element_type | solution.py:705
  117.6 3.7 %convert_element_type.113.refs_2_ = bf16[4,2,4,8,2304]{4,3,2,1,0:T(8,128)(2,1)} reshape(bf16[256,9,256]{2,1,0:T(8,128)(2,1)} %copy.42) | data formatting | bytes 2359296 | tf_op jit(solution)/shard_map/convert_element_type | solution.py:705
  121.3 0.9 fusion.41
  123.4 1.0 fusion.10
  125.1 4.8 %fusion.50 = (bf16[128,1408]{1,0:T(8,128)(2,1)S(1)}, f32[128,1408]{1,0:T(8,128)}) fusion(bf16[128,1536]{1,0:T(8,128)(2,1)S(1)} %reshape.255, bf16[1408,1536]{1,0:T(8,128)(2,1)} %bitcast.140), kind=kOutput, calls=%fused_computation.108 | convolution fusion | flops 554008576 | bytes 5799936 | tf_op jit(solution)/shard_map/dot_general | solution.py:724
  129.9 0.7 copy-done.15
  130.6 3.2 %fusion.7 = bf16[768,128]{1,0:T(8,128)(2,1)} fusion(bf16[128,1408]{1,0:T(8,128)(2,1)S(1)} %get-tuple-element.88, bf16[768,1536]{1,0:T(8,128)(2,1)} %bitcast.142), kind=kOutput, calls=%fused_computation.19 | convolution fusion | flops 276922368 | bytes 2719744 | tf_op jit(solution)/shard_map/dot_general | solution.py:728
  133.8 70.6 %shard_map.172 = (bf16[8,96,128]{2,1,0:T(8,128)(2,1)}, bf16[3,8,96,128]{3,2,1,0:T(8,128)(2,1)}) custom-call(bf16[3,8,96,128]{3,2,1,0:T(8,128)(2,1)} %fusion.6.proj, bf16[8,96,128]{2,1,0:T(8,128)(2,1)} %bitcast.171), custom_call_target="tpu_custom_call" | custom-call | tf_op jit(solution)/shard_map/pallas_call | solution.py:616
  204.4 1.0 slice.132
  205.4 2.9 fusion.1
  208.4 3.1 %fusion.44 = (f32[128]{0:T(128)S(1)}, f32[128]{0:T(128)S(1)}, f32[128,1408]{1,0:T(8,128)}) fusion(f32[128]{0:T(128)S(1)} %add_rsqrt_fusion.2, f32[128]{0:T(128)S(1)} %broadcast_multiply_fusion.7, bf16[128,1408]{1,0:T(8,128)(2,1)S(1)} %copy-done.5, f32[1408]{0:T(1024)S(1)} %copy-done.24, bf16[2304,128]{1,0:T(8,128)(2,1)S(1)} %bitcast.170, ...), kind=kOutput, calls=%fused_computation.102 | convolution fusion | flops 831733504 | bytes 8166912 | tf_op jit(solution)/shard_map/dot_general | solution.py:754
  211.6 3.5 %fusion = bf16[1536,1536]{1,0:T(8,128)(2,1)} fusion(bf16[128,1536]{0,1:T(8,128)(2,1)S(1)} %bitcast.156, bf16[128,1536]{1,0:T(8,128)(2,1)S(1)} %copy-done.8), kind=kOutput, calls=%fused_computation.1 | convolution fusion | flops 608698368 | bytes 5505024 | tf_op jit(solution)/shard_map/dot_general | solution.py:65
  215.2 1.7 multiply_convert_fusion
  217.0 0.7 reshape.266
  217.7 1.0 pad.43
  218.7 1.3 copy-done.3
  220.0 72.6 %shard_map.173 = (f32[48,768]{1,0:T(8,128)S(1)}, f32[24,1408]{1,0:T(8,128)S(1)}, f32[48,768]{1,0:T(8,128)S(1)}, f32[8,2304]{1,0:T(8,128)S(1)}, f32[16,256]{1,0:T(8,128)S(1)}) custom-call(bf16[4,2,4,48,1536]{4,3,2,1,0:T(8,128)(2,1)} %bitcast.150, bf16[4,2,4,24,1408]{4,3,2,1,0:T(8,128)(2,1)S(1)} %bitcast.141, bf16[4,2,4,8,2304]{4,3,2,1,0:T(8,128)(2,1)S(1)} %copy-done.3, ...), custom_call_target="tpu_custom_call" | custom-call | tf_op jit(solution)/shard_map/pallas_call | solution.py:338
  292.6 0.7 pad_maximum_fusion
  293.3 1.1 fusion.26
  294.4 0.7 copy.90
  295.0 0.6 copy.91
  295.6 0.6 copy.92
  (107 shorter events, 6.4 us)
Async XLA Ops:
  0.6 91.8 %copy-start = (bf16[3,3,256,256]{3,2,1,0:T(8,128)(2,1)S(1)}, bf16[3,3,256,256]{3,2,1,0:T(8,128)(2,1)}, u32[]{:S(2)}) copy-start(bf16[3,3,256,256]{3,2,1,0:T(8,128)(2,1)} %param.25) | copy-start | bytes 3538948
  0.6 4.7 %copy-start.5 = (bf16[128,1408]{1,0:T(8,128)(2,1)S(1)}, bf16[128,1408]{1,0:T(8,128)(2,1)}, u32[]{:S(2)}) copy-start(bf16[128,1408]{1,0:T(8,128)(2,1)} %param.17) | copy-start | bytes 1081348
  0.7 4.7 %copy-start.14 = (bf16[128,1408]{1,0:T(8,128)(2,1)S(1)}, bf16[128,1408]{1,0:T(8,128)(2,1)}, u32[]{:S(2)}) copy-start(bf16[128,1408]{1,0:T(8,128)(2,1)} %param.16) | copy-start | bytes 1081348
  60.0 2.7 copy-start.1
  62.7 1.4 copy-start.4
  64.2 2.0 copy-start.2
  66.9 0.9 copy-start.17
  66.9 1.5 copy-start.23
  67.9 17.1 %copy-start.12 = (bf16[512,384]{1,0:T(8,128)(2,1)}, bf16[512,384]{1,0:T(8,128)(2,1)S(1)}, u32[]{:S(2)}) copy-start(bf16[512,384]{1,0:T(8,128)(2,1)S(1)} %reshape.249) | copy-start | bytes 1179652
  69.3 22.3 %collective-permute-start.1 = (bf16[1,128,256]{2,1,0:T(8,128)(2,1)}, bf16[1,128,256]{2,1,0:T(8,128)(2,1)S(1)}, u32[]{:S(2)}, u32[]{:S(2)}) collective-permute-start(bf16[1,128,256]{2,1,0:T(8,128)(2,1)} %get-tuple-element.68), channel_id=1, source_target_pairs={{1,0},{2,1},{3,2},{4,3},{5,4},{6,5},{7,6},{8,7},{9,8},{10,9},{11,1... | collective-permute-start | bytes 196616 | tf_op jit(solution)/shard_map/ppermute | solution.py:29
  70.6 21.1 %collective-permute-start = (bf16[1,128,256]{2,1,0:T(8,128)(2,1)S(1)}, bf16[1,128,256]{2,1,0:T(8,128)(2,1)S(1)}, u32[]{:S(2)}, u32[]{:S(2)}) collective-permute-start(bf16[1,128,256]{2,1,0:T(8,128)(2,1)S(1)} %get-tuple-element.67), channel_id=1, source_target_pairs={{0,1},{1,2},{2,3},{3,4},{4,5},{5,6},{6,7},{7,8},{8,9},{9,10},{10,1... | collective-permute-start | bytes 196616 | tf_op jit(solution)/shard_map/ppermute | solution.py:26
  75.2 9.8 %copy-start.24 = (f32[1408]{0:T(1024)S(1)}, f32[1408]{0:T(1024)}, u32[]{:S(2)}) copy-start(f32[1408]{0:T(1024)} %param.19) | copy-start | bytes 16900
  75.2 9.8 %copy-start.26 = (f32[3]{0:T(128)S(1)}, f32[3]{0:T(128)}, u32[]{:S(2)}) copy-start(f32[3]{0:T(128)} %constant.91.clone) | copy-start | bytes 40
  91.7 0.6 copy-start.18
  92.4 4.8 %copy-start.16 = (bf16[4,128,256]{2,1,0:T(8,128)(2,1)S(1)}, bf16[4,128,256]{2,1,0:T(8,128)(2,1)}, u32[]{:S(2)}) copy-start(bf16[4,128,256]{2,1,0:T(8,128)(2,1)} %param.18) | copy-start | bytes 786436
  92.4 4.8 %copy-start.25 = (f32[256]{0:T(256)S(1)}, f32[256]{0:T(256)}, u32[]{:S(2)}) copy-start(f32[256]{0:T(256)} %param.26) | copy-start | bytes 3076
  103.9 6.5 %copy-start.19 = (bf16[1,128,256]{2,1,0:T(8,128)(2,1)S(1)}, bf16[1,128,256]{2,1,0:T(8,128)(2,1)}, u32[]{:S(2)}) copy-start(bf16[1,128,256]{2,1,0:T(8,128)(2,1)} %copy-done.18) | copy-start | bytes 196612
  105.9 15.4 %collective-permute-start.2 = (bf16[128,256]{1,0:T(8,128)(2,1)}, bf16[128,256]{1,0:T(8,128)(2,1)S(1)}, u32[]{:S(2)}, u32[]{:S(2)}) collective-permute-start(bf16[128,256]{1,0:T(8,128)(2,1)} %bitcast.122), channel_id=1, source_target_pairs={{0,1},{1,2},{2,3},{3,4},{4,5},{5,6},{6,7},{7,8},{8,9},{9,10},{10,1... | collective-permute-start | bytes 196616 | tf_op jit(solution)/shard_map/ppermute | solution.py:37
  109.1 12.2 %collective-permute-start.3 = (bf16[128,256]{1,0:T(8,128)(2,1)}, bf16[128,256]{1,0:T(8,128)(2,1)}, u32[]{:S(2)}, u32[]{:S(2)}) collective-permute-start(bf16[128,256]{1,0:T(8,128)(2,1)} %bitcast.121), channel_id=1, source_target_pairs={{1,0},{2,1},{3,2},{4,3},{5,4},{6,5},{7,6},{8,7},{9,8},{10,9},{11,1... | collective-permute-start | bytes 196616 | tf_op jit(solution)/shard_map/ppermute | solution.py:37
  117.6 3.7 %copy-start.21 = (f32[1,1,128,256]{3,0,2,1:T(1,128)S(1)}, f32[1,1,128,256]{3,0,2,1:T(1,128)}, u32[]{:S(2)}) copy-start(f32[1,1,128,256]{3,0,2,1:T(1,128)} %slice.149) | copy-start | bytes 393220
  121.3 2.1 copy-start.13
  125.1 4.8 %copy-start.7 = (bf16[128,1536]{1,0:T(8,128)(2,1)}, bf16[128,1536]{1,0:T(8,128)(2,1)S(1)}, u32[]{:S(2)}) copy-start(bf16[128,1536]{1,0:T(8,128)(2,1)S(1)} %reshape.255) | copy-start | bytes 1179652
  125.1 83.3 %slice-start = ((s8[6488064]{0:T(1024)(128)(4,1)}), s8[4194304]{0:T(1024)(128)(4,1)S(1)}, s32[]{:S(2)}) async-start(s8[6488064]{0:T(1024)(128)(4,1)} %bitcast.136), calls=%async_computation | async-start | bytes 8388608
  129.9 0.7 copy-start.15
  130.6 77.8 %slice-start.1 = ((s8[6488064]{0:T(1024)(128)(4,1)}), s8[2293760]{0:T(1024)(128)(4,1)S(1)}, s32[]{:S(2)}) async-start(s8[6488064]{0:T(1024)(128)(4,1)} %bitcast.136), calls=%async_computation.1 | async-start | bytes 4587520
  204.4 4.0 %copy-start.20 = (bf16[3,8,96,128]{3,2,1,0:T(8,128)(2,1)S(1)}, bf16[3,8,96,128]{3,2,1,0:T(8,128)(2,1)}, u32[]{:S(2)}) copy-start(bf16[3,8,96,128]{3,2,1,0:T(8,128)(2,1)} %get-tuple-element.45) | copy-start | bytes 1769476
  208.4 3.2 %copy-start.8 = (bf16[128,1536]{1,0:T(8,128)(2,1)S(1)}, bf16[128,1536]{1,0:T(8,128)(2,1)}, u32[]{:S(2)}) copy-start(bf16[128,1536]{1,0:T(8,128)(2,1)} %copy-done.7) | copy-start | bytes 1179652
  208.4 3.2 %copy-start.11 = (bf16[128,32,48]{0,2,1:T(8,128)(2,1)S(1)}, bf16[128,32,48]{0,2,1:T(8,128)(2,1)}, u32[]{:S(2)}) copy-start(bf16[128,32,48]{0,2,1:T(8,128)(2,1)} %pad.41) | copy-start | bytes 1179652
  215.1 1.8 copy-start.22
  218.7 1.3 copy-start.3
  220.0 73.3 %copy-start.6 = (bf16[128,1408]{1,0:T(8,128)(2,1)S(1)}, bf16[128,1408]{1,0:T(8,128)(2,1)}, u32[]{:S(2)}) copy-start(bf16[128,1408]{1,0:T(8,128)(2,1)} %param.17) | copy-start | bytes 1081348
  220.0 73.3 %copy-start.9 = (f32[128,1408]{1,0:T(8,128)S(1)}, f32[128,1408]{1,0:T(8,128)}, u32[]{:S(2)}) copy-start(f32[128,1408]{1,0:T(8,128)} %get-tuple-element.76) | copy-start | bytes 2162692
  220.0 73.3 %copy-start.10 = (f32[128,1408]{1,0:T(8,128)S(1)}, f32[128,1408]{1,0:T(8,128)}, u32[]{:S(2)}) copy-start(f32[128,1408]{1,0:T(8,128)} %get-tuple-element.77) | copy-start | bytes 2162692

commit v4 on v3

--- a/solution.py
+++ b/solution.py
@@ -242,114 +242,108 @@
     )(*shards)
 
 
-def scatter_kernel(plan, *refs):
-    count = len(plan)
-    arrays = 1 + max(source for source, _, _, _ in plan)
-    ins, outs = refs[:arrays], refs[arrays : arrays + count]
-    rest = refs[arrays + count :]
-    land1, sum1, land2, sum2, land3 = (rest[k * count : (k + 1) * count] for k in range(5))
-    send, recv = rest[5 * count :]
-    x, zl, y, zh, core = place()
-    across = at_sp(x, 1 - zl, y)
-    row = [(x + k) % 4 for k in (1, 2, 3)]
-    column = [(y + k) % 4 for k in (1, 2, 3)]
-    greet([at_sp(k, zl, y) for k in row] + [at_sp(x, zl, k) for k in column] + [across])
-    copies = {}
-
-    def push(n, slot, src, dst, target):
+class Scatter:
+    def __init__(self, plan, parts, buffers, send, recv, local):
+        self.plan, self.parts = plan, parts
+        self.land1, self.sum1, self.land2, self.sum2, self.land3 = buffers
+        self.send, self.recv, self.local = send, recv, local
+        self.x, self.zl, self.y, _, _ = place()
+        self.row = [(self.x + k) % 4 for k in (1, 2, 3)]
+        self.column = [(self.y + k) % 4 for k in (1, 2, 3)]
+        self.copies, self.own = {}, {}
+
+    def push(self, n, slot, src, dst, target):
         copy = pltpu.make_async_remote_copy(
             src_ref=src,
             dst_ref=dst,
-            send_sem=send.at[n, slot],
-            recv_sem=recv.at[n, slot],
+            send_sem=self.send.at[n, slot],
+            recv_sem=self.recv.at[n, slot],
             device_id=target,
             device_id_type=MESH,
         )
         copy.start()
-        copies[n, slot] = copy
-
-    def to_row(k):
-        return at_sp(row[k], zl, y)
-
-    def to_column(k):
-        return at_sp(x, zl, column[k])
-
-    for n, (source, first, width, x_first) in enumerate(plan):
-        view = ins[source].at[:, :, :, :, pl.ds(first, width)]
+        self.copies[n, slot] = copy
+
+    def to_row(self, k):
+        return at_sp(self.row[k], self.zl, self.y)
+
+    def to_column(self, k):
+        return at_sp(self.x, self.zl, self.column[k])
+
+    def start(self, n):
+        source, first, width, x_first = self.plan[n]
+        view = self.parts[source].at[:, :, :, :, pl.ds(first, width)]
+        own = view.at[self.x] if x_first else view.at[:, :, self.y]
+        self.own[n] = pltpu.make_async_copy(own, self.sum1[n], self.local.at[n])
+        self.own[n].start()
         for k in range(3):
             if x_first:
-                push(n, k, view.at[row[k]], land1[n].at[k], to_row(k))
+                self.push(n, k, view.at[self.row[k]], self.land1[n].at[k], self.to_row(k))
             else:
-                push(n, k, view.at[:, :, column[k]], land1[n].at[k], to_column(k))
-    for n, (source, first, width, x_first) in enumerate(plan):
+                self.push(n, k, view.at[:, :, self.column[k]], self.land1[n].at[k], self.to_column(k))
+
+    def second(self, n):
+        x_first = self.plan[n][3]
+        sums, land = self.sum1[n], self.land1[n]
+        self.own[n].wait()
         for k in range(3):
-            copies[n, k].wait_recv()
-        outer, inner = sum1[n].shape[0], sum1[n].shape[1]
+            self.copies[n, k].wait_recv()
+        outer, inner = sums.shape[:2]
 
         def add(t, carry):
             p, q = t // inner, t % inner
-            if x_first:
-                own = ins[source][x, p, q, :, pl.ds(first, width)]
-            else:
-                own = ins[source][p, q, y, :, pl.ds(first, width)]
-            total = own.astype(jnp.float32)
+            total = sums[p, q].astype(jnp.float32)
             for k in range(3):
-                total += land1[n][k, p, q].astype(jnp.float32)
-            sum1[n][p, q] = total.astype(jnp.bfloat16)
+                total += land[k, p, q].astype(jnp.float32)
+            sums[p, q] = total.astype(jnp.bfloat16)
             return carry
 
         lax.fori_loop(0, outer * inner, add, 0)
         for k in range(3):
             if x_first:
-                push(n, 3 + k, sum1[n].at[:, column[k]], land2[n].at[k], to_column(k))
+                self.push(
+                    n, 3 + k, sums.at[:, self.column[k]], self.land2[n].at[k], self.to_column(k)
+                )
             else:
-                push(n, 3 + k, sum1[n].at[row[k]], land2[n].at[k], to_row(k))
-    for n, (source, first, width, x_first) in enumerate(plan):
+                self.push(n, 3 + k, sums.at[self.row[k]], self.land2[n].at[k], self.to_row(k))
+
+    def third(self, n):
+        x_first = self.plan[n][3]
         for k in range(3):
-            copies[n, 3 + k].wait_recv()
+            self.copies[n, 3 + k].wait_recv()
         for p in range(2):
-            own = sum1[n][p, y] if x_first else sum1[n][x, p]
+            own = self.sum1[n][p, self.y] if x_first else self.sum1[n][self.x, p]
             total = own.astype(jnp.float32)
             for k in range(3):
-                total += land2[n][k, p].astype(jnp.float32)
-            sum2[n][p] = total.astype(jnp.bfloat16)
-        push(n, 6, sum2[n].at[1 - zl], land3[n], across)
-    for n in range(count):
-        copies[n, 6].wait_recv()
-        outs[n][...] = sum2[n][zl].astype(jnp.float32) + land3[n][...].astype(jnp.float32)
-    for copy in copies.values():
-        copy.wait_send()
-
-
-def scatter_sums(parts, plan):
-    count = len(plan)
-    rows = [parts[source].shape[3] for source, _, _, _ in plan]
-    widths = [width for _, _, width, _ in plan]
-
-    def buffers(*lead):
-        return [pltpu.VMEM((*lead, r, w), jnp.bfloat16) for r, w in zip(rows, widths)]
-
-    def by_order(first, second, lead=()):
+                total += self.land2[n][k, p].astype(jnp.float32)
+            self.sum2[n][p] = total.astype(jnp.bfloat16)
+        across = at_sp(self.x, 1 - self.zl, self.y)
+        self.push(n, 6, self.sum2[n].at[1 - self.zl], self.land3[n], across)
+
+    def finish(self, n, out):
+        self.copies[n, 6].wait_recv()
+        out[...] = self.sum2[n][self.zl].astype(jnp.float32) + self.land3[n][...].astype(
+            jnp.float32
+        )
+
+    def settle(self):
+        for copy in self.copies.values():
+            copy.wait_send()
+
+
+def scatter_buffers(plan, rows):
+    chunks = [(rows[source], width, order) for source, _, width, order in plan]
+
+    def ordered(*lead):
         return [
-            pltpu.VMEM((*lead, *(first if order else second), r, w), jnp.bfloat16)
-            for r, w, (_, _, _, order) in zip(rows, widths, plan)
+            pltpu.VMEM((*lead, *((2, 4) if order else (4, 2)), r, w), jnp.bfloat16)
+            for r, w, order in chunks
         ]
 
-    return pl.pallas_call(
-        functools.partial(scatter_kernel, plan),
-        out_shape=[jax.ShapeDtypeStruct((r, w), jnp.float32) for r, w in zip(rows, widths)],
-        in_specs=[pl.BlockSpec(memory_space=pltpu.VMEM)] * len(parts),
-        out_specs=[pl.BlockSpec(memory_space=pltpu.VMEM)] * count,
-        scratch_shapes=by_order((2, 4), (4, 2), (3,))
-        + by_order((2, 4), (4, 2))
-        + buffers(3, 2)
-        + buffers(2)
-        + buffers()
-        + [pltpu.SemaphoreType.DMA((count, 7)), pltpu.SemaphoreType.DMA((count, 7))],
-        compiler_params=pltpu.CompilerParams(
-            collective_id=1, has_side_effects=True, vmem_limit_bytes=48 * 2**20
-        ),
-    )(*parts)
+    def plain(*lead):
+        return [pltpu.VMEM((*lead, r, w), jnp.bfloat16) for r, w, _ in chunks]
+
+    return [ordered(3), ordered(), plain(3, 2), plain(2), plain()]
 
 
 TILE = 128
@@ -367,37 +361,50 @@
     return block.T[:HEAD_PAD].astype(jnp.bfloat16)
 
 
-def attention_kernel(
-    proj,
-    grad,
-    attn_out,
-    dqkv_out,
-    q_in,
-    g_in,
-    kv_in,
-    key_t,
-    value_t,
-    key,
-    value,
-    query,
-    cot,
-    query_t,
-    cot_t,
-    score,
-    weight,
-    inverse,
-    offset,
-    attended,
-    o_send,
-    dq_send,
-    d_send,
-    d_land,
-    d_sum,
-    o_land,
-    d_res,
-    send,
-    recv,
-):
+SUM_PLAN = [
+    (0, 0, 2 * DEC, True),
+    (0, 2 * DEC, 2 * DEC, False),
+    (1, 0, 9 * LAT, True),
+    (2, 0, LAT, True),
+    (3, 0, 1408, False),
+]
+OUT_ROWS = 22
+OUT_ROWS_STEP = 24
+
+
+def attention_kernel(proj, grad, d_x1, dec_part, conv_part, lat_part, *refs):
+    attn_out, dqkv_out, *sum_outs = refs[:7]
+    (
+        q_in,
+        g_in,
+        kv_in,
+        key_t,
+        value_t,
+        key,
+        value,
+        query,
+        cot,
+        query_t,
+        cot_t,
+        score,
+        weight,
+        inverse,
+        offset,
+        attended,
+        o_send,
+        dq_send,
+        d_send,
+        d_land,
+        d_sum,
+        o_land,
+        d_res,
+        out_part,
+    ) = refs[7:31]
+    groups = [refs[31 + 5 * k : 36 + 5 * k] for k in range(5)]
+    send, recv, sum_send, sum_recv, sum_local = refs[56:]
+    sums = Scatter(
+        SUM_PLAN, [dec_part, conv_part, lat_part, out_part], groups, sum_send, sum_recv, sum_local
+    )
     x, zl, y, zh, core = place()
     m = x * 2 + zl
     plane = [(m + k) % 8 for k in range(8)]
@@ -446,6 +453,8 @@
         pass_on(k)
     for k in range(1, 8):
         push(g_at + k, grad.at[plane[k]], g_in.at[m], at_plane(k))
+    for n in (0, 2, 3):
+        sums.start(n)
     zero_rows = jnp.zeros((TILE - HEAD_PAD, key_t.shape[1]), jnp.bfloat16)
     key_t[HEAD_PAD:] = zero_rows
     value_t[HEAD_PAD:] = zero_rows
@@ -477,6 +486,7 @@
             copies[ring_at + 3 * k + j - 1].wait_recv()
         first = ((y + 4 - j) % 4) * 8
         lax.fori_loop(first, first + 8, prepare, 0)
+    sums.start(1)
     for k in range(1, 8):
         copies[g_at + k].wait_recv()
     lax.fori_loop(0, 8, prepare_cots, 0)
@@ -550,6 +560,25 @@
         d_res[kind + 1, m] = d_sum[kind, m]
 
     key_side(cot_t, 1)
+    for k in range(1, 8):
+        copies[o_at + k].wait_recv()
+    attn_out[...] = o_land[...]
+    spread = 4 * OUT_ROWS_STEP
+    r = lax.broadcasted_iota(jnp.int32, (spread, HEAD_PAD), 0)
+    c = lax.broadcasted_iota(jnp.int32, (spread, HEAD_PAD), 1)
+    picked = c < 0
+    for k in range(4):
+        low, first = k * OUT_ROWS, k * OUT_ROWS_STEP
+        picked |= (c - low == r - first) & (c >= low) & (c < low + OUT_ROWS) & (r >= first)
+    pick = jnp.where(picked, 1.0, 0.0).astype(jnp.bfloat16)
+    for t in range(8):
+        rows = jnp.dot(pick, o_land[t], preferred_element_type=jnp.float32).astype(jnp.bfloat16)
+        term = jnp.dot(rows, d_x1[...], preferred_element_type=jnp.float32) * grad_scale
+        for k in range(4):
+            out_part[t // 2, t % 2, k] = term[
+                k * OUT_ROWS_STEP : (k + 1) * OUT_ROWS_STEP
+            ].astype(jnp.bfloat16)
+    sums.start(4)
 
     def backward(i, carry):
         at = pl.ds(pl.multiple_of(i * QUERY_BLOCK, QUERY_BLOCK), QUERY_BLOCK)
@@ -570,20 +599,27 @@
     for k in range(1, 8):
         push(dq_at + k, dq_send.at[plane[k]], d_res.at[0, m], at_plane(k))
     d_res[0, m] = dq_send[m]
+    for n in (0, 1, 2, 3):
+        sums.second(n)
     key_home(1)
     key_home(0)
-    for k in range(1, 8):
-        copies[o_at + k].wait_recv()
-    attn_out[...] = o_land[...]
+    sums.second(4)
+    for n in range(5):
+        sums.third(n)
     for first in (dq_at, home_at, home_at + 8):
         for k in range(1, 8):
             copies[first + k].wait_recv()
     dqkv_out[...] = d_res[...]
+    for n in range(5):
+        sums.finish(n, sum_outs[n])
     for copy in copies.values():
         copy.wait_send()
-
-
-def attend_both_ways(proj, grad):
+    sums.settle()
+
+
+def attend_both_ways(proj, grad, d_x1, dec_part, conv_part, lat_part):
+    rows = [part.shape[3] for part in (dec_part, conv_part, lat_part)] + [OUT_ROWS_STEP]
+    groups = scatter_buffers(SUM_PLAN, rows)
     heads = grad.shape[0]
     tokens, queries = 32 * TILE, 8 * TILE
     bf16, f32 = jnp.bfloat16, jnp.float32
@@ -612,21 +648,27 @@
         ((2, 8, *block), bf16),
         ((8, *block), bf16),
         ((3, 8, *block), bf16),
+        ((4, 2, 4, OUT_ROWS_STEP, d_x1.shape[1]), bf16),
     ]
+    sum_sems = pltpu.SemaphoreType.DMA((len(SUM_PLAN), 7))
     return pl.pallas_call(
         attention_kernel,
         out_shape=[
             jax.ShapeDtypeStruct((heads, *block), bf16),
             jax.ShapeDtypeStruct((3, heads, *block), bf16),
-        ],
-        in_specs=[pl.BlockSpec(memory_space=pltpu.VMEM)] * 2,
-        out_specs=[pl.BlockSpec(memory_space=pltpu.VMEM)] * 2,
+        ]
+        + [jax.ShapeDtypeStruct((rows[source], width), f32) for source, _, width, _ in SUM_PLAN],
+        in_specs=[pl.BlockSpec(memory_space=pltpu.VMEM)] * 3
+        + [pl.BlockSpec(memory_space=pl.ANY)] * 3,
+        out_specs=[pl.BlockSpec(memory_space=pltpu.VMEM)] * 7,
         scratch_shapes=[pltpu.VMEM(shape, kind) for shape, kind in shapes]
-        + [pltpu.SemaphoreType.DMA((88,)), pltpu.SemaphoreType.DMA((88,))],
+        + [buffer for group in groups for buffer in group]
+        + [pltpu.SemaphoreType.DMA((88,)), pltpu.SemaphoreType.DMA((88,))]
+        + [sum_sems, sum_sems, pltpu.SemaphoreType.DMA((len(SUM_PLAN),))],
         compiler_params=pltpu.CompilerParams(
             collective_id=2, has_side_effects=True, vmem_limit_bytes=56 * 2**20
         ),
-    )(proj, grad)
+    )(proj, grad, d_x1, dec_part, conv_part, lat_part)
 
 
 def per_device(
@@ -728,13 +770,19 @@
     dattn = lax.dot_general(
         out_full, d_x1, (((1,), (1,)), ((), ())), preferred_element_type=jnp.float32
     ).astype(jnp.bfloat16)
-    projected = lax.dot_general(
-        qkv_full, normalized_rows, (((0,), (1,)), ((), ())), preferred_element_type=jnp.float32
-    ).reshape(3, HEADS, HEAD_PAD, tokens_here)
+    projected = lax.optimization_barrier(
+        jnp.dot(normalized_rows, qkv_full, preferred_element_type=jnp.float32)
+    )
+    projected = projected.T.reshape(3, HEADS, HEAD_PAD, tokens_here)
     scales = jnp.array([score_scale, 1.0, 1.0], jnp.float32).reshape(3, 1, 1, 1)
     projected = (projected * scales).astype(jnp.bfloat16)
-    attn_heads, dqkv = attend_both_ways(
-        projected, dattn.reshape(HEADS, HEAD_PAD, tokens_here)
+    attn_heads, dqkv, dec_low, dec_high, conv_rows, lat_sums, out_rows = attend_both_ways(
+        projected,
+        dattn.reshape(HEADS, HEAD_PAD, tokens_here),
+        d_x1,
+        dec_part,
+        conv_part,
+        lat_part,
     )
     mixed = lax.dot_general(
         attn_heads.reshape(HEADS * HEAD_PAD, tokens_here),
@@ -743,14 +791,6 @@
         preferred_element_type=jnp.float32,
     )
     x_one = (y_one.astype(jnp.float32) - mixed).astype(jnp.bfloat16)
-    attn_band = attn_heads[:, :HEAD]
-    spread_attn = jnp.pad(
-        attn_band.reshape(devices, out_depth, tokens_here), ((0, 0), (0, 24 - out_depth), (0, 0))
-    ).reshape(devices * 24, tokens_here)
-    out_product = lax.dot_general(
-        spread_attn, d_x1, (((1,), (0,)), ((), ())), preferred_element_type=jnp.float32
-    )
-    out_part = (out_product * grad_scale).astype(jnp.bfloat16).reshape(4, 2, 4, 24, -1)
     normalized_gradient = lax.dot_general(
         dqkv.reshape(3 * HEADS * HEAD_PAD, tokens_here),
         qkv_full, (((0,), (1,)), ((), ())), preferred_element_type=jnp.float32
@@ -761,17 +801,6 @@
             normalized_gradient * layer_norm_gain, standardized_input, inverse_deviation
         )
     ).astype(jnp.bfloat16)
-    half = 2 * DEC
-    dec_low, out_rows, dec_high, conv_rows, lat_sums = scatter_sums(
-        [dec_part, out_part, conv_part, lat_part],
-        [
-            (0, 0, half, True),
-            (1, 0, out_part.shape[4], False),
-            (0, half, half, True),
-            (2, 0, 9 * LAT, False),
-            (3, 0, LAT, False),
-        ],
-    )
     g_deconv = jnp.concatenate([dec_low[:depth], dec_high[:depth]], axis=1)
     g_out = out_rows[:out_depth]
     g_lateral = lat_sums[:lat_rows]

time: 301 us -> 297 us (0.987)
  Pallas kernels: 198 us -> 171 us
  other arithmetic: 6.84 us -> 19.4 us
  local copies, waits for them, and re-layouts: 41.2 us -> 52 us
    pallas_call x1 -> x0, Pallas kernels: 72.6 us -> none  [scatter_sums(): pl.pallas_call(functools.partial(scatter_kernel, plan), out_shape=[jax.Sh...]
    pallas_call x1, Pallas kernels: 70.6 us -> 116 us  [attend_both_ways(): pl.pallas_call(attention_kernel, out_shape=[jax.ShapeDtypeStruct((heads,...]
    dot_general x1 -> x0, local copies, waits for them, and re-layouts: 9.72 us -> none  [per_device(): lax.dot_general(qkv_full, normalized_rows, (((0,), (1,)), ((), ())), pref...]
    reshape x2, local copies, waits for them, and re-layouts: 0.36 us -> 3.87 us  [per_device(): upsampled.reshape(rows_here, GRID_W, 2, 2, DEC).transpose(0, 2, 1, 3, 4)]
    reshape x2, local copies, waits for them, and re-layouts: 0.42 us -> 3.92 us  [per_device(): dpixels.reshape(rows_here, 2, GRID_W, 2, DEC).transpose(0, 2, 1, 3, 4)]
    dot_general x2 -> x1, matrix products: 7.34 us -> 5.09 us  [per_device(): jnp.dot(normalized_rows, qkv_full, preferred_element_type=jnp.float32)]
    unnamed x71 -> x93, local copies, waits for them, and re-layouts: 12.6 us -> 13.1 us
  transfers between devices with their start and end apart: 4 -> 4, of which waited for: 0 -> 0; matrix products, arithmetic and copies ran while one was open for 9% -> 11% of each run, Pallas kernels for 0% -> 0%
where the time goes in v4:
time: 297 us; the launch traced here: 292 us
  Pallas kernels  171 us (58%)
  local copies, waits for them, and re-layouts  52 us (18%)
  matrix products  37.2 us (13%)
  other arithmetic  19.4 us (7%)
  starting transfers between devices  11.4 us (4%)
    pallas_call x1, Pallas kernels, attend_both_ways(): pl.pallas_call(attention_kernel, out_shape=[jax.ShapeDtypeStruct((heads,...  116 us
    pallas_call x1, Pallas kernels, gather_weights(): pl.pallas_call(functools.partial(gather_kernel, shapes), out_shape=[jax.S...  54.2 us
    unnamed x93, local copies, waits for them, and re-layouts  13.1 us
    conv_general_dilated x2, matrix products, conv_valid(): lax.conv_general_dilated(padded[None], kernel, (1, 1), 'VALID', dimension...  10 us
    convert_element_type x2, local copies, waits for them, and re-layouts, per_device(): (conv_product.reshape(4, 2, 4, LAT // devices, 9 * LAT) * grad_scale).ast...  8.15 us
    ppermute x2, starting transfers between devices, shifted_2(): return lax.ppermute(array, axis, pairs)  6.45 us
  transfers between devices with their start and end apart: 4, of which 0 were waited for; matrix products, arithmetic and copies ran while one was open for 11% of the time, Pallas kernels for 0%

profile of v4, /device:TPU:64, one launch (start us, length us, event | category | flops | bytes accessed | tf_op | source)
XLA Modules:
  0.0 292.2 jit_solution(11177252697491584725)
XLA Ops:
  0.7 1.2 convert_reduce_fusion
  1.9 1.5 pad.34.refs_2_
  3.5 1.6 pad.32.refs_0_
  5.0 1.3 reshape.235
  10.9 54.2 %shard_map.171 = (bf16[8,176,1536]{2,1,0:T(8,128)(2,1)S(1)}, bf16[8,176,2304]{2,1,0:T(8,128)(2,1)S(1)}, bf16[8,96,1536]{2,1,0:T(8,128)(2,1)S(1)}) custom-call(bf16[48,1536]{1,0:T(8,128)(2,1)S(1)} %copy-done.5, bf16[48,2304]{1,0:T(8,128)(2,1)S(1)} %copy-done.4, bf16[32,1536]{1,0:T(8,128)(2,1)S(1)} %copy-done.6), custom_call_target="tpu_custom_call" | custom-call | tf_op jit(solution)/shard_map/pallas_call | solution.py:225
  65.0 2.7 copy-done.1
  67.7 2.1 copy-done.2
  69.8 1.5 convolution_convert_fusion
  71.4 1.9 reshape.241
  73.2 2.0 copy.73
  75.2 1.9 reshape.242
  77.1 1.5 fusion.46
  81.7 3.1 %collective-permute-start = (bf16[1,128,256]{2,1,0:T(8,128)(2,1)}, bf16[1,128,256]{2,1,0:T(8,128)(2,1)}, u32[]{:S(2)}, u32[]{:S(2)}) collective-permute-start(bf16[1,128,256]{2,1,0:T(8,128)(2,1)} %get-tuple-element.67), channel_id=1, source_target_pairs={{0,1},{1,2},{2,3},{3,4},{4,5},{5,6},{6,7},{7,8},{8,9},{9,10},{10,1... | collective-permute-start | bytes 196616 | tf_op jit(solution)/shard_map/ppermute | solution.py:26
  84.8 1.8 collective-permute-start.1
  87.3 5.1 %fusion.35 = f32[128,2304]{1,0:T(8,128)} fusion(bf16[1408,2304]{1,0:T(8,128)(2,1)} %bitcast.125, bf16[128,1408]{1,0:T(8,128)(2,1)S(1)} %copy-done.11, f32[1408]{0:T(1024)S(1)} %copy-done.30, f32[128]{0:T(128)S(1)} %add_rsqrt_fusion.2, f32[128]{0:T(128)} %copy-done.33), kind=kOutput, calls=%fused_computation.63 | convolution fusion | flops 831373312 | bytes 8034816 | tf_op jit(solution)/shard_map/dot_general | solution.py:774
  92.4 2.7 copy.35
  95.0 2.3 multiply_convert_fusion.1.proj
  97.3 1.9 copy.40
  99.2 1.8 reshape.250
  101.0 1.8 pad.37
  102.8 1.1 fusion.71
  103.9 4.5 %fusion.47 = (f32[4,128]{1,0:T(4,128)S(1)}, f32[1,4,128,256]{3,0,2,1:T(1,128)S(1)}) fusion(bf16[3,3,256,256]{3,2,1,0:T(8,128)(2,1)S(1)} %copy-done, bf16[1,6,130,256]{3,2,1,0:T(8,128)(2,1)S(1)} %fusion.71), kind=kOutput, calls=%fused_computation.104 | convolution fusion | flops 604110336 | bytes 2105344 | tf_op jit(solution)/shard_map/conv_general_dilated | solution.py:53
  109.6 5.5 %fusion.48 = (bf16[1,6,128,256]{3,0,2,1:T(2,128)(2,1)S(1)}, f32[1,6,128,256]{3,0,2,1:T(1,128)S(1)}) fusion(bf16[3,3,256,256]{3,2,1,0:T(8,128)(2,1)S(1)} %copy-done, bf16[1,8,130,256]{3,2,1,0:T(8,128)(2,1)S(1)} %pad_bitcast_fusion), kind=kOutput, calls=%fused_computation.105 | convolution fusion | flops 906166272 | bytes 2891776 | tf_op jit(solution)/shard_map/conv_general_dilated | solution.py:53
  116.6 5.2 %collective-permute-start.2 = (bf16[128,256]{1,0:T(8,128)(2,1)}, bf16[128,256]{1,0:T(8,128)(2,1)}, u32[]{:S(2)}, u32[]{:S(2)}) collective-permute-start(bf16[128,256]{1,0:T(8,128)(2,1)} %bitcast.112), channel_id=1, source_target_pairs={{0,1},{1,2},{2,3},{3,4},{4,5},{5,6},{6,7},{7,8},{8,9},{9,10},{10,1... | collective-permute-start | bytes 196616 | tf_op jit(solution)/shard_map/ppermute | solution.py:37
  121.8 1.3 collective-permute-start.3
  123.1 1.0 fusion.34
  125.7 1.8 fusion.5
  129.4 4.4 %copy.42 = bf16[256,9,256]{2,1,0:T(8,128)(2,1)} copy(bf16[256,9,256]{0,2,1:T(8,128)(2,1)} %fusion.5) | data formatting | bytes 2359296 | tf_op jit(solution)/shard_map/convert_element_type | solution.py:747
  133.8 3.7 %convert_element_type.105.conv_part = bf16[4,2,4,8,2304]{4,3,2,1,0:T(8,128)(2,1)} reshape(bf16[256,9,256]{2,1,0:T(8,128)(2,1)} %copy.42) | data formatting | bytes 2359296 | tf_op jit(solution)/shard_map/convert_element_type | solution.py:747
  137.6 1.7 fusion.42
  139.2 1.6 fusion.40
  140.8 1.5 multiply_reduce_fusion
  142.3 1.2 multiply_reduce_fusion.1
  143.5 1.4 multiply_convert_fusion.2
  144.9 1.0 fusion.9
  145.9 1.1 convolution_convert_fusion.1
  147.0 1.7 reshape.254
  148.7 1.7 pad.38
  150.4 1.9 reshape.247
  152.2 2.0 copy.72
  154.3 2.0 reshape.248
  156.3 4.8 %fusion.49 = (bf16[128,1408]{1,0:T(8,128)(2,1)S(1)}, f32[128,1408]{1,0:T(8,128)}) fusion(bf16[128,1536]{1,0:T(8,128)(2,1)} %reshape.248, bf16[1408,1536]{1,0:T(8,128)(2,1)} %bitcast.130), kind=kOutput, calls=%fused_computation.106 | convolution fusion | flops 554008576 | bytes 5799936 | tf_op jit(solution)/shard_map/dot_general | solution.py:766
  161.1 3.6 %fusion = bf16[1536,1536]{1,0:T(8,128)(2,1)} fusion(bf16[128,1536]{0,1:T(8,128)(2,1)S(1)} %bitcast.140, bf16[128,1536]{1,0:T(8,128)(2,1)S(1)} %copy-done.15), kind=kOutput, calls=%fused_computation.1 | convolution fusion | flops 608698368 | bytes 5505024 | tf_op jit(solution)/shard_map/dot_general | solution.py:65
  164.7 1.4 fusion.6
  166.1 116.5 %shard_map.172 = (bf16[8,96,128]{2,1,0:T(8,128)(2,1)}, bf16[3,8,96,128]{3,2,1,0:T(8,128)(2,1)}, f32[48,768]{1,0:T(8,128)}, f32[48,768]{1,0:T(8,128)}, f32[8,2304...) custom-call(bf16[3,8,96,128]{3,2,1,0:T(8,128)(2,1)} %multiply_convert_fusion.1.proj, ...), custom_call_target="tpu_custom_call" | custom-call | tf_op jit(solution)/shard_map/pallas_call | solution.py:654
  282.6 3.0 %fusion.1 = bf16[128,1408]{1,0:T(8,128)(2,1)} fusion(bf16[768,128]{1,0:T(8,128)(2,1)} %bitcast.154, bf16[768,1536]{1,0:T(8,128)(2,1)} %bitcast.132, bf16[128,1408]{1,0:T(8,128)(2,1)S(1)} %copy-done.22), kind=kOutput, calls=%fused_computation.6 | convolution fusion | flops 277364736 | bytes 3080192 | tf_op jit(solution)/shard_map/dot_general | solution.py:787
  285.7 2.4 fusion.43
  288.9 1.1 fusion.25
  (125 shorter events, 17.0 us)
Async XLA Ops:
  0.6 103.3 %copy-start = (bf16[3,3,256,256]{3,2,1,0:T(8,128)(2,1)S(1)}, bf16[3,3,256,256]{3,2,1,0:T(8,128)(2,1)}, u32[]{:S(2)}) copy-start(bf16[3,3,256,256]{3,2,1,0:T(8,128)(2,1)} %param.25) | copy-start | bytes 3538948
  0.6 6.7 %copy-start.10 = (bf16[128,1408]{1,0:T(8,128)(2,1)S(1)}, bf16[128,1408]{1,0:T(8,128)(2,1)}, u32[]{:S(2)}) copy-start(bf16[128,1408]{1,0:T(8,128)(2,1)} %param.17) | copy-start | bytes 1081348
  0.7 6.7 %copy-start.21 = (bf16[128,1408]{1,0:T(8,128)(2,1)S(1)}, bf16[128,1408]{1,0:T(8,128)(2,1)}, u32[]{:S(2)}) copy-start(bf16[128,1408]{1,0:T(8,128)(2,1)} %param.16) | copy-start | bytes 1081348
  1.9 5.4 %copy-start.33 = (f32[128]{0:T(128)}, f32[128]{0:T(128)S(1)}, u32[]{:S(2)}) copy-start(f32[128]{0:T(128)S(1)} %broadcast_multiply_fusion.7) | copy-start | bytes 1540
  8.1 0.9 copy-start.4
  9.1 0.9 copy-start.5
  10.0 0.9 copy-start.6
  10.9 56.9 %copy-start.16 = (bf16[128,1408]{1,0:T(8,128)(2,1)}, bf16[128,1408]{1,0:T(8,128)(2,1)S(1)}, u32[]{:S(2)}) copy-start(bf16[128,1408]{1,0:T(8,128)(2,1)S(1)} %get-tuple-element.63) | copy-start | bytes 1081348
  65.0 2.7 copy-start.1
  67.7 2.1 copy-start.2
  67.7 97.0 %copy-start.3 = (bf16[8,96,1536]{2,1,0:T(8,128)(2,1)}, bf16[8,96,1536]{2,1,0:T(8,128)(2,1)S(1)}, u32[]{:S(2)}) copy-start(bf16[8,96,1536]{2,1,0:T(8,128)(2,1)S(1)} %get-tuple-element.42) | copy-start | bytes 7077892
  71.4 15.9 %copy-start.30 = (f32[1408]{0:T(1024)S(1)}, f32[1408]{0:T(1024)}, u32[]{:S(2)}) copy-start(f32[1408]{0:T(1024)} %param.19) | copy-start | bytes 16900
  77.1 10.2 %copy-start.11 = (bf16[128,1408]{1,0:T(8,128)(2,1)S(1)}, bf16[128,1408]{1,0:T(8,128)(2,1)}, u32[]{:S(2)}) copy-start(bf16[128,1408]{1,0:T(8,128)(2,1)} %param.17) | copy-start | bytes 1081348
  78.6 0.8 copy-start.7
  80.3 0.7 copy-start.13
  81.7 21.1 %collective-permute-start = (bf16[1,128,256]{2,1,0:T(8,128)(2,1)}, bf16[1,128,256]{2,1,0:T(8,128)(2,1)}, u32[]{:S(2)}, u32[]{:S(2)}) collective-permute-start(bf16[1,128,256]{2,1,0:T(8,128)(2,1)} %get-tuple-element.67), channel_id=1, source_target_pairs={{0,1},{1,2},{2,3},{3,4},{4,5},{5,6},{6,7},{7,8},{8,9},{9,10},{10,1... | collective-permute-start | bytes 196616 | tf_op jit(solution)/shard_map/ppermute | solution.py:26
  84.8 18.0 %collective-permute-start.1 = (bf16[1,128,256]{2,1,0:T(8,128)(2,1)}, bf16[1,128,256]{2,1,0:T(8,128)(2,1)}, u32[]{:S(2)}, u32[]{:S(2)}) collective-permute-start(bf16[1,128,256]{2,1,0:T(8,128)(2,1)} %get-tuple-element.68), channel_id=1, source_target_pairs={{1,0},{2,1},{3,2},{4,3},{5,4},{6,5},{7,6},{8,7},{9,8},{10,9},{11,1... | collective-permute-start | bytes 196616 | tf_op jit(solution)/shard_map/ppermute | solution.py:29
  87.3 5.1 %copy-start.35 = (f32[128]{0:T(128)}, f32[128]{0:T(128)S(1)}, u32[]{:S(2)}) copy-start(f32[128]{0:T(128)S(1)} %add_rsqrt_fusion.2) | copy-start | bytes 1540
  103.9 4.8 %copy-start.23 = (bf16[4,128,256]{2,1,0:T(8,128)(2,1)S(1)}, bf16[4,128,256]{2,1,0:T(8,128)(2,1)}, u32[]{:S(2)}) copy-start(bf16[4,128,256]{2,1,0:T(8,128)(2,1)} %param.18) | copy-start | bytes 786436
  103.9 4.8 %copy-start.37 = (f32[256]{0:T(256)S(1)}, f32[256]{0:T(256)}, u32[]{:S(2)}) copy-start(f32[256]{0:T(256)} %param.26) | copy-start | bytes 3076
  109.6 13.5 %copy-start.14 = (bf16[512,256]{1,0:T(8,128)(2,1)S(1)}, bf16[512,256]{1,0:T(8,128)(2,1)}, u32[]{:S(2)}) copy-start(bf16[512,256]{1,0:T(8,128)(2,1)} %copy-done.13) | copy-start | bytes 786436
  116.6 20.9 %collective-permute-start.2 = (bf16[128,256]{1,0:T(8,128)(2,1)}, bf16[128,256]{1,0:T(8,128)(2,1)}, u32[]{:S(2)}, u32[]{:S(2)}) collective-permute-start(bf16[128,256]{1,0:T(8,128)(2,1)} %bitcast.112), channel_id=1, source_target_pairs={{0,1},{1,2},{2,3},{3,4},{4,5},{5,6},{6,7},{7,8},{8,9},{9,10},{10,1... | collective-permute-start | bytes 196616 | tf_op jit(solution)/shard_map/ppermute | solution.py:37
  121.8 17.4 %collective-permute-start.3 = (bf16[128,256]{1,0:T(8,128)(2,1)}, bf16[128,256]{1,0:T(8,128)(2,1)}, u32[]{:S(2)}, u32[]{:S(2)}) collective-permute-start(bf16[128,256]{1,0:T(8,128)(2,1)} %bitcast.111), channel_id=1, source_target_pairs={{1,0},{2,1},{3,2},{4,3},{5,4},{6,5},{7,6},{8,7},{9,8},{10,9},{11,1... | collective-permute-start | bytes 196616 | tf_op jit(solution)/shard_map/ppermute | solution.py:37
  124.1 1.3 copy-start.8
  124.1 1.3 copy-start.31
  137.6 6.0 %copy-start.9 = (f32[512,256]{1,0:T(8,128)S(1)}, f32[512,256]{1,0:T(8,128)}, u32[]{:S(2)}) copy-start(f32[512,256]{1,0:T(8,128)} %copy-done.7) | copy-start | bytes 1572868
  137.6 7.4 %copy-start.19 = (bf16[512,384]{1,0:T(8,128)(2,1)S(1)}, bf16[512,384]{1,0:T(8,128)(2,1)}, u32[]{:S(2)}) copy-start(bf16[512,384]{1,0:T(8,128)(2,1)} %reshape.242) | copy-start | bytes 1179652
  137.6 8.4 %copy-start.24 = (bf16[384,256]{1,0:T(8,128)(2,1)S(1)}, bf16[384,256]{1,0:T(8,128)(2,1)}, u32[]{:S(2)}) copy-start(bf16[384,256]{1,0:T(8,128)(2,1)} %param.23) | copy-start | bytes 589828
  156.3 4.8 %copy-start.15 = (bf16[128,1536]{1,0:T(8,128)(2,1)S(1)}, bf16[128,1536]{1,0:T(8,128)(2,1)}, u32[]{:S(2)}) copy-start(bf16[128,1536]{1,0:T(8,128)(2,1)} %reshape.248) | copy-start | bytes 1179652
  156.3 4.8 %copy-start.18 = (bf16[128,32,48]{0,2,1:T(8,128)(2,1)S(1)}, bf16[128,32,48]{0,2,1:T(8,128)(2,1)}, u32[]{:S(2)}) copy-start(bf16[128,32,48]{0,2,1:T(8,128)(2,1)} %pad.37) | copy-start | bytes 1179652
  161.1 3.6 %copy-start.20 = (bf16[128,1408]{1,0:T(8,128)(2,1)}, bf16[128,1408]{1,0:T(8,128)(2,1)S(1)}, u32[]{:S(2)}) copy-start(bf16[128,1408]{1,0:T(8,128)(2,1)S(1)} %get-tuple-element.88.d_x1) | copy-start | bytes 1081348
  164.7 121.0 %slice-start = ((s8[6488064]{0:T(1024)(128)(4,1)}), s8[4194304]{0:T(1024)(128)(4,1)S(1)}, s32[]{:S(2)}) async-start(s8[6488064]{0:T(1024)(128)(4,1)} %bitcast.126), calls=%async_computation | async-start | bytes 8388608
  166.1 116.5 %copy-start.22 = (bf16[128,1408]{1,0:T(8,128)(2,1)S(1)}, bf16[128,1408]{1,0:T(8,128)(2,1)}, u32[]{:S(2)}) copy-start(bf16[128,1408]{1,0:T(8,128)(2,1)} %param.16) | copy-start | bytes 1081348
  166.1 119.6 %slice-start.1 = ((s8[6488064]{0:T(1024)(128)(4,1)}), s8[2293760]{0:T(1024)(128)(4,1)S(1)}, s32[]{:S(2)}) async-start(s8[6488064]{0:T(1024)(128)(4,1)} %bitcast.126), calls=%async_computation.1 | async-start | bytes 4587520
  282.6 3.1 %copy-start.12 = (bf16[128,1408]{1,0:T(8,128)(2,1)S(1)}, bf16[128,1408]{1,0:T(8,128)(2,1)}, u32[]{:S(2)}) copy-start(bf16[128,1408]{1,0:T(8,128)(2,1)} %param.17) | copy-start | bytes 1081348
  282.6 3.1 %copy-start.25 = (bf16[3,8,96,128]{3,2,1,0:T(8,128)(2,1)S(1)}, bf16[3,8,96,128]{3,2,1,0:T(8,128)(2,1)}, u32[]{:S(2)}) copy-start(bf16[3,8,96,128]{3,2,1,0:T(8,128)(2,1)} %get-tuple-element.45) | copy-start | bytes 1769476
  282.6 3.1 %copy-start.34 = (f32[128]{0:T(128)S(1)}, f32[128]{0:T(128)}, u32[]{:S(2)}) copy-start(f32[128]{0:T(128)} %copy-done.33) | copy-start | bytes 1540
  282.6 3.1 %copy-start.36 = (f32[128]{0:T(128)S(1)}, f32[128]{0:T(128)}, u32[]{:S(2)}) copy-start(f32[128]{0:T(128)} %copy-done.35) | copy-start | bytes 1540
  285.7 2.5 copy-start.26
  285.7 2.5 copy-start.27
  285.7 3.2 %copy-start.17 = (f32[128,1408]{1,0:T(8,128)S(1)}, f32[128,1408]{1,0:T(8,128)}, u32[]{:S(2)}) copy-start(f32[128,1408]{1,0:T(8,128)} %get-tuple-element.76) | copy-start | bytes 2162692
  288.1 1.9 copy-start.28
  288.1 2.5 copy-start.32
  288.1 3.1 %copy-start.29 = (f32[8,2304]{1,0:T(8,128)S(1)}, f32[8,2304]{1,0:T(8,128)}, u32[]{:S(2)}) copy-start(f32[8,2304]{1,0:T(8,128)} %get-tuple-element.50) | copy-start | bytes 221188

commit v5 on v4

--- a/solution.py
+++ b/solution.py
@@ -18,25 +18,6 @@
 grad_scale = 0.015625
 
 
-def padded_2(block, sides, width):
-    for axis, dim in sides:
-        count = lax.axis_size(axis)
-        forward = [(i, i + 1) for i in range(count - 1)]
-        backward = [(target, source) for source, target in forward]
-        low = lax.ppermute(
-            lax.slice_in_dim(block, block.shape[dim] - width, None, axis=dim), axis, forward
-        )
-        high = lax.ppermute(lax.slice_in_dim(block, 0, width, axis=dim), axis, backward)
-        block = jnp.concatenate([low, block, high], axis=dim)
-    return block
-
-
-def shifted_2(array, axis, by):
-    count = lax.axis_size(axis)
-    pairs = [(i, i + by) for i in range(count) if 0 <= i + by < count]
-    return lax.ppermute(array, axis, pairs)
-
-
 def apply_layer_norm(values):
     centered = values - jnp.mean(values, axis=-1, keepdims=True)
     inverse = lax.rsqrt(jnp.mean(centered * centered, axis=-1, keepdims=True) + epsilon)
@@ -47,25 +28,6 @@
     first = jnp.mean(upstream, axis=-1, keepdims=True)
     second = jnp.mean(upstream * normalized_rows, axis=-1, keepdims=True)
     return inverse * (upstream - first - normalized_rows * second)
-
-
-def conv_valid(padded, kernel):
-    result = lax.conv_general_dilated(
-        padded[None],
-        kernel,
-        (1, 1),
-        "VALID",
-        dimension_numbers=("NHWC", "HWIO", "NHWC"),
-        preferred_element_type=jnp.float32,
-    )
-    return result[0]
-
-
-def rounded_part(left, right):
-    product = lax.dot_general(
-        left, right, (((0,), (0,)), ((), ())), preferred_element_type=jnp.float32
-    )
-    return (product * grad_scale).astype(jnp.bfloat16)
 
 
 MESH = pl.DeviceIdType.MESH
@@ -91,11 +53,28 @@
     pl.semaphore_wait(barrier, len(targets))
 
 
+def one_hot(rows, per, block):
+    r = lax.broadcasted_iota(jnp.int32, (block, 4 * rows), 0)
+    c = lax.broadcasted_iota(jnp.int32, (block, 4 * rows), 1)
+    skipped = jnp.zeros_like(r)
+    for k in (1, 2, 3):
+        skipped += jnp.where(r >= k * per, rows - per, 0)
+    return jnp.where(c == r + skipped, 1.0, 0.0)
+
+
 def gather_kernel(shapes, *refs):
     count = len(shapes)
-    ins, outs, shards, packs = (refs[k * count : (k + 1) * count] for k in range(4))
-    send, recv, local = refs[4 * count :]
+    ins = refs[:3]
+    y_one, second, cot, w_lateral, lat_gain, w_conv, conv_gain = refs[3:10]
+    qkv_out, w_out_out, half_out, d_x1_out, dec_out, conv_out, lat_out = refs[10:17]
+    deconv, *rest = refs[17:]
+    outs = [deconv, qkv_out, w_out_out]
+    shards, packs, rest = rest[:3], rest[3:6], rest[6:]
+    feature, pixels, act, dconv, cot_low, cot_high, norm_lat, dup, *sems = rest
+    send, recv, local, halo_send, halo_recv = sems
     x, zl, y, zh, core = place()
+    s = lax.axis_index("sp")
+    below, above = {"sp": (s + 1) % 32}, {"sp": (s + 31) % 32}
     xm, xp, xo = (x + 3) % 4, (x + 1) % 4, (x + 2) % 4
     left, right = at_sp(xm, zl, y), at_sp(xp, zl, y)
     across = (x * 2 + 1 - zl) * 4 + y
@@ -103,7 +82,7 @@
     down = {"img": ((zh + zl + 3) % 4) * 2 + core, "sp": across}
     twin = {"img": zh * 2 + 1 - core}
     column = [at_sp(x, zl, (y + k) % 4) for k in (1, 2, 3)]
-    greet(column + [left, right, up, down, twin])
+    greet(column + [left, right, up, down, twin, below, above])
     copies = {}
 
     def push(a, slot, src, dst, target):
@@ -144,12 +123,7 @@
         high = block - low
         for k in range(3):
             copies[a, k].wait_recv()
-        r = lax.broadcasted_iota(jnp.int32, (block, 4 * rows), 0)
-        c = lax.broadcasted_iota(jnp.int32, (block, 4 * rows), 1)
-        skipped = jnp.zeros_like(r)
-        for k in (1, 2, 3):
-            skipped += jnp.where(r >= k * per, rows - per, 0)
-        pick = jnp.where(c == r + skipped, 1.0, 0.0).astype(jnp.bfloat16)
+        pick = one_hot(rows, per, block).astype(jnp.bfloat16)
         packs[a][...] = jnp.dot(
             pick, shards[a][...].reshape(4 * rows, half), preferred_element_type=jnp.float32
         ).astype(jnp.bfloat16)
@@ -199,47 +173,237 @@
             copies[a, 8 + 2 * n].wait_recv()
             forward(a, 21 + 2 * n, bx, 1 - zl, low, high, twin)
 
-    for step in range(count + 2):
-        if step < count:
-            near(step)
-        if 0 <= step - 1 < count:
-            far(step - 1)
-        if 0 <= step - 2 < count:
-            deep(step - 2)
-    for a in range(count):
+    def twins(a):
         for slot in range(15, 28):
             copies[a, slot].wait_recv()
-    for keep in keeps:
+
+    row = GRID_W
+    inner_rows = 4 * row
+    halos = {}
+
+    def swap_edges(ref, first):
+        ends = (
+            (first, pl.ds(inner_rows, row), pl.ds(0, row), below),
+            (first + 1, pl.ds(row, row), pl.ds(inner_rows + row, row), above),
+        )
+        for slot, src_rows, dst_rows, target in ends:
+            copy = pltpu.make_async_remote_copy(
+                src_ref=ref.at[pl.ds(1, 2), src_rows],
+                dst_ref=ref.at[pl.ds(1, 2), dst_rows],
+                send_sem=halo_send.at[slot],
+                recv_sem=halo_recv.at[slot],
+                device_id=target,
+                device_id_type=MESH,
+            )
+            copy.start()
+            halos[slot] = copy
+
+    def fill_sides(ref, first):
+        halos[first].wait_recv()
+        halos[first + 1].wait_recv()
+        for b in (1, 2):
+            head, tail = pl.ds(0, row), pl.ds(inner_rows + row, row)
+            ref[b, head] = jnp.where(s == 0, 0.0, ref[b, head].astype(jnp.float32)).astype(
+                jnp.bfloat16
+            )
+            ref[b, tail] = jnp.where(s == 31, 0.0, ref[b, tail].astype(jnp.float32)).astype(
+                jnp.bfloat16
+            )
+        rows = ref.shape[1]
+        at = lax.broadcasted_iota(jnp.int32, (rows, LAT), 0) % row
+        moved = pltpu.roll(ref[2].astype(jnp.float32), 1, 0)
+        ref[0] = jnp.where(at == 0, 0.0, moved).astype(jnp.bfloat16)
+        moved = pltpu.roll(ref[1].astype(jnp.float32), rows - 1, 0)
+        ref[3] = jnp.where(at == row - 1, 0.0, moved).astype(jnp.bfloat16)
+
+    def taps():
+        return [(i, j) for i in range(3) for j in range(3)]
+
+    def upward():
+        feature[...] = ((y_one[...].astype(jnp.float32) + second[...].astype(jnp.float32)) * 0.5).astype(
+            jnp.bfloat16
+        )
+        wide = cot[...].reshape(8 * row, LAT).astype(jnp.float32)
+        cot_low[...] = wide[:, : LAT // 2]
+        cot_high[...] = wide[:, LAT // 2 :]
+        depth = deconv.shape[0] * deconv.shape[1]
+        for ab in range(4):
+            plane = pl.ds(ab * DEC, DEC)
+            up = jnp.dot(
+                feature[...],
+                deconv[:, :, plane].reshape(depth, DEC),
+                preferred_element_type=jnp.float32,
+            ).astype(jnp.bfloat16)
+            for r in range(2):
+                pixels[pl.ds((ab % 2) * inner_rows + (2 * r + ab // 2) * row, row)] = up[
+                    r * row : (r + 1) * row
+                ]
+        lat = jnp.dot(pixels[...], w_lateral[...], preferred_element_type=jnp.float32)
+        lhat, linv = apply_layer_norm(lat)
+        norm_lat[...] = lhat
+        scaled = (lhat * lat_gain[...]).astype(jnp.bfloat16)
+        for b in range(2):
+            act[1 + b, pl.ds(row, inner_rows)] = scaled[b * inner_rows : (b + 1) * inner_rows]
+        swap_edges(act, 0)
+        return linv
+
+    def convolve():
+        fill_sides(act, 0)
+        for b in range(2):
+            total = jnp.zeros((inner_rows, LAT), jnp.float32)
+            for i, j in taps():
+                total += jnp.dot(
+                    act[b + j, pl.ds(i * row, inner_rows)],
+                    w_conv[3 * i + j],
+                    preferred_element_type=jnp.float32,
+                )
+            chat, cinv = apply_layer_norm(total)
+            every = pl.ds(b, inner_rows, stride=2)
+            upstream = jnp.concatenate([cot_low[every, :], cot_high[every, :]], axis=1)
+            upstream = upstream * conv_gain[...]
+            dconv[1 + b, pl.ds(row, inner_rows)] = layer_norm_reverse(upstream, chat, cinv).astype(
+                jnp.bfloat16
+            )
+        swap_edges(dconv, 2)
+
+    def downward(linv):
+        fill_sides(dconv, 2)
+        for b in range(2):
+            total = jnp.zeros((inner_rows, LAT), jnp.float32)
+            for i, j in taps():
+                total += lax.dot_general(
+                    dconv[b - j + 2, pl.ds((2 - i) * row, inner_rows)],
+                    w_conv[3 * i + j],
+                    (((1,), (1,)), ((), ())),
+                    preferred_element_type=jnp.float32,
+                )
+            here = slice(b * inner_rows, (b + 1) * inner_rows)
+            dlat = layer_norm_reverse(
+                total * lat_gain[...], norm_lat[pl.ds(b * inner_rows, inner_rows)], linv[here]
+            ).astype(jnp.bfloat16)
+            term = jnp.dot(
+                pixels[pl.ds(b * inner_rows, inner_rows)].astype(jnp.float32).T.astype(jnp.bfloat16),
+                dlat,
+                preferred_element_type=jnp.float32,
+            )
+            lat_term = term if b == 0 else lat_term + term
+            dpixels = lax.dot_general(
+                dlat, w_lateral[...], (((1,), (1,)), ((), ())), preferred_element_type=jnp.float32
+            ).astype(jnp.bfloat16)
+            for line in range(4):
+                r, a = line // 2, line % 2
+                dup[pl.ds(r * row, row), pl.ds((2 * a + b) * DEC, DEC)] = dpixels[
+                    line * row : (line + 1) * row
+                ]
+        lat_out[...] = (lat_term * grad_scale).astype(jnp.bfloat16)
+        depth = deconv.shape[0] * deconv.shape[1]
+        half = 0.5 * lax.dot_general(
+            dup[...],
+            deconv[...].reshape(depth, 4 * DEC),
+            (((1,), (1,)), ((), ())),
+            preferred_element_type=jnp.float32,
+        )
+        half_out[...] = half
+        d_x1_out[...] = half.astype(jnp.bfloat16)
+
+    def conv_term():
+        turned_grads = [
+            dconv[1 + b, pl.ds(row, inner_rows)].astype(jnp.float32).T.astype(jnp.bfloat16)
+            for b in range(2)
+        ]
+        for i, j in taps():
+            total = jnp.zeros((LAT, LAT), jnp.float32)
+            for b in range(2):
+                total += jnp.dot(
+                    turned_grads[b],
+                    act[b + j, pl.ds(i * row, inner_rows)],
+                    preferred_element_type=jnp.float32,
+                )
+            conv_out[:, pl.ds((3 * i + j) * LAT, LAT)] = (total.T * grad_scale).astype(jnp.bfloat16)
+
+    def deconv_term():
+        rows, per, block, _ = shapes[0]
+        wide = feature[...].astype(jnp.float32).T
+        pick = one_hot(rows, per, block).T.astype(jnp.bfloat16)
+        for g in range(8):
+            group = jnp.dot(
+                pick,
+                wide[g * block : (g + 1) * block].astype(jnp.bfloat16),
+                preferred_element_type=jnp.float32,
+            ).astype(jnp.bfloat16)
+            term = jnp.dot(group, dup[...], preferred_element_type=jnp.float32) * grad_scale
+            dec_out[pl.ds(g * 4 * rows, 4 * rows)] = term.astype(jnp.bfloat16)
+
+    near(0)
+    near(1)
+    far(0)
+    deep(0)
+    twins(0)
+    keeps[0].wait()
+    linv = upward()
+    far(1)
+    near(2)
+    convolve()
+    far(2)
+    downward(linv)
+    deep(1)
+    conv_term()
+    deep(2)
+    deconv_term()
+    twins(1)
+    twins(2)
+    for keep in keeps[1:]:
         keep.wait()
-    for copy in copies.values():
+    for copy in list(copies.values()) + list(halos.values()):
         copy.wait_send()
 
 
-def gather_weights(shards, pers):
+def gather_and_pyramid(shards, pers, *others):
     count = len(shards)
     shapes = []
     for shard, per in zip(shards, pers):
         block = -(-4 * per // 16) * 16
         shapes.append((shard.shape[0], per, block, shard.shape[1]))
     halves = [(rows, block, width // 2) for rows, _, block, width in shapes]
+    tokens, features = others[0].shape
+    bf16, f32 = jnp.bfloat16, jnp.float32
+    full = [jax.ShapeDtypeStruct((8, block, width), bf16) for _, _, block, width in shapes]
+    pixel_count = 4 * tokens
     return pl.pallas_call(
         functools.partial(gather_kernel, shapes),
-        out_shape=[
-            jax.ShapeDtypeStruct((8, block, width), jnp.bfloat16) for _, _, block, width in shapes
+        out_shape=full[1:]
+        + [
+            jax.ShapeDtypeStruct((tokens, features), f32),
+            jax.ShapeDtypeStruct((tokens, features), bf16),
+            jax.ShapeDtypeStruct((32 * ROWS_PAD, 4 * DEC), bf16),
+            jax.ShapeDtypeStruct((LAT, 9 * LAT), bf16),
+            jax.ShapeDtypeStruct((DEC, LAT), bf16),
         ],
-        in_specs=[pl.BlockSpec(memory_space=pltpu.VMEM)] * count,
-        out_specs=[pl.BlockSpec(memory_space=pl.ANY)] * count,
-        scratch_shapes=[pltpu.VMEM((4, rows, half), jnp.bfloat16) for rows, _, half in halves]
-        + [pltpu.VMEM((block, half), jnp.bfloat16) for _, block, half in halves]
+        in_specs=[pl.BlockSpec(memory_space=pltpu.VMEM)] * (count + len(others)),
+        out_specs=[pl.BlockSpec(memory_space=pl.ANY)] * (count - 1)
+        + [pl.BlockSpec(memory_space=pltpu.VMEM)] * 5,
+        scratch_shapes=[pltpu.VMEM(full[0].shape, bf16)]
+        + [pltpu.VMEM((4, rows, half), bf16) for rows, _, half in halves]
+        + [pltpu.VMEM((block, half), bf16) for _, block, half in halves]
         + [
+            pltpu.VMEM((tokens, features), bf16),
+            pltpu.VMEM((pixel_count, DEC), bf16),
+            pltpu.VMEM((4, 6 * GRID_W, LAT), bf16),
+            pltpu.VMEM((4, 6 * GRID_W, LAT), bf16),
+            pltpu.VMEM((pixel_count, LAT // 2), f32),
+            pltpu.VMEM((pixel_count, LAT // 2), f32),
+            pltpu.VMEM((pixel_count, LAT), f32),
+            pltpu.VMEM((tokens, 4 * DEC), bf16),
             pltpu.SemaphoreType.DMA((count, 28)),
             pltpu.SemaphoreType.DMA((count, 28)),
             pltpu.SemaphoreType.DMA((count,)),
+            pltpu.SemaphoreType.DMA((4,)),
+            pltpu.SemaphoreType.DMA((4,)),
         ],
         compiler_params=pltpu.CompilerParams(
-            collective_id=0, has_side_effects=True, vmem_limit_bytes=32 * 2**20
+            collective_id=0, has_side_effects=True, vmem_limit_bytes=56 * 2**20
         ),
-    )(*shards)
+    )(*shards, *others)
 
 
 class Scatter:
@@ -686,7 +850,6 @@
 ):
     devices = lax.axis_size("sp")
     tokens_here = y_one.shape[0]
-    rows_here = tokens_here // GRID_W
     score_scale = HEAD ** (-0.5)
     standardized_input, inverse_deviation = apply_layer_norm(
         second_stream_state.astype(jnp.float32)
@@ -701,72 +864,25 @@
         w_out, ((0, OUT_ROWS_PAD - out_depth), (0, OUT_COLS_PAD - w_out.shape[1]))
     )
     deconv_shard = jnp.pad(w_deconv, ((0, ROWS_PAD - depth), (0, 0)))
-    deconv_full, qkv_full, out_full = gather_weights(
-        [deconv_shard, qkv_shard, out_shard], [depth, depth, out_depth]
+    qkv_full, out_full, halfway_split, d_x1, dec_part, conv_part, lat_part = gather_and_pyramid(
+        [deconv_shard, qkv_shard, out_shard],
+        [depth, depth, out_depth],
+        y_one,
+        second_stream_state,
+        cot,
+        w_lateral,
+        lat_gain[None],
+        w_conv.reshape(9, LAT, LAT),
+        conv_gain[None],
     )
-    deconv_full = deconv_full.reshape(devices * depth, -1)
+    dec_part = dec_part.reshape(4, 2, 4, ROWS_PAD, 4 * DEC)
+    conv_part = conv_part.reshape(4, 2, 4, LAT // devices, 9 * LAT)
+    lat_rows = DEC // devices
+    lat_part = jnp.pad(
+        lat_part.reshape(devices, lat_rows, LAT), ((0, 0), (0, 16 - lat_rows), (0, 0))
+    ).reshape(4, 2, 4, 16, LAT)
     qkv_full = qkv_full.reshape(devices * depth, -1)
     out_full = out_full.reshape(HEADS * HEAD_PAD, -1)[:, : w_out.shape[1]]
-    feature = ((y_one.astype(jnp.float32) + second_stream_state.astype(jnp.float32)) * 0.5).astype(
-        jnp.bfloat16
-    )
-    upsampled = jnp.dot(feature, deconv_full, preferred_element_type=jnp.float32).astype(
-        jnp.bfloat16
-    )
-    pixel_rows = 2 * rows_here
-    pixel_cols = 2 * GRID_W
-    pixels = (
-        upsampled.reshape(rows_here, GRID_W, 2, 2, DEC)
-        .transpose(0, 2, 1, 3, 4)
-        .reshape(pixel_rows * pixel_cols, DEC)
-    )
-    lhat, linv = apply_layer_norm(jnp.dot(pixels, w_lateral, preferred_element_type=jnp.float32))
-    activation = (lhat * lat_gain).astype(jnp.bfloat16).reshape(pixel_rows, pixel_cols, LAT)
-    extended = padded_2(activation, (("sp", 0),), 1)
-    padded = jnp.pad(extended, ((0, 0), (1, 1), (0, 0)))
-    chat, cinv = apply_layer_norm(conv_valid(padded, w_conv))
-    dconv = layer_norm_reverse(cot.astype(jnp.float32) * conv_gain, chat, cinv).astype(jnp.bfloat16)
-    flipped = w_conv[::-1, ::-1].transpose(0, 1, 3, 2)
-    spread_rows = conv_valid(jnp.pad(dconv, ((2, 2), (1, 1), (0, 0))), flipped)
-    from_below = shifted_2(spread_rows[-1].astype(jnp.bfloat16), "sp", 1).astype(jnp.float32)
-    from_above = shifted_2(spread_rows[0].astype(jnp.bfloat16), "sp", -1).astype(jnp.float32)
-    dact = spread_rows[1:-1]
-    dact = dact.at[0].add(from_below).at[-1].add(from_above)
-    patches = jnp.stack(
-        [
-            padded[row_shift : row_shift + pixel_rows, col_shift : col_shift + pixel_cols].reshape(
-                -1, LAT
-            )
-            for row_shift in range(3)
-            for col_shift in range(3)
-        ]
-    )
-    conv_product = jnp.einsum(
-        "kpc,pd->ckd", patches, dconv.reshape(-1, LAT), preferred_element_type=jnp.float32
-    )
-    conv_part = (conv_product.reshape(4, 2, 4, LAT // devices, 9 * LAT) * grad_scale).astype(
-        jnp.bfloat16
-    )
-    dlat = layer_norm_reverse(dact.reshape(-1, LAT) * lat_gain, lhat, linv).astype(jnp.bfloat16)
-    lat_rows = DEC // devices
-    lat_part = rounded_part(pixels, dlat).reshape(devices, lat_rows, LAT)
-    lat_part = jnp.pad(lat_part, ((0, 0), (0, 16 - lat_rows), (0, 0))).reshape(4, 2, 4, 16, LAT)
-    dpixels = lax.dot_general(
-        dlat, w_lateral, (((1,), (1,)), ((), ())), preferred_element_type=jnp.float32
-    ).astype(jnp.bfloat16)
-    dup = (
-        dpixels.reshape(rows_here, 2, GRID_W, 2, DEC)
-        .transpose(0, 2, 1, 3, 4)
-        .reshape(tokens_here, 4 * DEC)
-    )
-    spread_feature = jnp.pad(
-        feature.reshape(tokens_here, devices, depth), ((0, 0), (0, 0), (0, ROWS_PAD - depth))
-    ).reshape(tokens_here, devices * ROWS_PAD)
-    dec_part = rounded_part(spread_feature, dup).reshape(4, 2, 4, ROWS_PAD, 4 * DEC)
-    halfway_split = 0.5 * lax.dot_general(
-        dup, deconv_full, (((1,), (1,)), ((), ())), preferred_element_type=jnp.float32
-    )
-    d_x1 = halfway_split.astype(jnp.bfloat16)
     dattn = lax.dot_general(
         out_full, d_x1, (((1,), (1,)), ((), ())), preferred_element_type=jnp.float32
     ).astype(jnp.bfloat16)

time: 297 us -> 214 us (0.72); the launches traced: 292 us -> 213 us
  local copies, waits for them, and re-layouts: 52 us -> 10.3 us
  matrix products: 37.2 us -> 12.6 us
  other arithmetic: 19.4 us -> 4.5 us
  Pallas kernels: 171 us -> 185 us
  starting transfers between devices: 11.4 us -> 0 us
    pallas_call x1, Pallas kernels: 54.2 us -> 76.4 us  [gather_and_pyramid(): pl.pallas_call(functools.partial(gather_kernel, shapes), out_shape=full[1...]
    dot_general x7 -> x0, matrix products: 15.3 us -> none  [the longest x1 4.78 us: per_device(): lax.dot_general(dup, deconv_full, (((1,), (1,)), ((), ())), preferred_ele...]
    reshape x8 -> x1, local copies, waits for them, and re-layouts: 15.2 us -> 0.05 us  [per_device(): lat_part.reshape(devices, lat_rows, LAT)]
    ppermute x4 -> x0, starting transfers between devices: 11.4 us -> none  [the longest x2 6.45 us: shifted_2(): return lax.ppermute(array, axis, pairs)]
    unnamed x93 -> x36, local copies, waits for them, and re-layouts: 13.1 us -> 2.7 us
    convert_element_type x3 -> x0, local copies, waits for them, and re-layouts: 10 us -> none  [the longest x2 8.15 us: per_device(): (conv_product.reshape(4, 2, 4, LAT // devices, 9 * LAT) * grad_scale).ast...]
    conv_general_dilated x2 -> x0, matrix products: 10 us -> none  [conv_valid(): lax.conv_general_dilated(padded[None], kernel, (1, 1), 'VALID', dimension...]
    pallas_call x1, Pallas kernels: 116 us -> 108 us  [attend_both_ways(): pl.pallas_call(attention_kernel, out_shape=[jax.ShapeDtypeStruct((heads,...]
  transfers between devices with their start and end apart: 4 -> 0, of which waited for: 0 -> 0; matrix products, arithmetic and copies ran while one was open for 11% -> 0% of each run, Pallas kernels for 0% -> 0%
where the time goes in v5:
time: 214 us; the launch traced here: 213 us
  Pallas kernels  185 us (86%)
  matrix products  12.6 us (6%)
  local copies, waits for them, and re-layouts  10.3 us (5%)
  other arithmetic  4.5 us (2%)
    pallas_call x1, Pallas kernels, attend_both_ways(): pl.pallas_call(attention_kernel, out_shape=[jax.ShapeDtypeStruct((heads,...  108 us
    pallas_call x1, Pallas kernels, gather_and_pyramid(): pl.pallas_call(functools.partial(gather_kernel, shapes), out_shape=full[1...  76.4 us

profile of v5, /device:TPU:64, one launch (start us, length us, event | category | flops | bytes accessed | tf_op | source)
XLA Modules:
  0.0 213.0 jit_solution(13369269886861485416)
XLA Ops:
  0.6 0.0 copy-start
  0.6 1.6 pad.16.refs_0_
  2.3 1.3 reshape.79
  3.6 0.0 copy-start.11
  3.6 0.1 pad.17
  3.6 0.9 reshape.80.refs_1_
  4.6 1.5 pad.18.refs_2_
  6.1 76.4 %shard_map.171 = (bf16[8,176,2304]{2,1,0:T(8,128)(2,1)}, bf16[8,96,1536]{2,1,0:T(8,128)(2,1)}, f32[128,1408]{1,0:T(8,128)}, bf16[128,1408]{1,0:T(8,128)(2,1)}, b...) custom-call(bf16[48,1536]{1,0:T(8,128)(2,1)} %pad.16.refs_0_, ...), custom_call_target="tpu_custom_call" | custom-call | tf_op jit(solution)/shard_map/pallas_call | solution.py:372
  82.5 0.0 copy-done
  82.5 0.1 convert_reduce_fusion
  82.6 0.2 fusion.18
  82.9 0.0 copy-done.11
  82.9 4.0 %fusion.19 = f32[128,2304]{1,0:T(8,128)S(1)} fusion(bf16[1408,2304]{1,0:T(8,128)(2,1)} %bitcast.25, bf16[128,1408]{1,0:T(8,128)(2,1)S(1)} %copy-done, f32[1408]{0:T(1024)S(1)} %copy-done.11, f32[128]{0:T(128)S(1)} %add_rsqrt_fusion, f32[128]{0:T(128)S(1)} %broadcast_multiply_fusion.2), kind=kOutput, calls=%fused_computation.22 | convolution fusion | flops 831373312 | bytes 8034816 | tf_op jit(solution)/shard_map/dot_general | solution.py:890
  86.9 0.0 copy-start.13
  86.9 0.0 copy-start.1
  86.9 1.4 copy.20
  88.3 0.0 copy-done.13
  88.4 2.3 %multiply_convert_fusion.proj = bf16[3,8,96,128]{3,2,1,0:T(8,128)(2,1)} fusion(f32[3,8,96,128]{3,2,1,0:T(8,128)} %bitcast.31, f32[3]{0:T(128)S(1)} %copy-done.13), kind=kLoop, calls=%fused_computation.6 | loop fusion | flops 589824 | bytes 1769484 | tf_op jit(solution)/shard_map/convert_element_type | solution.py:894
  90.6 0.0 copy-done.1
  90.7 3.2 %fusion.4 = bf16[768,128]{1,0:T(8,128)(2,1)} fusion(bf16[128,1408]{1,0:T(8,128)(2,1)S(1)} %copy-done.1, bf16[768,1536]{1,0:T(8,128)(2,1)} %bitcast.32), kind=kOutput, calls=%fused_computation.7 | convolution fusion | flops 276922368 | bytes 2719744 | tf_op jit(solution)/shard_map/dot_general | solution.py:886
  93.8 0.0 copy-done.6
  93.9 0.7 pad.19
  94.6 108.4 %shard_map.172 = (bf16[8,96,128]{2,1,0:T(8,128)(2,1)}, bf16[3,8,96,128]{3,2,1,0:T(8,128)(2,1)}, f32[48,768]{1,0:T(8,128)}, f32[48,768]{1,0:T(8,128)}, f32[8,2304...) custom-call(bf16[3,8,96,128]{3,2,1,0:T(8,128)(2,1)} %multiply_convert_fusion.proj, bf16[8,96,128]{2,1,0:T(8,128)(2,1)} %bitcast.39, ...), custom_call_target="tpu_custom_call" | custom-call | tf_op jit(solution)/shard_map/pallas_call | solution.py:818
  203.0 0.0 copy-start.5
  203.0 0.0 copy-done.3
  203.0 3.0 %fusion = bf16[128,1408]{1,0:T(8,128)(2,1)} fusion(bf16[768,128]{1,0:T(8,128)(2,1)} %bitcast.38, bf16[768,1536]{1,0:T(8,128)(2,1)} %bitcast.33, bf16[128,1408]{1,0:T(8,128)(2,1)S(1)} %copy-done.3), kind=kOutput, calls=%fused_computation.2 | convolution fusion | flops 277364736 | bytes 3080192 | tf_op jit(solution)/shard_map/dot_general | solution.py:903
  206.1 0.0 slice-done
  206.1 0.0 slice-done.1
  206.1 0.0 copy-done.5
  206.1 0.0 copy-start.4
  206.1 0.0 copy-start.7
  206.1 0.0 copy-start.8
  206.1 2.4 %fusion.24 = (f32[128]{0:T(128)S(1)}, f32[128]{0:T(128)S(1)}, f32[128,1408]{1,0:T(8,128)S(1)}) fusion(f32[128]{0:T(128)S(1)} %add_rsqrt_fusion, f32[128]{0:T(128)S(1)} %broadcast_multiply_fusion.2, bf16[128,1408]{1,0:T(8,128)(2,1)S(1)} %copy-done, f32[1408]{0:T(1024)S(1)} %copy-done.11, bf16[2304,128]{1,0:T(8,128)(2,1)S(1)} %bitcast.37, ...), kind=kOutput, calls=%fused_computation.31 | convolution fusion | flops 831733504 | bytes 8166912 | tf_op jit(solution)/shard_map/dot_general | solution.py:910
  208.5 0.0 copy-start.2
  208.5 0.0 copy-start.9
  208.5 0.0 copy-start.12
  208.5 0.0 copy-start.10
  208.5 0.0 copy-done.4
  208.5 1.1 fusion.17
  209.6 0.0 copy-done.7
  209.6 0.0 copy-done.8
  209.6 0.7 pad_maximum_fusion
  210.3 0.0 copy-done.2
  210.3 0.7 copy.25
  211.1 0.0 copy-done.9
  211.1 0.7 copy.26
  211.7 0.6 copy.27
  212.3 0.6 copy.28
  (11 shorter events, 0.1 us)
Async XLA Ops:
  0.6 81.8 %copy-start = (bf16[128,1408]{1,0:T(8,128)(2,1)S(1)}, bf16[128,1408]{1,0:T(8,128)(2,1)}, u32[]{:S(2)}) copy-start(bf16[128,1408]{1,0:T(8,128)(2,1)} %refs_4_.1) | copy-start | bytes 1081348
  3.6 79.3 %copy-start.11 = (f32[1408]{0:T(1024)S(1)}, f32[1408]{0:T(1024)}, u32[]{:S(2)}) copy-start(f32[1408]{0:T(1024)} %param.15) | copy-start | bytes 16900
  86.9 1.4 copy-start.13
  86.9 3.7 %copy-start.1 = (bf16[128,1408]{1,0:T(8,128)(2,1)S(1)}, bf16[128,1408]{1,0:T(8,128)(2,1)}, u32[]{:S(2)}) copy-start(bf16[128,1408]{1,0:T(8,128)(2,1)} %get-tuple-element.48.d_x1) | copy-start | bytes 1081348
  88.4 5.5 %copy-start.6 = (bf16[384,256]{1,0:T(8,128)(2,1)S(1)}, bf16[384,256]{1,0:T(8,128)(2,1)}, u32[]{:S(2)}) copy-start(bf16[384,256]{1,0:T(8,128)(2,1)} %get-tuple-element.26) | copy-start | bytes 589828
  90.7 115.4 %slice-start = ((s8[6488064]{0:T(1024)(128)(4,1)}), s8[2293760]{0:T(1024)(128)(4,1)S(1)}, s32[]{:S(2)}) async-start(s8[6488064]{0:T(1024)(128)(4,1)} %bitcast.26), calls=%async_computation | async-start | bytes 4587520
  94.6 108.4 %copy-start.3 = (bf16[128,1408]{1,0:T(8,128)(2,1)S(1)}, bf16[128,1408]{1,0:T(8,128)(2,1)}, u32[]{:S(2)}) copy-start(bf16[128,1408]{1,0:T(8,128)(2,1)} %refs_3_.1) | copy-start | bytes 1081348
  94.6 111.5 %slice-start.1 = ((s8[6488064]{0:T(1024)(128)(4,1)}), s8[4194304]{0:T(1024)(128)(4,1)S(1)}, s32[]{:S(2)}) async-start(s8[6488064]{0:T(1024)(128)(4,1)} %bitcast.26), calls=%async_computation.1 | async-start | bytes 8388608
  203.0 3.1 %copy-start.5 = (bf16[3,8,96,128]{3,2,1,0:T(8,128)(2,1)S(1)}, bf16[3,8,96,128]{3,2,1,0:T(8,128)(2,1)}, u32[]{:S(2)}) copy-start(bf16[3,8,96,128]{3,2,1,0:T(8,128)(2,1)} %get-tuple-element.29) | copy-start | bytes 1769476
  206.1 2.5 %copy-start.4 = (f32[128,1408]{1,0:T(8,128)S(1)}, f32[128,1408]{1,0:T(8,128)}, u32[]{:S(2)}) copy-start(f32[128,1408]{1,0:T(8,128)} %get-tuple-element.28) | copy-start | bytes 2162692
  206.1 3.5 %copy-start.7 = (f32[48,768]{1,0:T(8,128)S(1)}, f32[48,768]{1,0:T(8,128)}, u32[]{:S(2)}) copy-start(f32[48,768]{1,0:T(8,128)} %get-tuple-element.31) | copy-start | bytes 442372
  206.1 3.5 %copy-start.8 = (f32[48,768]{1,0:T(8,128)S(1)}, f32[48,768]{1,0:T(8,128)}, u32[]{:S(2)}) copy-start(f32[48,768]{1,0:T(8,128)} %get-tuple-element.32) | copy-start | bytes 442372
  208.5 1.9 copy-start.2
  208.5 2.6 %copy-start.9 = (f32[24,1408]{1,0:T(8,128)S(1)}, f32[24,1408]{1,0:T(8,128)}, u32[]{:S(2)}) copy-start(f32[24,1408]{1,0:T(8,128)} %get-tuple-element.30) | copy-start | bytes 405508
  208.5 3.3 %copy-start.12 = (f32[16,256]{1,0:T(8,128)S(1)}, f32[16,256]{1,0:T(8,128)}, u32[]{:S(2)}) copy-start(f32[16,256]{1,0:T(8,128)} %get-tuple-element.33) | copy-start | bytes 49156
  208.5 3.9 %copy-start.10 = (f32[8,2304]{1,0:T(8,128)S(1)}, f32[8,2304]{1,0:T(8,128)}, u32[]{:S(2)}) copy-start(f32[8,2304]{1,0:T(8,128)} %get-tuple-element.34) | copy-start | bytes 221188

commit v6 on v5

--- a/solution.py
+++ b/solution.py
@@ -406,89 +406,104 @@
     )(*shards, *others)
 
 
+AXES = {"x": 4, "z": 2, "y": 4}
+
+
+def leads(order):
+    left = list(AXES)
+    sizes = []
+    for axis in order:
+        left = [name for name in left if name != axis]
+        sizes.append([AXES[name] for name in left])
+    return sizes
+
+
 class Scatter:
     def __init__(self, plan, parts, buffers, send, recv, local):
         self.plan, self.parts = plan, parts
-        self.land1, self.sum1, self.land2, self.sum2, self.land3 = buffers
+        self.land = [buffers[0], buffers[2], buffers[4]]
+        self.sums = [buffers[1], buffers[3]]
         self.send, self.recv, self.local = send, recv, local
-        self.x, self.zl, self.y, _, _ = place()
-        self.row = [(self.x + k) % 4 for k in (1, 2, 3)]
-        self.column = [(self.y + k) % 4 for k in (1, 2, 3)]
+        x, zl, y, _, _ = place()
+        self.me = {"x": x, "z": zl, "y": y}
+        self.peers = {
+            "x": [(x + k) % 4 for k in (1, 2, 3)],
+            "y": [(y + k) % 4 for k in (1, 2, 3)],
+            "z": [1 - zl],
+        }
         self.copies, self.own = {}, {}
 
-    def push(self, n, slot, src, dst, target):
-        copy = pltpu.make_async_remote_copy(
-            src_ref=src,
-            dst_ref=dst,
-            send_sem=self.send.at[n, slot],
-            recv_sem=self.recv.at[n, slot],
-            device_id=target,
-            device_id_type=MESH,
-        )
-        copy.start()
-        self.copies[n, slot] = copy
-
-    def to_row(self, k):
-        return at_sp(self.row[k], self.zl, self.y)
-
-    def to_column(self, k):
-        return at_sp(self.x, self.zl, self.column[k])
+    def take(self, n, step, view, where):
+        order = self.plan[n][3]
+        left = [name for name in AXES if name not in order[:step]]
+        lead = [slice(None)] * left.index(order[step])
+        return view.at[(*lead, where)]
+
+    def ship(self, n, step, view):
+        axis = self.plan[n][3][step]
+        for k, peer in enumerate(self.peers[axis]):
+            at = dict(self.me)
+            at[axis] = peer
+            copy = pltpu.make_async_remote_copy(
+                src_ref=self.take(n, step, view, peer),
+                dst_ref=self.land[step][n].at[k],
+                send_sem=self.send.at[n, 3 * step + k],
+                recv_sem=self.recv.at[n, 3 * step + k],
+                device_id=at_sp(at["x"], at["z"], at["y"]),
+                device_id_type=MESH,
+            )
+            copy.start()
+            self.copies[n, step, k] = copy
+
+    def arrived(self, n, step):
+        count = len(self.peers[self.plan[n][3][step]])
+        for k in range(count):
+            self.copies[n, step, k].wait_recv()
+        return count
 
     def start(self, n):
-        source, first, width, x_first = self.plan[n]
+        source, first, width, order = self.plan[n]
         view = self.parts[source].at[:, :, :, :, pl.ds(first, width)]
-        own = view.at[self.x] if x_first else view.at[:, :, self.y]
-        self.own[n] = pltpu.make_async_copy(own, self.sum1[n], self.local.at[n])
+        own = self.take(n, 0, view, self.me[order[0]])
+        self.own[n] = pltpu.make_async_copy(own, self.sums[0][n], self.local.at[n])
         self.own[n].start()
-        for k in range(3):
-            if x_first:
-                self.push(n, k, view.at[self.row[k]], self.land1[n].at[k], self.to_row(k))
-            else:
-                self.push(n, k, view.at[:, :, self.column[k]], self.land1[n].at[k], self.to_column(k))
+        self.ship(n, 0, view)
 
     def second(self, n):
-        x_first = self.plan[n][3]
-        sums, land = self.sum1[n], self.land1[n]
+        sums, land = self.sums[0][n], self.land[0][n]
         self.own[n].wait()
-        for k in range(3):
-            self.copies[n, k].wait_recv()
+        count = self.arrived(n, 0)
         outer, inner = sums.shape[:2]
 
         def add(t, carry):
             p, q = t // inner, t % inner
             total = sums[p, q].astype(jnp.float32)
-            for k in range(3):
+            for k in range(count):
                 total += land[k, p, q].astype(jnp.float32)
             sums[p, q] = total.astype(jnp.bfloat16)
             return carry
 
         lax.fori_loop(0, outer * inner, add, 0)
-        for k in range(3):
-            if x_first:
-                self.push(
-                    n, 3 + k, sums.at[:, self.column[k]], self.land2[n].at[k], self.to_column(k)
-                )
-            else:
-                self.push(n, 3 + k, sums.at[self.row[k]], self.land2[n].at[k], self.to_row(k))
+        self.ship(n, 1, sums)
 
     def third(self, n):
-        x_first = self.plan[n][3]
-        for k in range(3):
-            self.copies[n, 3 + k].wait_recv()
-        for p in range(2):
-            own = self.sum1[n][p, self.y] if x_first else self.sum1[n][self.x, p]
-            total = own.astype(jnp.float32)
-            for k in range(3):
-                total += self.land2[n][k, p].astype(jnp.float32)
-            self.sum2[n][p] = total.astype(jnp.bfloat16)
-        across = at_sp(self.x, 1 - self.zl, self.y)
-        self.push(n, 6, self.sum2[n].at[1 - self.zl], self.land3[n], across)
+        land, sums = self.land[1][n], self.sums[1][n]
+        order = self.plan[n][3]
+        count = self.arrived(n, 1)
+        own = self.take(n, 1, self.sums[0][n], self.me[order[1]])
+        for p in range(sums.shape[0]):
+            total = own[p].astype(jnp.float32)
+            for k in range(count):
+                total += land[k, p].astype(jnp.float32)
+            sums[p] = total.astype(jnp.bfloat16)
+        self.ship(n, 2, sums)
 
     def finish(self, n, out):
-        self.copies[n, 6].wait_recv()
-        out[...] = self.sum2[n][self.zl].astype(jnp.float32) + self.land3[n][...].astype(
-            jnp.float32
-        )
+        count = self.arrived(n, 2)
+        total = self.sums[1][n][self.me[self.plan[n][3][2]]].astype(jnp.float32)
+        for k in range(count):
+            total += self.land[2][n][k].astype(jnp.float32)
+        out[...] = total
 
     def settle(self):
         for copy in self.copies.values():
@@ -496,18 +511,16 @@
 
 
 def scatter_buffers(plan, rows):
-    chunks = [(rows[source], width, order) for source, _, width, order in plan]
-
-    def ordered(*lead):
-        return [
-            pltpu.VMEM((*lead, *((2, 4) if order else (4, 2)), r, w), jnp.bfloat16)
-            for r, w, order in chunks
-        ]
-
-    def plain(*lead):
-        return [pltpu.VMEM((*lead, r, w), jnp.bfloat16) for r, w, _ in chunks]
-
-    return [ordered(3), ordered(), plain(3, 2), plain(2), plain()]
+    groups = [[], [], [], [], []]
+    for source, _, width, order in plan:
+        sizes = leads(order)
+        for step in range(3):
+            peers = AXES[order[step]] - 1
+            tail = (rows[source], width)
+            groups[2 * step].append(pltpu.VMEM((peers, *sizes[step], *tail), jnp.bfloat16))
+            if step < 2:
+                groups[2 * step + 1].append(pltpu.VMEM((*sizes[step], *tail), jnp.bfloat16))
+    return groups
 
 
 TILE = 128
@@ -526,11 +539,11 @@
 
 
 SUM_PLAN = [
-    (0, 0, 2 * DEC, True),
-    (0, 2 * DEC, 2 * DEC, False),
-    (1, 0, 9 * LAT, True),
-    (2, 0, LAT, True),
-    (3, 0, 1408, False),
+    (0, 0, 2 * DEC, "xyz"),
+    (0, 2 * DEC, 2 * DEC, "zxy"),
+    (1, 0, 9 * LAT, "zxy"),
+    (2, 0, LAT, "zxy"),
+    (3, 0, 1408, "yxz"),
 ]
 OUT_ROWS = 22
 OUT_ROWS_STEP = 24
@@ -617,7 +630,7 @@
         pass_on(k)
     for k in range(1, 8):
         push(g_at + k, grad.at[plane[k]], g_in.at[m], at_plane(k))
-    for n in (0, 2, 3):
+    for n in (0, 1, 2, 3):
         sums.start(n)
     zero_rows = jnp.zeros((TILE - HEAD_PAD, key_t.shape[1]), jnp.bfloat16)
     key_t[HEAD_PAD:] = zero_rows
@@ -650,7 +663,6 @@
             copies[ring_at + 3 * k + j - 1].wait_recv()
         first = ((y + 4 - j) % 4) * 8
         lax.fori_loop(first, first + 8, prepare, 0)
-    sums.start(1)
     for k in range(1, 8):
         copies[g_at + k].wait_recv()
     lax.fori_loop(0, 8, prepare_cots, 0)
@@ -756,19 +768,25 @@
         attended[at, :] = query_grad * (inverse[at, :] * HEAD ** (-0.5))
         return carry
 
-    lax.fori_loop(0, queries // QUERY_BLOCK, backward, 0)
+    for i in range(queries // QUERY_BLOCK):
+        backward(i, 0)
+        if i == 0:
+            key_home(1)
+            sums.second(3)
+            sums.second(2)
     key_side(query_t, 0)
     for t in range(8):
         dq_send[t] = head_rows(attended[pl.ds(t * TILE, TILE), :])
     for k in range(1, 8):
         push(dq_at + k, dq_send.at[plane[k]], d_res.at[0, m], at_plane(k))
     d_res[0, m] = dq_send[m]
-    for n in (0, 1, 2, 3):
-        sums.second(n)
-    key_home(1)
+    sums.second(0)
+    sums.second(1)
+    sums.third(3)
+    sums.third(2)
     key_home(0)
     sums.second(4)
-    for n in range(5):
+    for n in (0, 1, 4):
         sums.third(n)
     for first in (dq_at, home_at, home_at + 8):
         for k in range(1, 8):
@@ -814,7 +832,7 @@
         ((3, 8, *block), bf16),
         ((4, 2, 4, OUT_ROWS_STEP, d_x1.shape[1]), bf16),
     ]
-    sum_sems = pltpu.SemaphoreType.DMA((len(SUM_PLAN), 7))
+    sum_sems = pltpu.SemaphoreType.DMA((len(SUM_PLAN), 9))
     return pl.pallas_call(
         attention_kernel,
         out_shape=[

time: 214 us -> 213 us (level)
  no operation moved by 1% of the time
where the time goes in v6:
time: 213 us
  Pallas kernels  185 us (87%)
  matrix products  12.6 us (6%)
  local copies, waits for them, and re-layouts  10.3 us (5%)
  other arithmetic  4.5 us (2%)
    pallas_call x1, Pallas kernels, attend_both_ways(): pl.pallas_call(attention_kernel, out_shape=[jax.ShapeDtypeStruct((heads,...  109 us
    pallas_call x1, Pallas kernels, gather_and_pyramid(): pl.pallas_call(functools.partial(gather_kernel, shapes), out_shape=full[1...  76.4 us

profile of v6, /device:TPU:64, one launch (start us, length us, event | category | flops | bytes accessed | tf_op | source)
XLA Modules:
  0.0 213.1 jit_solution(17618984789003514356)
XLA Ops:
  0.6 0.0 copy-start
  0.6 1.6 pad.16.refs_0_
  2.3 1.3 reshape.79
  3.6 0.0 copy-start.11
  3.6 0.1 pad.17
  3.6 0.9 reshape.80.refs_1_
  4.6 1.5 pad.18.refs_2_
  6.1 76.4 %shard_map.171 = (bf16[8,176,2304]{2,1,0:T(8,128)(2,1)}, bf16[8,96,1536]{2,1,0:T(8,128)(2,1)}, f32[128,1408]{1,0:T(8,128)}, bf16[128,1408]{1,0:T(8,128)(2,1)}, b...) custom-call(bf16[48,1536]{1,0:T(8,128)(2,1)} %pad.16.refs_0_, ...), custom_call_target="tpu_custom_call" | custom-call | tf_op jit(solution)/shard_map/pallas_call | solution.py:372
  82.5 0.0 copy-done
  82.5 0.1 convert_reduce_fusion
  82.6 0.2 fusion.18
  82.9 0.0 copy-done.11
  82.9 4.0 %fusion.19 = f32[128,2304]{1,0:T(8,128)S(1)} fusion(bf16[1408,2304]{1,0:T(8,128)(2,1)} %bitcast.25, bf16[128,1408]{1,0:T(8,128)(2,1)S(1)} %copy-done, f32[1408]{0:T(1024)S(1)} %copy-done.11, f32[128]{0:T(128)S(1)} %add_rsqrt_fusion, f32[128]{0:T(128)S(1)} %broadcast_multiply_fusion.2), kind=kOutput, calls=%fused_computation.22 | convolution fusion | flops 831373312 | bytes 8034816 | tf_op jit(solution)/shard_map/dot_general | solution.py:908
  86.9 0.0 copy-start.13
  86.9 0.0 copy-start.1
  86.9 1.4 copy.20
  88.3 0.0 copy-done.13
  88.4 2.3 %multiply_convert_fusion.proj = bf16[3,8,96,128]{3,2,1,0:T(8,128)(2,1)} fusion(f32[3,8,96,128]{3,2,1,0:T(8,128)} %bitcast.31, f32[3]{0:T(128)S(1)} %copy-done.13), kind=kLoop, calls=%fused_computation.6 | loop fusion | flops 589824 | bytes 1769484 | tf_op jit(solution)/shard_map/convert_element_type | solution.py:912
  90.6 0.0 copy-done.1
  90.7 3.2 %fusion.4 = bf16[768,128]{1,0:T(8,128)(2,1)} fusion(bf16[128,1408]{1,0:T(8,128)(2,1)S(1)} %copy-done.1, bf16[768,1536]{1,0:T(8,128)(2,1)} %bitcast.32), kind=kOutput, calls=%fused_computation.7 | convolution fusion | flops 276922368 | bytes 2719744 | tf_op jit(solution)/shard_map/dot_general | solution.py:904
  93.8 0.0 copy-done.6
  93.9 0.7 pad.19
  94.6 108.5 %shard_map.172 = (bf16[8,96,128]{2,1,0:T(8,128)(2,1)}, bf16[3,8,96,128]{3,2,1,0:T(8,128)(2,1)}, f32[48,768]{1,0:T(8,128)}, f32[48,768]{1,0:T(8,128)}, f32[8,2304...) custom-call(bf16[3,8,96,128]{3,2,1,0:T(8,128)(2,1)} %multiply_convert_fusion.proj, bf16[8,96,128]{2,1,0:T(8,128)(2,1)} %bitcast.39, ...), custom_call_target="tpu_custom_call" | custom-call | tf_op jit(solution)/shard_map/pallas_call | solution.py:836
  203.1 0.0 copy-start.5
  203.1 0.0 copy-done.3
  203.1 3.0 %fusion = bf16[128,1408]{1,0:T(8,128)(2,1)} fusion(bf16[768,128]{1,0:T(8,128)(2,1)} %bitcast.38, bf16[768,1536]{1,0:T(8,128)(2,1)} %bitcast.33, bf16[128,1408]{1,0:T(8,128)(2,1)S(1)} %copy-done.3), kind=kOutput, calls=%fused_computation.2 | convolution fusion | flops 277364736 | bytes 3080192 | tf_op jit(solution)/shard_map/dot_general | solution.py:921
  206.2 0.0 slice-done
  206.2 0.0 slice-done.1
  206.2 0.0 copy-done.5
  206.2 0.0 copy-start.4
  206.2 0.0 copy-start.7
  206.2 0.0 copy-start.8
  206.2 2.4 %fusion.24 = (f32[128]{0:T(128)S(1)}, f32[128]{0:T(128)S(1)}, f32[128,1408]{1,0:T(8,128)S(1)}) fusion(f32[128]{0:T(128)S(1)} %add_rsqrt_fusion, f32[128]{0:T(128)S(1)} %broadcast_multiply_fusion.2, bf16[128,1408]{1,0:T(8,128)(2,1)S(1)} %copy-done, f32[1408]{0:T(1024)S(1)} %copy-done.11, bf16[2304,128]{1,0:T(8,128)(2,1)S(1)} %bitcast.37, ...), kind=kOutput, calls=%fused_computation.31 | convolution fusion | flops 831733504 | bytes 8166912 | tf_op jit(solution)/shard_map/dot_general | solution.py:928
  208.6 0.0 copy-start.2
  208.6 0.0 copy-start.9
  208.6 0.0 copy-start.12
  208.6 0.0 copy-start.10
  208.6 0.0 copy-done.4
  208.6 1.1 fusion.17
  209.7 0.0 copy-done.7
  209.7 0.0 copy-done.8
  209.7 0.7 pad_maximum_fusion
  210.4 0.0 copy-done.2
  210.5 0.7 copy.25
  211.2 0.0 copy-done.9
  211.2 0.7 copy.26
  211.8 0.6 copy.27
  212.5 0.6 copy.28
  (11 shorter events, 0.1 us)
Async XLA Ops:
  0.6 81.8 %copy-start = (bf16[128,1408]{1,0:T(8,128)(2,1)S(1)}, bf16[128,1408]{1,0:T(8,128)(2,1)}, u32[]{:S(2)}) copy-start(bf16[128,1408]{1,0:T(8,128)(2,1)} %refs_4_.1) | copy-start | bytes 1081348
  3.6 79.3 %copy-start.11 = (f32[1408]{0:T(1024)S(1)}, f32[1408]{0:T(1024)}, u32[]{:S(2)}) copy-start(f32[1408]{0:T(1024)} %param.15) | copy-start | bytes 16900
  86.9 1.4 copy-start.13
  86.9 3.7 %copy-start.1 = (bf16[128,1408]{1,0:T(8,128)(2,1)S(1)}, bf16[128,1408]{1,0:T(8,128)(2,1)}, u32[]{:S(2)}) copy-start(bf16[128,1408]{1,0:T(8,128)(2,1)} %get-tuple-element.48.d_x1) | copy-start | bytes 1081348
  88.4 5.5 %copy-start.6 = (bf16[384,256]{1,0:T(8,128)(2,1)S(1)}, bf16[384,256]{1,0:T(8,128)(2,1)}, u32[]{:S(2)}) copy-start(bf16[384,256]{1,0:T(8,128)(2,1)} %get-tuple-element.26) | copy-start | bytes 589828
  90.7 115.5 %slice-start = ((s8[6488064]{0:T(1024)(128)(4,1)}), s8[2293760]{0:T(1024)(128)(4,1)S(1)}, s32[]{:S(2)}) async-start(s8[6488064]{0:T(1024)(128)(4,1)} %bitcast.26), calls=%async_computation | async-start | bytes 4587520
  94.6 108.5 %copy-start.3 = (bf16[128,1408]{1,0:T(8,128)(2,1)S(1)}, bf16[128,1408]{1,0:T(8,128)(2,1)}, u32[]{:S(2)}) copy-start(bf16[128,1408]{1,0:T(8,128)(2,1)} %refs_3_.1) | copy-start | bytes 1081348
  94.6 111.6 %slice-start.1 = ((s8[6488064]{0:T(1024)(128)(4,1)}), s8[4194304]{0:T(1024)(128)(4,1)S(1)}, s32[]{:S(2)}) async-start(s8[6488064]{0:T(1024)(128)(4,1)} %bitcast.26), calls=%async_computation.1 | async-start | bytes 8388608
  203.1 3.1 %copy-start.5 = (bf16[3,8,96,128]{3,2,1,0:T(8,128)(2,1)S(1)}, bf16[3,8,96,128]{3,2,1,0:T(8,128)(2,1)}, u32[]{:S(2)}) copy-start(bf16[3,8,96,128]{3,2,1,0:T(8,128)(2,1)} %get-tuple-element.29) | copy-start | bytes 1769476
  206.2 2.5 %copy-start.4 = (f32[128,1408]{1,0:T(8,128)S(1)}, f32[128,1408]{1,0:T(8,128)}, u32[]{:S(2)}) copy-start(f32[128,1408]{1,0:T(8,128)} %get-tuple-element.28) | copy-start | bytes 2162692
  206.2 3.5 %copy-start.7 = (f32[48,768]{1,0:T(8,128)S(1)}, f32[48,768]{1,0:T(8,128)}, u32[]{:S(2)}) copy-start(f32[48,768]{1,0:T(8,128)} %get-tuple-element.31) | copy-start | bytes 442372
  206.2 3.5 %copy-start.8 = (f32[48,768]{1,0:T(8,128)S(1)}, f32[48,768]{1,0:T(8,128)}, u32[]{:S(2)}) copy-start(f32[48,768]{1,0:T(8,128)} %get-tuple-element.32) | copy-start | bytes 442372
  208.6 1.9 copy-start.2
  208.6 2.6 %copy-start.9 = (f32[24,1408]{1,0:T(8,128)S(1)}, f32[24,1408]{1,0:T(8,128)}, u32[]{:S(2)}) copy-start(f32[24,1408]{1,0:T(8,128)} %get-tuple-element.30) | copy-start | bytes 405508
  208.6 3.3 %copy-start.12 = (f32[16,256]{1,0:T(8,128)S(1)}, f32[16,256]{1,0:T(8,128)}, u32[]{:S(2)}) copy-start(f32[16,256]{1,0:T(8,128)} %get-tuple-element.33) | copy-start | bytes 49156
  208.6 3.9 %copy-start.10 = (f32[8,2304]{1,0:T(8,128)S(1)}, f32[8,2304]{1,0:T(8,128)}, u32[]{:S(2)}) copy-start(f32[8,2304]{1,0:T(8,128)} %get-tuple-element.34) | copy-start | bytes 221188

commit v7 on v6

--- a/solution.py
+++ b/solution.py
@@ -115,8 +115,9 @@
         for k in range(3):
             push(a, k, mine, shards[a].at[y], column[k])
         shards[a][y] = ins[a][:, pl.ds(first, half)]
-    keeps = []
-    for a in range(count):
+    keeps = {}
+
+    def pack(a):
         rows, per, block, _ = shapes[a]
         half, first = part(a)
         low = (block // 32) * 16
@@ -130,7 +131,7 @@
         own, whole = packs[a], region(a, x, zl, 0, block)
         keep = pltpu.make_async_copy(own, whole, local.at[a])
         keep.start()
-        keeps.append(keep)
+        keeps[a] = keep
         push(a, 3, own, whole, right)
         push(a, 4, own, whole, left)
         push(a, 7, own.at[pl.ds(0, low)], region(a, x, zl, 0, low), up)
@@ -334,9 +335,12 @@
             term = jnp.dot(group, dup[...], preferred_element_type=jnp.float32) * grad_scale
             dec_out[pl.ds(g * 4 * rows, 4 * rows)] = term.astype(jnp.bfloat16)
 
+    pack(0)
     near(0)
+    pack(1)
+    far(0)
+    pack(2)
     near(1)
-    far(0)
     deep(0)
     twins(0)
     keeps[0].wait()
@@ -352,8 +356,8 @@
     deconv_term()
     twins(1)
     twins(2)
-    for keep in keeps[1:]:
-        keep.wait()
+    for a in range(1, count):
+        keeps[a].wait()
     for copy in list(copies.values()) + list(halos.values()):
         copy.wait_send()
 
@@ -543,14 +547,15 @@
     (0, 2 * DEC, 2 * DEC, "zxy"),
     (1, 0, 9 * LAT, "zxy"),
     (2, 0, LAT, "zxy"),
-    (3, 0, 1408, "yxz"),
+    (3, 0, 768, "yxz"),
+    (3, 768, 640, "xyz"),
 ]
 OUT_ROWS = 22
 OUT_ROWS_STEP = 24
 
 
 def attention_kernel(proj, grad, d_x1, dec_part, conv_part, lat_part, *refs):
-    attn_out, dqkv_out, *sum_outs = refs[:7]
+    attn_out, dqkv_out, *sum_outs = refs[:8]
     (
         q_in,
         g_in,
@@ -576,9 +581,10 @@
         o_land,
         d_res,
         out_part,
-    ) = refs[7:31]
-    groups = [refs[31 + 5 * k : 36 + 5 * k] for k in range(5)]
-    send, recv, sum_send, sum_recv, sum_local = refs[56:]
+    ) = refs[8:32]
+    chunks = len(SUM_PLAN)
+    groups = [refs[32 + chunks * k : 32 + chunks * (k + 1)] for k in range(5)]
+    send, recv, sum_send, sum_recv, sum_local = refs[32 + 5 * chunks :]
     sums = Scatter(
         SUM_PLAN, [dec_part, conv_part, lat_part, out_part], groups, sum_send, sum_recv, sum_local
     )
@@ -609,6 +615,8 @@
         copy.start()
         copies[slot] = copy
 
+    for n in (0, 1, 2, 3):
+        sums.start(n)
     kv_at, q_at, g_at, ring_at, o_at, dq_at, back_at, home_at = 0, 8, 16, 24, 48, 56, 64, 72
     for k in range(1, 8):
         push(kv_at + k, proj.at[pl.ds(1, 2), plane[k]], kv_in.at[y, m], at_plane(k))
@@ -630,8 +638,6 @@
         pass_on(k)
     for k in range(1, 8):
         push(g_at + k, grad.at[plane[k]], g_in.at[m], at_plane(k))
-    for n in (0, 1, 2, 3):
-        sums.start(n)
     zero_rows = jnp.zeros((TILE - HEAD_PAD, key_t.shape[1]), jnp.bfloat16)
     key_t[HEAD_PAD:] = zero_rows
     value_t[HEAD_PAD:] = zero_rows
@@ -693,6 +699,8 @@
         offset[at, :] = jnp.sum(mixed * cot[at, :].astype(jnp.float32), axis=1, keepdims=True)
         return carry
 
+    for n in (3, 2, 0, 1):
+        sums.second(n)
     lax.fori_loop(0, queries // QUERY_BLOCK, forward, 0)
     for t in range(8):
         at = pl.ds(t * TILE, TILE)
@@ -736,6 +744,8 @@
         d_res[kind + 1, m] = d_sum[kind, m]
 
     key_side(cot_t, 1)
+    for n in (3, 2, 0, 1):
+        sums.third(n)
     for k in range(1, 8):
         copies[o_at + k].wait_recv()
     attn_out[...] = o_land[...]
@@ -755,6 +765,7 @@
                 k * OUT_ROWS_STEP : (k + 1) * OUT_ROWS_STEP
             ].astype(jnp.bfloat16)
     sums.start(4)
+    sums.start(5)
 
     def backward(i, carry):
         at = pl.ds(pl.multiple_of(i * QUERY_BLOCK, QUERY_BLOCK), QUERY_BLOCK)
@@ -772,27 +783,22 @@
         backward(i, 0)
         if i == 0:
             key_home(1)
-            sums.second(3)
-            sums.second(2)
     key_side(query_t, 0)
     for t in range(8):
         dq_send[t] = head_rows(attended[pl.ds(t * TILE, TILE), :])
     for k in range(1, 8):
         push(dq_at + k, dq_send.at[plane[k]], d_res.at[0, m], at_plane(k))
     d_res[0, m] = dq_send[m]
-    sums.second(0)
-    sums.second(1)
-    sums.third(3)
-    sums.third(2)
+    sums.second(4)
+    sums.second(5)
     key_home(0)
-    sums.second(4)
-    for n in (0, 1, 4):
-        sums.third(n)
+    sums.third(4)
+    sums.third(5)
     for first in (dq_at, home_at, home_at + 8):
         for k in range(1, 8):
             copies[first + k].wait_recv()
     dqkv_out[...] = d_res[...]
-    for n in range(5):
+    for n in range(chunks):
         sums.finish(n, sum_outs[n])
     for copy in copies.values():
         copy.wait_send()
@@ -842,7 +848,7 @@
         + [jax.ShapeDtypeStruct((rows[source], width), f32) for source, _, width, _ in SUM_PLAN],
         in_specs=[pl.BlockSpec(memory_space=pltpu.VMEM)] * 3
         + [pl.BlockSpec(memory_space=pl.ANY)] * 3,
-        out_specs=[pl.BlockSpec(memory_space=pltpu.VMEM)] * 7,
+        out_specs=[pl.BlockSpec(memory_space=pltpu.VMEM)] * 8,
         scratch_shapes=[pltpu.VMEM(shape, kind) for shape, kind in shapes]
         + [buffer for group in groups for buffer in group]
         + [pltpu.SemaphoreType.DMA((88,)), pltpu.SemaphoreType.DMA((88,))]
@@ -910,7 +916,7 @@
     projected = projected.T.reshape(3, HEADS, HEAD_PAD, tokens_here)
     scales = jnp.array([score_scale, 1.0, 1.0], jnp.float32).reshape(3, 1, 1, 1)
     projected = (projected * scales).astype(jnp.bfloat16)
-    attn_heads, dqkv, dec_low, dec_high, conv_rows, lat_sums, out_rows = attend_both_ways(
+    attn_heads, dqkv, *summed = attend_both_ways(
         projected,
         dattn.reshape(HEADS, HEAD_PAD, tokens_here),
         d_x1,
@@ -918,6 +924,7 @@
         conv_part,
         lat_part,
     )
+    dec_low, dec_high, conv_rows, lat_sums, out_low, out_high = summed
     mixed = lax.dot_general(
         attn_heads.reshape(HEADS * HEAD_PAD, tokens_here),
         out_full,
@@ -936,7 +943,7 @@
         )
     ).astype(jnp.bfloat16)
     g_deconv = jnp.concatenate([dec_low[:depth], dec_high[:depth]], axis=1)
-    g_out = out_rows[:out_depth]
+    g_out = jnp.concatenate([out_low[:out_depth], out_high[:out_depth]], axis=1)
     g_lateral = lat_sums[:lat_rows]
     g_conv = conv_rows.reshape(conv_rows.shape[0], 3, 3, LAT).transpose(1, 2, 0, 3)
     return (x_one, d_x1, second_input_gradient, g_out, g_deconv, g_lateral, g_conv)

time: 213 us -> 225 us (1.056)
  Pallas kernels: 185 us -> 197 us
    pallas_call x1, Pallas kernels: 109 us -> 127 us  [attend_both_ways(): pl.pallas_call(attention_kernel, out_shape=[jax.ShapeDtypeStruct((heads,...]
    pallas_call x1, Pallas kernels: 76.4 us -> 70 us  [gather_and_pyramid(): pl.pallas_call(functools.partial(gather_kernel, shapes), out_shape=full[1...]
where the time goes in v7:
time: 225 us; the launch traced here: 223 us
  Pallas kernels  197 us (88%)
  matrix products  12.6 us (6%)
  local copies, waits for them, and re-layouts  8.87 us (4%)
  other arithmetic  3.88 us (2%)
    pallas_call x1, Pallas kernels, attend_both_ways(): pl.pallas_call(attention_kernel, out_shape=[jax.ShapeDtypeStruct((heads,...  127 us
    pallas_call x1, Pallas kernels, gather_and_pyramid(): pl.pallas_call(functools.partial(gather_kernel, shapes), out_shape=full[1...  70 us

profile of v7, /device:TPU:64, one launch (start us, length us, event | category | flops | bytes accessed | tf_op | source)
XLA Modules:
  0.0 223.0 jit_solution(11266557257793496631)
XLA Ops:
  0.6 0.0 copy-start
  0.6 1.6 pad.16.refs_0_
  2.3 1.3 reshape.79
  3.6 0.0 copy-start.12
  3.6 0.1 pad.17
  3.6 0.9 reshape.80.refs_1_
  4.6 1.5 pad.18.refs_2_
  6.1 70.0 %shard_map.171 = (bf16[8,176,2304]{2,1,0:T(8,128)(2,1)}, bf16[8,96,1536]{2,1,0:T(8,128)(2,1)}, f32[128,1408]{1,0:T(8,128)}, bf16[128,1408]{1,0:T(8,128)(2,1)}, b...) custom-call(bf16[48,1536]{1,0:T(8,128)(2,1)} %pad.16.refs_0_, ...), custom_call_target="tpu_custom_call" | custom-call | tf_op jit(solution)/shard_map/pallas_call | solution.py:376
  76.1 0.0 copy-done
  76.1 0.1 convert_reduce_fusion
  76.2 0.2 fusion.18
  76.5 0.0 copy-done.12
  76.5 4.0 %fusion.19 = f32[128,2304]{1,0:T(8,128)S(1)} fusion(bf16[1408,2304]{1,0:T(8,128)(2,1)} %bitcast.26, bf16[128,1408]{1,0:T(8,128)(2,1)S(1)} %copy-done, f32[1408]{0:T(1024)S(1)} %copy-done.12, f32[128]{0:T(128)S(1)} %add_rsqrt_fusion, f32[128]{0:T(128)S(1)} %broadcast_multiply_fusion.2), kind=kOutput, calls=%fused_computation.22 | convolution fusion | flops 831373312 | bytes 8034816 | tf_op jit(solution)/shard_map/dot_general | solution.py:914
  80.5 0.0 copy-start.14
  80.6 0.0 copy-start.1
  80.6 0.4 copy.20
  80.9 0.3 copy-done.14
  81.2 1.0 multiply_convert_fusion.proj
  82.2 0.0 copy-done.1
  82.2 3.2 %fusion.4 = bf16[768,128]{1,0:T(8,128)(2,1)} fusion(bf16[128,1408]{1,0:T(8,128)(2,1)S(1)} %copy-done.1, bf16[768,1536]{1,0:T(8,128)(2,1)} %bitcast.33), kind=kOutput, calls=%fused_computation.7 | convolution fusion | flops 276922368 | bytes 2719744 | tf_op jit(solution)/shard_map/dot_general | solution.py:910
  85.4 0.0 copy-done.6
  85.4 0.7 pad.19
  86.2 126.8 %shard_map.172 = (bf16[8,96,128]{2,1,0:T(8,128)(2,1)}, bf16[3,8,96,128]{3,2,1,0:T(8,128)(2,1)}, f32[48,768]{1,0:T(8,128)}, f32[48,768]{1,0:T(8,128)}, f32[8,2304...) custom-call(bf16[3,8,96,128]{3,2,1,0:T(8,128)(2,1)} %multiply_convert_fusion.proj, ...), custom_call_target="tpu_custom_call" | custom-call | tf_op jit(solution)/shard_map/pallas_call | solution.py:842
  212.9 0.0 copy-start.5
  213.0 0.0 copy-done.3
  213.0 3.0 %fusion = bf16[128,1408]{1,0:T(8,128)(2,1)} fusion(bf16[768,128]{1,0:T(8,128)(2,1)} %bitcast.39, bf16[768,1536]{1,0:T(8,128)(2,1)} %bitcast.34, bf16[128,1408]{1,0:T(8,128)(2,1)S(1)} %copy-done.3), kind=kOutput, calls=%fused_computation.2 | convolution fusion | flops 277364736 | bytes 3080192 | tf_op jit(solution)/shard_map/dot_general | solution.py:928
  216.0 0.0 slice-done
  216.0 0.0 slice-done.1
  216.0 0.0 copy-done.5
  216.0 0.0 copy-start.4
  216.0 0.0 copy-start.10
  216.0 0.0 copy-start.11
  216.0 2.4 %fusion.24 = (f32[128]{0:T(128)S(1)}, f32[128]{0:T(128)S(1)}, f32[128,1408]{1,0:T(8,128)S(1)}) fusion(f32[128]{0:T(128)S(1)} %add_rsqrt_fusion, f32[128]{0:T(128)S(1)} %broadcast_multiply_fusion.2, bf16[128,1408]{1,0:T(8,128)(2,1)S(1)} %copy-done, f32[1408]{0:T(1024)S(1)} %copy-done.12, bf16[2304,128]{1,0:T(8,128)(2,1)S(1)} %bitcast.38, ...), kind=kOutput, calls=%fused_computation.32 | convolution fusion | flops 831733504 | bytes 8166912 | tf_op jit(solution)/shard_map/dot_general | solution.py:935
  218.4 0.0 copy-start.7
  218.4 0.0 copy-start.8
  218.4 0.0 copy-start.2
  218.4 0.0 copy-start.13
  218.5 0.0 copy-start.9
  218.5 0.0 copy-done.4
  218.5 1.1 fusion.17
  219.6 0.0 copy-done.10
  219.6 0.0 copy-done.11
  219.6 0.7 pad_maximum_fusion.1
  220.2 0.0 copy-done.7
  220.2 0.7 pad_maximum_fusion
  221.0 0.7 copy.24
  221.7 0.6 copy.25
  222.3 0.6 copy.26
  (13 shorter events, 0.1 us)
Async XLA Ops:
  0.6 75.5 %copy-start = (bf16[128,1408]{1,0:T(8,128)(2,1)S(1)}, bf16[128,1408]{1,0:T(8,128)(2,1)}, u32[]{:S(2)}) copy-start(bf16[128,1408]{1,0:T(8,128)(2,1)} %refs_4_.1) | copy-start | bytes 1081348
  3.6 72.9 %copy-start.12 = (f32[1408]{0:T(1024)S(1)}, f32[1408]{0:T(1024)}, u32[]{:S(2)}) copy-start(f32[1408]{0:T(1024)} %param.15) | copy-start | bytes 16900
  80.5 0.7 copy-start.14
  80.6 1.7 copy-start.1
  81.2 4.2 %copy-start.6 = (bf16[384,256]{1,0:T(8,128)(2,1)S(1)}, bf16[384,256]{1,0:T(8,128)(2,1)}, u32[]{:S(2)}) copy-start(bf16[384,256]{1,0:T(8,128)(2,1)} %get-tuple-element.27) | copy-start | bytes 589828
  82.2 133.8 %slice-start = ((s8[6488064]{0:T(1024)(128)(4,1)}), s8[2293760]{0:T(1024)(128)(4,1)S(1)}, s32[]{:S(2)}) async-start(s8[6488064]{0:T(1024)(128)(4,1)} %bitcast.27), calls=%async_computation | async-start | bytes 4587520
  86.2 126.8 %copy-start.3 = (bf16[128,1408]{1,0:T(8,128)(2,1)S(1)}, bf16[128,1408]{1,0:T(8,128)(2,1)}, u32[]{:S(2)}) copy-start(bf16[128,1408]{1,0:T(8,128)(2,1)} %refs_3_.1) | copy-start | bytes 1081348
  86.2 129.8 %slice-start.1 = ((s8[6488064]{0:T(1024)(128)(4,1)}), s8[4194304]{0:T(1024)(128)(4,1)S(1)}, s32[]{:S(2)}) async-start(s8[6488064]{0:T(1024)(128)(4,1)} %bitcast.27), calls=%async_computation.1 | async-start | bytes 8388608
  212.9 3.1 %copy-start.5 = (bf16[3,8,96,128]{3,2,1,0:T(8,128)(2,1)S(1)}, bf16[3,8,96,128]{3,2,1,0:T(8,128)(2,1)}, u32[]{:S(2)}) copy-start(bf16[3,8,96,128]{3,2,1,0:T(8,128)(2,1)} %get-tuple-element.30) | copy-start | bytes 1769476
  216.0 2.5 %copy-start.4 = (f32[128,1408]{1,0:T(8,128)S(1)}, f32[128,1408]{1,0:T(8,128)}, u32[]{:S(2)}) copy-start(f32[128,1408]{1,0:T(8,128)} %get-tuple-element.29) | copy-start | bytes 2162692
  216.0 3.5 %copy-start.10 = (f32[24,768]{1,0:T(8,128)S(1)}, f32[24,768]{1,0:T(8,128)}, u32[]{:S(2)}) copy-start(f32[24,768]{1,0:T(8,128)} %get-tuple-element.31) | copy-start | bytes 221188
  216.0 3.5 %copy-start.11 = (f32[24,640]{1,0:T(8,128)S(1)}, f32[24,640]{1,0:T(8,128)}, u32[]{:S(2)}) copy-start(f32[24,640]{1,0:T(8,128)} %get-tuple-element.32) | copy-start | bytes 184324
  218.4 1.8 copy-start.7
  218.4 1.8 copy-start.8
  218.4 2.5 %copy-start.2 = (bf16[128,1408]{1,0:T(8,128)(2,1)S(1)}, bf16[128,1408]{1,0:T(8,128)(2,1)}, u32[]{:S(2)}) copy-start(bf16[128,1408]{1,0:T(8,128)(2,1)} %get-tuple-element.50.d_x1) | copy-start | bytes 1081348
  218.4 3.3 %copy-start.13 = (f32[16,256]{1,0:T(8,128)S(1)}, f32[16,256]{1,0:T(8,128)}, u32[]{:S(2)}) copy-start(f32[16,256]{1,0:T(8,128)} %get-tuple-element.35) | copy-start | bytes 49156
  218.5 3.9 %copy-start.9 = (f32[8,2304]{1,0:T(8,128)S(1)}, f32[8,2304]{1,0:T(8,128)}, u32[]{:S(2)}) copy-start(f32[8,2304]{1,0:T(8,128)} %get-tuple-element.36) | copy-start | bytes 221188

commit v8 on v7

--- a/solution.py
+++ b/solution.py
@@ -615,8 +615,6 @@
         copy.start()
         copies[slot] = copy
 
-    for n in (0, 1, 2, 3):
-        sums.start(n)
     kv_at, q_at, g_at, ring_at, o_at, dq_at, back_at, home_at = 0, 8, 16, 24, 48, 56, 64, 72
     for k in range(1, 8):
         push(kv_at + k, proj.at[pl.ds(1, 2), plane[k]], kv_in.at[y, m], at_plane(k))
@@ -638,6 +636,8 @@
         pass_on(k)
     for k in range(1, 8):
         push(g_at + k, grad.at[plane[k]], g_in.at[m], at_plane(k))
+    for n in (0, 1, 2, 3):
+        sums.start(n)
     zero_rows = jnp.zeros((TILE - HEAD_PAD, key_t.shape[1]), jnp.bfloat16)
     key_t[HEAD_PAD:] = zero_rows
     value_t[HEAD_PAD:] = zero_rows
@@ -699,8 +699,6 @@
         offset[at, :] = jnp.sum(mixed * cot[at, :].astype(jnp.float32), axis=1, keepdims=True)
         return carry
 
-    for n in (3, 2, 0, 1):
-        sums.second(n)
     lax.fori_loop(0, queries // QUERY_BLOCK, forward, 0)
     for t in range(8):
         at = pl.ds(t * TILE, TILE)
@@ -744,8 +742,6 @@
         d_res[kind + 1, m] = d_sum[kind, m]
 
     key_side(cot_t, 1)
-    for n in (3, 2, 0, 1):
-        sums.third(n)
     for k in range(1, 8):
         copies[o_at + k].wait_recv()
     attn_out[...] = o_land[...]
@@ -766,6 +762,8 @@
             ].astype(jnp.bfloat16)
     sums.start(4)
     sums.start(5)
+    for n in (3, 2, 0, 1):
+        sums.second(n)
 
     def backward(i, carry):
         at = pl.ds(pl.multiple_of(i * QUERY_BLOCK, QUERY_BLOCK), QUERY_BLOCK)
@@ -789,9 +787,11 @@
     for k in range(1, 8):
         push(dq_at + k, dq_send.at[plane[k]], d_res.at[0, m], at_plane(k))
     d_res[0, m] = dq_send[m]
+    key_home(0)
+    for n in (3, 2, 0, 1):
+        sums.third(n)
     sums.second(4)
     sums.second(5)
-    key_home(0)
     sums.third(4)
     sums.third(5)
     for first in (dq_at, home_at, home_at + 8):

time: 225 us -> 207 us (0.920)
  Pallas kernels: 197 us -> 181 us
    pallas_call x1, Pallas kernels: 127 us -> 111 us  [attend_both_ways(): pl.pallas_call(attention_kernel, out_shape=[jax.ShapeDtypeStruct((heads,...]
where the time goes in v8:
time: 207 us
  Pallas kernels  181 us (87%)
  matrix products  12.6 us (6%)
  local copies, waits for them, and re-layouts  8.87 us (4%)
  other arithmetic  3.88 us (2%)
    pallas_call x1, Pallas kernels, attend_both_ways(): pl.pallas_call(attention_kernel, out_shape=[jax.ShapeDtypeStruct((heads,...  111 us
    pallas_call x1, Pallas kernels, gather_and_pyramid(): pl.pallas_call(functools.partial(gather_kernel, shapes), out_shape=full[1...  70 us

profile of v8, /device:TPU:64, one launch (start us, length us, event | category | flops | bytes accessed | tf_op | source)
XLA Modules:
  0.0 207.0 jit_solution(4833869119695178174)
XLA Ops:
  0.6 0.0 copy-start
  0.6 1.6 pad.16.refs_0_
  2.3 1.3 reshape.79
  3.6 0.0 copy-start.12
  3.6 0.1 pad.17
  3.6 0.9 reshape.80.refs_1_
  4.6 1.5 pad.18.refs_2_
  6.1 70.0 %shard_map.171 = (bf16[8,176,2304]{2,1,0:T(8,128)(2,1)}, bf16[8,96,1536]{2,1,0:T(8,128)(2,1)}, f32[128,1408]{1,0:T(8,128)}, bf16[128,1408]{1,0:T(8,128)(2,1)}, b...) custom-call(bf16[48,1536]{1,0:T(8,128)(2,1)} %pad.16.refs_0_, ...), custom_call_target="tpu_custom_call" | custom-call | tf_op jit(solution)/shard_map/pallas_call | solution.py:376
  76.1 0.0 copy-done
  76.1 0.1 convert_reduce_fusion
  76.2 0.2 fusion.18
  76.5 0.0 copy-done.12
  76.5 4.0 %fusion.19 = f32[128,2304]{1,0:T(8,128)S(1)} fusion(bf16[1408,2304]{1,0:T(8,128)(2,1)} %bitcast.26, bf16[128,1408]{1,0:T(8,128)(2,1)S(1)} %copy-done, f32[1408]{0:T(1024)S(1)} %copy-done.12, f32[128]{0:T(128)S(1)} %add_rsqrt_fusion, f32[128]{0:T(128)S(1)} %broadcast_multiply_fusion.2), kind=kOutput, calls=%fused_computation.22 | convolution fusion | flops 831373312 | bytes 8034816 | tf_op jit(solution)/shard_map/dot_general | solution.py:914
  80.5 0.0 copy-start.14
  80.6 0.0 copy-start.1
  80.6 0.4 copy.20
  80.9 0.3 copy-done.14
  81.2 1.0 multiply_convert_fusion.proj
  82.2 0.0 copy-done.1
  82.2 3.2 %fusion.4 = bf16[768,128]{1,0:T(8,128)(2,1)} fusion(bf16[128,1408]{1,0:T(8,128)(2,1)S(1)} %copy-done.1, bf16[768,1536]{1,0:T(8,128)(2,1)} %bitcast.33), kind=kOutput, calls=%fused_computation.7 | convolution fusion | flops 276922368 | bytes 2719744 | tf_op jit(solution)/shard_map/dot_general | solution.py:910
  85.4 0.0 copy-done.6
  85.4 0.7 pad.19
  86.2 110.9 %shard_map.172 = (bf16[8,96,128]{2,1,0:T(8,128)(2,1)}, bf16[3,8,96,128]{3,2,1,0:T(8,128)(2,1)}, f32[48,768]{1,0:T(8,128)}, f32[48,768]{1,0:T(8,128)}, f32[8,2304...) custom-call(bf16[3,8,96,128]{3,2,1,0:T(8,128)(2,1)} %multiply_convert_fusion.proj, ...), custom_call_target="tpu_custom_call" | custom-call | tf_op jit(solution)/shard_map/pallas_call | solution.py:842
  197.0 0.0 copy-start.5
  197.1 0.0 copy-done.3
  197.1 3.0 %fusion = bf16[128,1408]{1,0:T(8,128)(2,1)} fusion(bf16[768,128]{1,0:T(8,128)(2,1)} %bitcast.39, bf16[768,1536]{1,0:T(8,128)(2,1)} %bitcast.34, bf16[128,1408]{1,0:T(8,128)(2,1)S(1)} %copy-done.3), kind=kOutput, calls=%fused_computation.2 | convolution fusion | flops 277364736 | bytes 3080192 | tf_op jit(solution)/shard_map/dot_general | solution.py:928
  200.1 0.0 slice-done
  200.1 0.0 slice-done.1
  200.1 0.0 copy-done.5
  200.1 0.0 copy-start.4
  200.1 0.0 copy-start.10
  200.1 0.0 copy-start.11
  200.1 2.4 %fusion.24 = (f32[128]{0:T(128)S(1)}, f32[128]{0:T(128)S(1)}, f32[128,1408]{1,0:T(8,128)S(1)}) fusion(f32[128]{0:T(128)S(1)} %add_rsqrt_fusion, f32[128]{0:T(128)S(1)} %broadcast_multiply_fusion.2, bf16[128,1408]{1,0:T(8,128)(2,1)S(1)} %copy-done, f32[1408]{0:T(1024)S(1)} %copy-done.12, bf16[2304,128]{1,0:T(8,128)(2,1)S(1)} %bitcast.38, ...), kind=kOutput, calls=%fused_computation.32 | convolution fusion | flops 831733504 | bytes 8166912 | tf_op jit(solution)/shard_map/dot_general | solution.py:935
  202.5 0.0 copy-start.7
  202.5 0.0 copy-start.8
  202.5 0.0 copy-start.2
  202.5 0.0 copy-start.13
  202.5 0.0 copy-start.9
  202.6 0.0 copy-done.4
  202.6 1.1 fusion.17
  203.6 0.0 copy-done.10
  203.7 0.0 copy-done.11
  203.7 0.7 pad_maximum_fusion.1
  204.3 0.0 copy-done.7
  204.3 0.7 pad_maximum_fusion
  205.1 0.7 copy.24
  205.8 0.6 copy.25
  206.4 0.6 copy.26
  (13 shorter events, 0.1 us)
Async XLA Ops:
  0.6 75.5 %copy-start = (bf16[128,1408]{1,0:T(8,128)(2,1)S(1)}, bf16[128,1408]{1,0:T(8,128)(2,1)}, u32[]{:S(2)}) copy-start(bf16[128,1408]{1,0:T(8,128)(2,1)} %refs_4_.1) | copy-start | bytes 1081348
  3.6 72.9 %copy-start.12 = (f32[1408]{0:T(1024)S(1)}, f32[1408]{0:T(1024)}, u32[]{:S(2)}) copy-start(f32[1408]{0:T(1024)} %param.15) | copy-start | bytes 16900
  80.5 0.7 copy-start.14
  80.6 1.7 copy-start.1
  81.2 4.2 %copy-start.6 = (bf16[384,256]{1,0:T(8,128)(2,1)S(1)}, bf16[384,256]{1,0:T(8,128)(2,1)}, u32[]{:S(2)}) copy-start(bf16[384,256]{1,0:T(8,128)(2,1)} %get-tuple-element.27) | copy-start | bytes 589828
  82.2 117.9 %slice-start = ((s8[6488064]{0:T(1024)(128)(4,1)}), s8[2293760]{0:T(1024)(128)(4,1)S(1)}, s32[]{:S(2)}) async-start(s8[6488064]{0:T(1024)(128)(4,1)} %bitcast.27), calls=%async_computation | async-start | bytes 4587520
  86.2 110.9 %copy-start.3 = (bf16[128,1408]{1,0:T(8,128)(2,1)S(1)}, bf16[128,1408]{1,0:T(8,128)(2,1)}, u32[]{:S(2)}) copy-start(bf16[128,1408]{1,0:T(8,128)(2,1)} %refs_3_.1) | copy-start | bytes 1081348
  86.2 113.9 %slice-start.1 = ((s8[6488064]{0:T(1024)(128)(4,1)}), s8[4194304]{0:T(1024)(128)(4,1)S(1)}, s32[]{:S(2)}) async-start(s8[6488064]{0:T(1024)(128)(4,1)} %bitcast.27), calls=%async_computation.1 | async-start | bytes 8388608
  197.0 3.1 %copy-start.5 = (bf16[3,8,96,128]{3,2,1,0:T(8,128)(2,1)S(1)}, bf16[3,8,96,128]{3,2,1,0:T(8,128)(2,1)}, u32[]{:S(2)}) copy-start(bf16[3,8,96,128]{3,2,1,0:T(8,128)(2,1)} %get-tuple-element.30) | copy-start | bytes 1769476
  200.1 2.5 %copy-start.4 = (f32[128,1408]{1,0:T(8,128)S(1)}, f32[128,1408]{1,0:T(8,128)}, u32[]{:S(2)}) copy-start(f32[128,1408]{1,0:T(8,128)} %get-tuple-element.29) | copy-start | bytes 2162692
  200.1 3.5 %copy-start.10 = (f32[24,768]{1,0:T(8,128)S(1)}, f32[24,768]{1,0:T(8,128)}, u32[]{:S(2)}) copy-start(f32[24,768]{1,0:T(8,128)} %get-tuple-element.31) | copy-start | bytes 221188
  200.1 3.5 %copy-start.11 = (f32[24,640]{1,0:T(8,128)S(1)}, f32[24,640]{1,0:T(8,128)}, u32[]{:S(2)}) copy-start(f32[24,640]{1,0:T(8,128)} %get-tuple-element.32) | copy-start | bytes 184324
  202.5 1.8 copy-start.7
  202.5 1.8 copy-start.8
  202.5 2.5 %copy-start.2 = (bf16[128,1408]{1,0:T(8,128)(2,1)S(1)}, bf16[128,1408]{1,0:T(8,128)(2,1)}, u32[]{:S(2)}) copy-start(bf16[128,1408]{1,0:T(8,128)(2,1)} %get-tuple-element.50.d_x1) | copy-start | bytes 1081348
  202.5 3.3 %copy-start.13 = (f32[16,256]{1,0:T(8,128)S(1)}, f32[16,256]{1,0:T(8,128)}, u32[]{:S(2)}) copy-start(f32[16,256]{1,0:T(8,128)} %get-tuple-element.35) | copy-start | bytes 49156
  202.5 3.9 %copy-start.9 = (f32[8,2304]{1,0:T(8,128)S(1)}, f32[8,2304]{1,0:T(8,128)}, u32[]{:S(2)}) copy-start(f32[8,2304]{1,0:T(8,128)} %get-tuple-element.36) | copy-start | bytes 221188

commit v9 on v8

--- a/solution.py
+++ b/solution.py
@@ -33,8 +33,6 @@
 MESH = pl.DeviceIdType.MESH
 ROWS_PAD = 48
 HEAD_PAD = 96
-OUT_ROWS_PAD = 32
-OUT_COLS_PAD = 1536
 
 
 def place():
@@ -70,8 +68,12 @@
     deconv, *rest = refs[17:]
     outs = [deconv, qkv_out, w_out_out]
     shards, packs, rest = rest[:3], rest[3:6], rest[6:]
-    feature, pixels, act, dconv, cot_low, cot_high, norm_lat, dup, *sems = rest
+    deconv_shard, out_shard, feature, pixels, act, dconv, cot_low, cot_high, norm_lat, dup, *sems = rest
     send, recv, local, halo_send, halo_recv = sems
+    for shard, padded in ((ins[0], deconv_shard), (ins[2], out_shard)):
+        padded[...] = jnp.zeros_like(padded)
+        padded[: shard.shape[0], : shard.shape[1]] = shard[...]
+    ins = [deconv_shard, ins[1], out_shard]
     x, zl, y, zh, core = place()
     s = lax.axis_index("sp")
     below, above = {"sp": (s + 1) % 32}, {"sp": (s + 31) % 32}
@@ -345,11 +347,11 @@
     twins(0)
     keeps[0].wait()
     linv = upward()
+    convolve()
     far(1)
     near(2)
-    convolve()
+    downward(linv)
     far(2)
-    downward(linv)
     deep(1)
     conv_term()
     deep(2)
@@ -367,7 +369,8 @@
     shapes = []
     for shard, per in zip(shards, pers):
         block = -(-4 * per // 16) * 16
-        shapes.append((shard.shape[0], per, block, shard.shape[1]))
+        width = -(-shard.shape[1] // 256) * 256
+        shapes.append((-(-per // 16) * 16, per, block, width))
     halves = [(rows, block, width // 2) for rows, _, block, width in shapes]
     tokens, features = others[0].shape
     bf16, f32 = jnp.bfloat16, jnp.float32
@@ -390,6 +393,8 @@
         + [pltpu.VMEM((4, rows, half), bf16) for rows, _, half in halves]
         + [pltpu.VMEM((block, half), bf16) for _, block, half in halves]
         + [
+            pltpu.VMEM((shapes[0][0], shapes[0][3]), bf16),
+            pltpu.VMEM((shapes[2][0], shapes[2][3]), bf16),
             pltpu.VMEM((tokens, features), bf16),
             pltpu.VMEM((pixel_count, DEC), bf16),
             pltpu.VMEM((4, 6 * GRID_W, LAT), bf16),
@@ -507,7 +512,8 @@
         total = self.sums[1][n][self.me[self.plan[n][3][2]]].astype(jnp.float32)
         for k in range(count):
             total += self.land[2][n][k].astype(jnp.float32)
-        out[...] = total
+        _, first, width, _ = self.plan[n]
+        out[:, pl.ds(first, width)] = total[: out.shape[0]]
 
     def settle(self):
         for copy in self.copies.values():
@@ -555,7 +561,7 @@
 
 
 def attention_kernel(proj, grad, d_x1, dec_part, conv_part, lat_part, *refs):
-    attn_out, dqkv_out, *sum_outs = refs[:8]
+    attn_out, dqkv_out, *sum_outs = refs[:6]
     (
         q_in,
         g_in,
@@ -581,10 +587,10 @@
         o_land,
         d_res,
         out_part,
-    ) = refs[8:32]
+    ) = refs[6:30]
     chunks = len(SUM_PLAN)
-    groups = [refs[32 + chunks * k : 32 + chunks * (k + 1)] for k in range(5)]
-    send, recv, sum_send, sum_recv, sum_local = refs[32 + 5 * chunks :]
+    groups = [refs[30 + chunks * k : 30 + chunks * (k + 1)] for k in range(5)]
+    send, recv, sum_send, sum_recv, sum_local = refs[30 + 5 * chunks :]
     sums = Scatter(
         SUM_PLAN, [dec_part, conv_part, lat_part, out_part], groups, sum_send, sum_recv, sum_local
     )
@@ -799,13 +805,13 @@
             copies[first + k].wait_recv()
     dqkv_out[...] = d_res[...]
     for n in range(chunks):
-        sums.finish(n, sum_outs[n])
+        sums.finish(n, sum_outs[SUM_PLAN[n][0]])
     for copy in copies.values():
         copy.wait_send()
     sums.settle()
 
 
-def attend_both_ways(proj, grad, d_x1, dec_part, conv_part, lat_part):
+def attend_both_ways(proj, grad, d_x1, dec_part, conv_part, lat_part, own_rows):
     rows = [part.shape[3] for part in (dec_part, conv_part, lat_part)] + [OUT_ROWS_STEP]
     groups = scatter_buffers(SUM_PLAN, rows)
     heads = grad.shape[0]
@@ -845,10 +851,13 @@
             jax.ShapeDtypeStruct((heads, *block), bf16),
             jax.ShapeDtypeStruct((3, heads, *block), bf16),
         ]
-        + [jax.ShapeDtypeStruct((rows[source], width), f32) for source, _, width, _ in SUM_PLAN],
+        + [
+            jax.ShapeDtypeStruct((w_rows, part.shape[-1]), f32)
+            for w_rows, part in zip(own_rows, (dec_part, conv_part, lat_part, d_x1))
+        ],
         in_specs=[pl.BlockSpec(memory_space=pltpu.VMEM)] * 3
         + [pl.BlockSpec(memory_space=pl.ANY)] * 3,
-        out_specs=[pl.BlockSpec(memory_space=pltpu.VMEM)] * 8,
+        out_specs=[pl.BlockSpec(memory_space=pltpu.VMEM)] * 6,
         scratch_shapes=[pltpu.VMEM(shape, kind) for shape, kind in shapes]
         + [buffer for group in groups for buffer in group]
         + [pltpu.SemaphoreType.DMA((88,)), pltpu.SemaphoreType.DMA((88,))]
@@ -884,12 +893,8 @@
         w_qkv.reshape(depth, 3 * HEADS, HEAD),
         ((0, ROWS_PAD - depth), (0, 0), (0, HEAD_PAD - HEAD)),
     ).reshape(ROWS_PAD, 3 * HEADS * HEAD_PAD)
-    out_shard = jnp.pad(
-        w_out, ((0, OUT_ROWS_PAD - out_depth), (0, OUT_COLS_PAD - w_out.shape[1]))
-    )
-    deconv_shard = jnp.pad(w_deconv, ((0, ROWS_PAD - depth), (0, 0)))
     qkv_full, out_full, halfway_split, d_x1, dec_part, conv_part, lat_part = gather_and_pyramid(
-        [deconv_shard, qkv_shard, out_shard],
+        [w_deconv, qkv_shard, w_out],
         [depth, depth, out_depth],
         y_one,
         second_stream_state,
@@ -923,8 +928,9 @@
         dec_part,
         conv_part,
         lat_part,
+        (depth, LAT // devices, lat_rows, out_depth),
     )
-    dec_low, dec_high, conv_rows, lat_sums, out_low, out_high = summed
+    g_deconv, conv_rows, g_lateral, g_out = summed
     mixed = lax.dot_general(
         attn_heads.reshape(HEADS * HEAD_PAD, tokens_here),
         out_full,
@@ -942,9 +948,6 @@
             normalized_gradient * layer_norm_gain, standardized_input, inverse_deviation
         )
     ).astype(jnp.bfloat16)
-    g_deconv = jnp.concatenate([dec_low[:depth], dec_high[:depth]], axis=1)
-    g_out = jnp.concatenate([out_low[:out_depth], out_high[:out_depth]], axis=1)
-    g_lateral = lat_sums[:lat_rows]
     g_conv = conv_rows.reshape(conv_rows.shape[0], 3, 3, LAT).transpose(1, 2, 0, 3)
     return (x_one, d_x1, second_input_gradient, g_out, g_deconv, g_lateral, g_conv)
 

time: 207 us -> 204 us (0.986)
    pad x2 -> x0, local copies, waits for them, and re-layouts: 3.16 us -> none  [the longest x1 1.63 us: per_device(): deconv_shard = jnp.pad(w_deconv, ((0, ROWS_PAD - depth), (0, 0)))]
where the time goes in v9:
time: 204 us; the launch traced here: 203 us
  Pallas kernels  180 us (88%)
  matrix products  12.6 us (6%)
  local copies, waits for them, and re-layouts  7.12 us (3%)
  other arithmetic  2.47 us (1%)
    pallas_call x1, Pallas kernels, attend_both_ways(): pl.pallas_call(attention_kernel, out_shape=[jax.ShapeDtypeStruct((heads,...  112 us
    pallas_call x1, Pallas kernels, gather_and_pyramid(): pl.pallas_call(functools.partial(gather_kernel, shapes), out_shape=full[1...  68.6 us

profile of v9, /device:TPU:64, one launch (start us, length us, event | category | flops | bytes accessed | tf_op | source)
XLA Modules:
  0.0 203.3 jit_solution(13187929177888671353)
XLA Ops:
  0.6 0.0 copy-start
  0.6 1.3 reshape.79
  2.0 0.0 copy-start.10
  2.0 0.1 pad.8
  2.1 0.9 reshape.80.refs_1_
  3.0 68.6 %shard_map.171 = (bf16[8,176,2304]{2,1,0:T(8,128)(2,1)}, bf16[8,96,1536]{2,1,0:T(8,128)(2,1)}, f32[128,1408]{1,0:T(8,128)}, bf16[128,1408]{1,0:T(8,128)(2,1)}, b...) custom-call(bf16[44,1536]{1,0:T(8,128)(2,1)} %refs_0_.1, ...), custom_call_target="tpu_custom_call" | custom-call | tf_op jit(solution)/shard_map/pallas_call | solution.py:379
  71.5 0.0 copy-done
  71.6 0.1 convert_reduce_fusion
  71.7 0.2 fusion.18
  71.9 0.0 copy-done.10
  72.0 4.0 %fusion.19 = f32[128,2304]{1,0:T(8,128)S(1)} fusion(bf16[1408,2304]{1,0:T(8,128)(2,1)} %bitcast.21, bf16[128,1408]{1,0:T(8,128)(2,1)S(1)} %copy-done, f32[1408]{0:T(1024)S(1)} %copy-done.10, f32[128]{0:T(128)S(1)} %add_rsqrt_fusion, f32[128]{0:T(128)S(1)} %broadcast_multiply_fusion.2), kind=kOutput, calls=%fused_computation.22 | convolution fusion | flops 831373312 | bytes 8034816 | tf_op jit(solution)/shard_map/dot_general | solution.py:919
  76.0 0.0 copy-start.12
  76.0 0.0 copy-start.1
  76.0 0.4 copy.20
  76.4 0.3 copy-done.12
  76.6 0.0 copy-start.7
  76.6 1.0 multiply_convert_fusion.proj
  77.6 0.0 copy-done.1
  77.6 0.0 slice-start
  77.6 3.2 %fusion.4 = bf16[768,128]{1,0:T(8,128)(2,1)} fusion(bf16[128,1408]{1,0:T(8,128)(2,1)S(1)} %copy-done.1, bf16[768,1536]{1,0:T(8,128)(2,1)} %bitcast.28), kind=kOutput, calls=%fused_computation.7 | convolution fusion | flops 276922368 | bytes 2719744 | tf_op jit(solution)/shard_map/dot_general | solution.py:915
  80.8 0.0 copy-done.7
  80.9 0.7 pad.9
  81.6 111.8 %shard_map.172 = (bf16[8,96,128]{2,1,0:T(8,128)(2,1)}, bf16[3,8,96,128]{3,2,1,0:T(8,128)(2,1)}, f32[44,1536]{1,0:T(8,128)}, f32[8,2304]{1,0:T(8,128)}, f32[12,256]{1,0:T(8,128)}, /*index=5*/f32[22,1408]{1,0:T(8,128)}) custom-call(bf16[3,8,96,128]{3,2,1,0:T(8,128)(2,1)} %multiply_convert_fusion.proj, bf16[8,96,128]{2,1,0:T(8,128)(2,1)} %bitcast.35, ...), custom_call_target="tpu_custom_call" | custom-call | tf_op jit(solution)/shard_map/pallas_call | solution.py:848
  193.4 0.0 copy-start.5
  193.4 0.0 copy-done.3
  193.4 3.0 %fusion = bf16[128,1408]{1,0:T(8,128)(2,1)} fusion(bf16[768,128]{1,0:T(8,128)(2,1)} %bitcast.34, bf16[768,1536]{1,0:T(8,128)(2,1)} %bitcast.29, bf16[128,1408]{1,0:T(8,128)(2,1)S(1)} %copy-done.3), kind=kOutput, calls=%fused_computation.2 | convolution fusion | flops 277364736 | bytes 3080192 | tf_op jit(solution)/shard_map/dot_general | solution.py:934
  196.4 0.0 slice-done
  196.4 0.0 slice-done.1
  196.4 0.0 copy-done.5
  196.5 0.0 copy-start.4
  196.5 2.4 %fusion.24 = (f32[128]{0:T(128)S(1)}, f32[128]{0:T(128)S(1)}, f32[128,1408]{1,0:T(8,128)S(1)}) fusion(f32[128]{0:T(128)S(1)} %add_rsqrt_fusion, f32[128]{0:T(128)S(1)} %broadcast_multiply_fusion.2, bf16[128,1408]{1,0:T(8,128)(2,1)S(1)} %copy-done, f32[1408]{0:T(1024)S(1)} %copy-done.10, bf16[2304,128]{1,0:T(8,128)(2,1)S(1)} %bitcast.33, ...), kind=kOutput, calls=%fused_computation.30 | convolution fusion | flops 831733504 | bytes 8166912 | tf_op jit(solution)/shard_map/dot_general | solution.py:941
  198.8 0.0 copy-start.2
  198.8 0.0 copy-start.8
  198.9 0.0 copy-start.6
  198.9 0.0 copy-start.11
  198.9 0.0 copy-start.9
  198.9 0.0 copy-done.4
  198.9 1.1 fusion.17
  200.0 0.0 copy-done.2
  200.0 0.7 copy.26
  200.7 0.0 copy-done.8
  200.7 0.7 copy.27
  201.4 0.0 copy-done.6
  201.4 0.7 copy.28
  202.1 0.0 copy-done.11
  202.1 0.6 copy.29
  202.7 0.0 copy-done.9
  202.7 0.6 copy.30
  (7 shorter events, 0.1 us)
Async XLA Ops:
  0.6 70.9 %copy-start = (bf16[128,1408]{1,0:T(8,128)(2,1)S(1)}, bf16[128,1408]{1,0:T(8,128)(2,1)}, u32[]{:S(2)}) copy-start(bf16[128,1408]{1,0:T(8,128)(2,1)} %refs_4_.1) | copy-start | bytes 1081348
  2.0 70.0 %copy-start.10 = (f32[1408]{0:T(1024)S(1)}, f32[1408]{0:T(1024)}, u32[]{:S(2)}) copy-start(f32[1408]{0:T(1024)} %param.15) | copy-start | bytes 16900
  76.0 0.7 copy-start.12
  76.0 1.6 copy-start.1
  76.6 4.2 %copy-start.7 = (bf16[384,256]{1,0:T(8,128)(2,1)S(1)}, bf16[384,256]{1,0:T(8,128)(2,1)}, u32[]{:S(2)}) copy-start(bf16[384,256]{1,0:T(8,128)(2,1)} %get-tuple-element.25) | copy-start | bytes 589828
  77.6 118.8 %slice-start = ((s8[6488064]{0:T(1024)(128)(4,1)}), s8[2293760]{0:T(1024)(128)(4,1)S(1)}, s32[]{:S(2)}) async-start(s8[6488064]{0:T(1024)(128)(4,1)} %bitcast.22), calls=%async_computation | async-start | bytes 4587520
  81.6 111.8 %copy-start.3 = (bf16[128,1408]{1,0:T(8,128)(2,1)S(1)}, bf16[128,1408]{1,0:T(8,128)(2,1)}, u32[]{:S(2)}) copy-start(bf16[128,1408]{1,0:T(8,128)(2,1)} %refs_3_.1) | copy-start | bytes 1081348
  81.6 114.9 %slice-start.1 = ((s8[6488064]{0:T(1024)(128)(4,1)}), s8[4194304]{0:T(1024)(128)(4,1)S(1)}, s32[]{:S(2)}) async-start(s8[6488064]{0:T(1024)(128)(4,1)} %bitcast.22), calls=%async_computation.1 | async-start | bytes 8388608
  193.4 3.1 %copy-start.5 = (bf16[3,8,96,128]{3,2,1,0:T(8,128)(2,1)S(1)}, bf16[3,8,96,128]{3,2,1,0:T(8,128)(2,1)}, u32[]{:S(2)}) copy-start(bf16[3,8,96,128]{3,2,1,0:T(8,128)(2,1)} %get-tuple-element.28) | copy-start | bytes 1769476
  196.5 2.4 %copy-start.4 = (f32[128,1408]{1,0:T(8,128)S(1)}, f32[128,1408]{1,0:T(8,128)}, u32[]{:S(2)}) copy-start(f32[128,1408]{1,0:T(8,128)} %get-tuple-element.27) | copy-start | bytes 2162692
  198.8 1.1 copy-start.2
  198.8 1.9 copy-start.8
  198.9 2.5 %copy-start.6 = (f32[44,1536]{1,0:T(8,128)S(1)}, f32[44,1536]{1,0:T(8,128)}, u32[]{:S(2)}) copy-start(f32[44,1536]{1,0:T(8,128)} %get-tuple-element.49) | copy-start | bytes 811012
  198.9 3.2 %copy-start.11 = (f32[12,256]{1,0:T(8,128)S(1)}, f32[12,256]{1,0:T(8,128)}, u32[]{:S(2)}) copy-start(f32[12,256]{1,0:T(8,128)} %get-tuple-element.50) | copy-start | bytes 36868
  198.9 3.8 %copy-start.9 = (f32[8,2304]{1,0:T(8,128)S(1)}, f32[8,2304]{1,0:T(8,128)}, u32[]{:S(2)}) copy-start(f32[8,2304]{1,0:T(8,128)} %get-tuple-element.32) | copy-start | bytes 221188
